TPU v7x, 512 devices: a whole 4x4x16 slice. The times are simulated.
512 devices in a mesh: lat: 16 (over y_lo, x, core), lon: 32 (over z, y_hi).
Axes of the slice: x: 4, y: 4 (y_hi: 2, y_lo: 2; y = y_hi * 2 + y_lo), z: 16, core: 2. Of those that a mesh axis runs over, the one named last changes fastest.
Arguments:
- tracers: float32 [4, 8, 256, 4096], P(None, None, 'lat', 'lon'), may hold values from -6 to 6
- velocity: float32 [2, 8, 256, 4096], P(None, None, 'lat', 'lon'), may hold values from -3 to 3
- surface: float32 [256, 4096], P('lat', 'lon'), may hold values from -2 to 2
- wind: float32 [2, 256, 4096], P(None, 'lat', 'lon'), may hold values from -5 to 5
- bottom: int32 [256, 4096], P('lat', 'lon'), may hold values from 0 to 8
Outputs:
- tracers_new: float32 [4, 8, 256, 4096], P(None, None, 'lat', 'lon')
- velocity_new: float32 [2, 8, 256, 4096], P(None, None, 'lat', 'lon')
- height: float32 [256, 4096], P('lat', 'lon')
- streamfunction: float32 [256, 4096], P('lat', 'lon')
All inputs are finite; a program needn't handle non-finite values.
Results may differ from a plain program's by a relative error of at most 0.0003.
Values sent between devices are 32-bit elements; how exact they have to be, the bound alone decides.
No kernel may reach another device: no remote copies, remote signals or barrier semaphores. Data moves between devices by JAX's collectives and lax.ppermute only.
A program may use at most 64 MiB of HBM per device.

v0:
```python
import jax
import jax.numpy as jnp
from jax import lax
from jax.sharding import PartitionSpec as P

LEVELS = 8
SUBSTEPS = 30
RIM_DEPTH = 10


time_step = 0.2
tracer_diffusion = 0.2
viscosity = 0.2
thermal_expansion = 2.0
haline_contraction = 1.5
coriolis_base = 1.0
gravity = 140.0
surface_scale = 40.0


def padded_2(block, sides, width):
    for axis, dim in sides:
        count = lax.axis_size(axis)
        forward = [(i, i + 1) for i in range(count - 1)]
        forward.append((count - 1, 0))
        backward = [(target, source) for source, target in forward]
        low = lax.ppermute(
            lax.slice_in_dim(block, block.shape[dim] - width, None, axis=dim), axis, forward
        )
        high = lax.ppermute(lax.slice_in_dim(block, 0, width, axis=dim), axis, backward)
        block = jnp.concatenate([low, block, high], axis=dim)
    return block


def prefix(part, axis, combine, identity):
    place = lax.axis_index(axis)
    gathered = lax.all_gather(part, axis)
    state = jnp.zeros_like(part) + jnp.asarray(identity, part.dtype)

    def one(hop, state):
        return combine(state, lax.dynamic_index_in_dim(gathered, hop, 0, False))

    return lax.fori_loop(0, place, one, state)


def window(values, rim, row_lo, row_hi, col_lo, col_hi):
    return values[..., rim + row_lo : rim + row_hi, rim + col_lo : rim + col_hi]


def baroclinic(tracer_wide, current_wide, bottom_wide, row_start, rows_total, wind):
    levels = tracer_wide.shape[1]
    row_count = bottom_wide.shape[0] - 6
    col_count = bottom_wide.shape[1] - 6
    thickness = 1.0 / levels
    level_ids = lax.broadcasted_iota(jnp.int32, (levels, 1, 1), 0)
    wet_mask = (level_ids < bottom_wide[None]).astype(jnp.float32)
    tracer_vals = tracer_wide * wet_mask

    def wet_win(row_lo, row_hi, col_lo, col_hi):
        return window(wet_mask, 3, row_lo, row_hi, col_lo, col_hi)

    def tracer_win(row_lo, row_hi, col_lo, col_hi):
        return window(tracer_vals, 3, row_lo, row_hi, col_lo, col_hi)

    zonal_flow = (
        current_wide[0]
        * wet_win(-1, row_count + 1, -1, col_count + 1)
        * wet_win(-1, row_count + 1, 0, col_count + 2)
    )
    merid_flow = (
        current_wide[1]
        * wet_win(-1, row_count + 1, -1, col_count + 1)
        * wet_win(0, row_count + 2, -1, col_count + 1)
    )

    def zonal_win(row_lo, row_hi, col_lo, col_hi):
        return window(zonal_flow, 1, row_lo, row_hi, col_lo, col_hi)

    def merid_win(row_lo, row_hi, col_lo, col_hi):
        return window(merid_flow, 1, row_lo, row_hi, col_lo, col_hi)

    east_face = wet_win(0, row_count, -1, col_count) * wet_win(0, row_count, 0, col_count + 1)
    east_value = (
        37.0
        * (tracer_win(0, row_count, -1, col_count) + tracer_win(0, row_count, 0, col_count + 1))
        - 8.0
        * (tracer_win(0, row_count, -2, col_count - 1) + tracer_win(0, row_count, 1, col_count + 2))
        + (tracer_win(0, row_count, -3, col_count - 2) + tracer_win(0, row_count, 2, col_count + 3))
    ) / 60.0
    east_flux = (
        tracer_diffusion
        * east_face
        * (tracer_win(0, row_count, 0, col_count + 1) - tracer_win(0, row_count, -1, col_count))
        - zonal_win(0, row_count, -1, col_count) * east_value
    )
    north_face = wet_win(-1, row_count, 0, col_count) * wet_win(0, row_count + 1, 0, col_count)
    north_value = (
        37.0
        * (tracer_win(-1, row_count, 0, col_count) + tracer_win(0, row_count + 1, 0, col_count))
        - 8.0
        * (tracer_win(-2, row_count - 1, 0, col_count) + tracer_win(1, row_count + 2, 0, col_count))
        + (tracer_win(-3, row_count - 2, 0, col_count) + tracer_win(2, row_count + 3, 0, col_count))
    ) / 60.0
    north_flux = (
        tracer_diffusion
        * north_face
        * (tracer_win(0, row_count + 1, 0, col_count) - tracer_win(-1, row_count, 0, col_count))
        - merid_win(-1, row_count, 0, col_count) * north_value
    )
    tendency = (
        east_flux[..., 1:] - east_flux[..., :-1] + north_flux[..., 1:, :] - north_flux[..., :-1, :]
    )
    wet_inner = wet_win(0, row_count, 0, col_count)
    tracers_new = (tracer_win(0, row_count, 0, col_count) + time_step * tendency) * wet_inner
    upper = tracer_win(0, row_count + 1, 0, col_count + 1)
    density = haline_contraction * upper[1] - thermal_expansion * upper[0]
    pressure = thickness * jnp.cumsum(density, axis=0)
    grad_x = pressure[:, :row_count, 1:] - pressure[:, :row_count, :col_count]
    grad_y = pressure[:, 1:, :col_count] - pressure[:, :row_count, :col_count]
    row_index = (row_start + lax.iota(jnp.int32, row_count)).astype(jnp.float32)[:, None]
    coriolis_u = coriolis_base * (0.5 + (row_index + 0.5) / rows_total)
    coriolis_v = coriolis_base * (0.5 + (row_index + 1.0) / rows_total)
    surface_level = (level_ids == 0).astype(jnp.float32)
    east_inner = east_face[..., 1:]
    north_inner = north_face[..., 1:, :]
    old_u = zonal_win(0, row_count, 0, col_count)
    old_v = merid_win(0, row_count, 0, col_count)
    v_at_u = 0.25 * (
        old_v
        + merid_win(0, row_count, 1, col_count + 1)
        + merid_win(-1, row_count - 1, 0, col_count)
        + merid_win(-1, row_count - 1, 1, col_count + 1)
    )
    u_at_v = 0.25 * (
        old_u
        + zonal_win(1, row_count + 1, 0, col_count)
        + zonal_win(0, row_count, -1, col_count - 1)
        + zonal_win(1, row_count + 1, -1, col_count - 1)
    )
    smooth_u = (
        zonal_win(0, row_count, 1, col_count + 1)
        + zonal_win(0, row_count, -1, col_count - 1)
        + zonal_win(1, row_count + 1, 0, col_count)
        + zonal_win(-1, row_count - 1, 0, col_count)
        - 4.0 * old_u
    )
    smooth_v = (
        merid_win(0, row_count, 1, col_count + 1)
        + merid_win(0, row_count, -1, col_count - 1)
        + merid_win(1, row_count + 1, 0, col_count)
        + merid_win(-1, row_count - 1, 0, col_count)
        - 4.0 * old_v
    )
    tend_u = east_inner * (
        coriolis_u * v_at_u - grad_x + viscosity * smooth_u + surface_level * wind[0]
    )
    tend_v = north_inner * (
        -coriolis_v * u_at_v - grad_y + viscosity * smooth_v + surface_level * wind[1]
    )
    star_u = old_u + time_step * tend_u
    star_v = old_v + time_step * tend_v
    column_u = jnp.maximum(thickness * jnp.sum(east_inner, axis=0), thickness)
    column_v = jnp.maximum(thickness * jnp.sum(north_inner, axis=0), thickness)

    def column_mean(values, column):
        return thickness * jnp.sum(values, axis=0) / column

    means = (
        column_mean(old_u, column_u),
        column_mean(old_v, column_v),
        column_mean(tend_u, column_u),
        column_mean(tend_v, column_v),
        column_mean(star_u, column_u),
        column_mean(star_v, column_v),
    )
    return (tracers_new, star_u, star_v, east_inner, north_inner, means)


def substep(
    height,
    zonal_flow,
    merid_flow,
    force_u,
    force_v,
    depth_u,
    depth_v,
    coriolis_u,
    coriolis_v,
    neighbour,
):
    sub_step = time_step / SUBSTEPS
    flux_u = depth_u * zonal_flow
    flux_v = depth_v * merid_flow
    height = height - sub_step * surface_scale * (
        flux_u - neighbour(flux_u, 0, -1) + flux_v - neighbour(flux_v, -1, 0)
    )
    open_u = (depth_u > 0.0).astype(jnp.float32)
    open_v = (depth_v > 0.0).astype(jnp.float32)
    v_at_u = 0.25 * (
        merid_flow
        + neighbour(merid_flow, 0, 1)
        + neighbour(merid_flow, -1, 0)
        + neighbour(merid_flow, -1, 1)
    )
    u_at_v = 0.25 * (
        zonal_flow
        + neighbour(zonal_flow, 1, 0)
        + neighbour(zonal_flow, 0, -1)
        + neighbour(zonal_flow, 1, -1)
    )
    new_u = open_u * (
        zonal_flow
        + sub_step * (coriolis_u * v_at_u - gravity * (neighbour(height, 0, 1) - height) + force_u)
    )
    new_v = open_v * (
        merid_flow
        + sub_step * (-coriolis_v * u_at_v - gravity * (neighbour(height, 1, 0) - height) + force_v)
    )
    return (height, new_u, new_v)


def slide(values, row_shift, col_shift):
    padded = jnp.pad(values, ((1, 1), (1, 1)))
    row_count, col_count = values.shape
    return padded[
        1 + row_shift : 1 + row_shift + row_count, 1 + col_shift : 1 + col_shift + col_count
    ]


def trim(values, amount):
    return values[..., amount : values.shape[-2] - amount, amount : values.shape[-1] - amount]


def add_parts(earlier, later):
    return earlier + later


def shards(tracers, velocity, surface, wind, bottom):
    row_count, col_count = surface.shape
    rows_total = lax.axis_size("lat") * row_count
    row_first = lax.axis_index("lat") * row_count
    deep = RIM_DEPTH
    thickness = 1.0 / LEVELS

    def band_rows(width):
        return row_first - width + lax.iota(jnp.int32, row_count + 2 * width)

    def inside(width):
        row_ids = band_rows(width)
        return ((row_ids >= 0) & (row_ids < rows_total))[:, None]

    def coriolis_rows(width, offset):
        row_ids = band_rows(width).astype(jnp.float32)[:, None]
        return coriolis_base * (0.5 + (row_ids + offset) / rows_total)

    bottom_wide = padded_2(bottom, (("lat", 0), ("lon", 1)), deep)
    bottom_wide = jnp.where(inside(deep), bottom_wide, 0)
    tracer_wide, current_wide = (
        padded_2(tracers, (("lat", 2), ("lon", 3)), 3),
        padded_2(velocity, (("lat", 2), ("lon", 3)), 3),
    )
    current_wide = trim(current_wide, 2)
    tracer_wide = jnp.where(inside(3), tracer_wide, 0.0)
    current_wide = jnp.where(inside(1), current_wide, 0.0)
    tracers_new, star_u, star_v, east_inner, north_inner, means = baroclinic(
        tracer_wide, current_wide, trim(bottom_wide, deep - 3), row_first, rows_total, wind
    )
    start_u, start_v, force_u, force_v, mean_u, mean_v = means
    depth_u_wide = thickness * jnp.minimum(bottom_wide, slide(bottom_wide, 0, 1)).astype(
        jnp.float32
    )
    depth_v_wide = thickness * jnp.minimum(bottom_wide, slide(bottom_wide, 1, 0)).astype(
        jnp.float32
    )
    opening_state = None
    opening = padded_2(
        jnp.stack([force_u, force_v, surface, start_u, start_v]), (("lat", 1), ("lon", 2)), deep
    )
    opening = jnp.where(inside(deep), opening, 0.0)
    forcing_wide = opening[0:2]
    opening_state = opening[2:5]
    coriolis_u = coriolis_rows(deep, 0.5)
    coriolis_v = coriolis_rows(deep, 1.0)
    height, flow_u, flow_v = (surface, start_u, start_v)
    running_u = jnp.zeros_like(start_u)
    running_v = jnp.zeros_like(start_v)

    def advance(turn_index, carry):
        level_now, east_now, north_now, east_sum, north_sum = carry
        level_now, east_now, north_now = substep(
            level_now,
            east_now,
            north_now,
            forcing_wide[0],
            forcing_wide[1],
            depth_u_wide,
            depth_v_wide,
            coriolis_u,
            coriolis_v,
            slide,
        )
        return (level_now, east_now, north_now, east_sum + east_now, north_sum + north_now)

    for block_index in range(SUBSTEPS // deep):
        if block_index == 0 and opening_state is not None:
            state_wide = opening_state
        else:
            state_wide = padded_2(
                jnp.stack([height, flow_u, flow_v]), (("lat", 1), ("lon", 2)), deep
            )
            state_wide = jnp.where(inside(deep), state_wide, 0.0)
        zeros_wide = jnp.zeros_like(state_wide[0])
        level_now, east_now, north_now, east_sum, north_sum = lax.fori_loop(
            0, deep, advance, (state_wide[0], state_wide[1], state_wide[2], zeros_wide, zeros_wide)
        )
        height = trim(level_now, deep)
        flow_u = trim(east_now, deep)
        flow_v = trim(north_now, deep)
        running_u = running_u + trim(east_sum, deep)
        running_v = running_v + trim(north_sum, deep)
    average_u = running_u / SUBSTEPS
    average_v = running_v / SUBSTEPS
    velocity_new = jnp.stack(
        [east_inner * (star_u - mean_u + average_u), north_inner * (star_v - mean_v + average_v)]
    )
    transport = trim(depth_u_wide, deep) * average_u
    local_totals = jnp.sum(transport, axis=0)
    before = prefix(local_totals, "lat", add_parts, jnp.zeros_like(local_totals))
    streamfunction = -(before[None] + jnp.cumsum(transport, axis=0))
    return (tracers_new, velocity_new, height, streamfunction)


def solution(mesh):
    placed = (
        P(None, None, "lat", "lon"),
        P(None, None, "lat", "lon"),
        P("lat", "lon"),
        P(None, "lat", "lon"),
        P("lat", "lon"),
    )
    return jax.shard_map(
        shards,
        mesh=mesh,
        in_specs=placed,
        out_specs=(
            P(None, None, "lat", "lon"),
            P(None, None, "lat", "lon"),
            P("lat", "lon"),
            P("lat", "lon"),
        ),
        check_vma=False,
    )
```

profile of v0, /device:TPU:1, one launch (start us, length us, event | category | flops | bytes accessed | tf_op | source)
XLA Modules:
  0.0 185.4 jit_solution(1672034750788433161)
XLA Ops:
  1.7 8.8 %collective-permute-start.1 = (f32[4,8,3,128]{3,2,1,0:T(4,128)S(1)}, f32[4,8,3,128]{3,2,1,0:T(4,128)S(1)}, u32[]{:S(2)}, u32[]{:S(2)}) collective-permute-start(f32[4,8,3,128]{3,2,1,0:T(4,128)S(1)} %get-tuple-element.859), channel_id=1, source_target_pairs={{32,0},{64,32},{96,64},{128,96},{160,128},{192,160},{224,192},{256... | collective-permute-start | bytes 147464 | tf_op jit(solution)/shard_map/ppermute | solution.py:30
  10.5 1.9 %collective-permute-start = (f32[4,8,3,128]{3,2,1,0:T(4,128)S(1)}, f32[4,8,3,128]{3,2,1,0:T(4,128)S(1)}, u32[]{:S(2)}, u32[]{:S(2)}) collective-permute-start(f32[4,8,3,128]{3,2,1,0:T(4,128)S(1)} %get-tuple-element.858), channel_id=1, source_target_pairs={{0,32},{32,64},{64,96},{96,128},{128,160},{160,192},{192,224},{224... | collective-permute-start | bytes 147464 | tf_op jit(solution)/shard_map/ppermute | solution.py:27
  12.4 2.4 %collective-permute-start.5 = (s32[10,128]{1,0:T(8,128)S(1)}, s32[10,128]{1,0:T(8,128)S(1)}, u32[]{:S(2)}, u32[]{:S(2)}) collective-permute-start(s32[10,128]{1,0:T(8,128)S(1)} %get-tuple-element.894), channel_id=1, source_target_pairs={{32,0},{64,32},{96,64},{128,96},{160,128},{192,160},{224,192},{256... | collective-permute-start | bytes 15368 | tf_op jit(solution)/shard_map/ppermute | solution.py:30
  14.8 3.2 %collective-permute-start.4 = (s32[10,128]{1,0:T(8,128)S(1)}, s32[10,128]{1,0:T(8,128)S(1)}, u32[]{:S(2)}, u32[]{:S(2)}) collective-permute-start(s32[10,128]{1,0:T(8,128)S(1)} %get-tuple-element.893), channel_id=1, source_target_pairs={{0,32},{32,64},{64,96},{96,128},{128,160},{160,192},{192,224},{224... | collective-permute-start | bytes 15368 | tf_op jit(solution)/shard_map/ppermute | solution.py:27
  18.1 4.0 %collective-permute-start.9 = (f32[2,8,3,128]{3,2,1,0:T(4,128)S(1)}, f32[2,8,3,128]{3,2,1,0:T(4,128)S(1)}, u32[]{:S(2)}, u32[]{:S(2)}) collective-permute-start(f32[2,8,3,128]{3,2,1,0:T(4,128)S(1)} %get-tuple-element.867), channel_id=1, source_target_pairs={{32,0},{64,32},{96,64},{128,96},{160,128},{192,160},{224,192},{256... | collective-permute-start | bytes 73736 | tf_op jit(solution)/shard_map/ppermute | solution.py:30
  22.3 11.3 %collective-permute-start.7 = (s32[36,10]{1,0:T(8,128)S(1)}, s32[36,10]{1,0:T(8,128)S(1)}, u32[]{:S(2)}, u32[]{:S(2)}) collective-permute-start(s32[36,10]{1,0:T(8,128)S(1)} %get-tuple-element.890), channel_id=1, source_target_pairs={{1,0},{2,1},{3,2},{4,3},{5,4},{6,5},{7,6},{8,7},{9,8},{10,9},{11,1... | collective-permute-start | bytes 4328 | tf_op jit(solution)/shard_map/ppermute | solution.py:30
  33.6 1.9 %collective-permute-start.6 = (s32[36,10]{1,0:T(8,128)S(1)}, s32[36,10]{1,0:T(8,128)S(1)}, u32[]{:S(2)}, u32[]{:S(2)}) collective-permute-start(s32[36,10]{1,0:T(8,128)S(1)} %get-tuple-element.889), channel_id=1, source_target_pairs={{0,1},{1,2},{2,3},{3,4},{4,5},{5,6},{6,7},{7,8},{8,9},{9,10},{10,1... | collective-permute-start | bytes 4328 | tf_op jit(solution)/shard_map/ppermute | solution.py:27
  35.6 1.9 %collective-permute-start.8 = (f32[2,8,3,128]{3,2,1,0:T(4,128)S(1)}, f32[2,8,3,128]{3,2,1,0:T(4,128)S(1)}, u32[]{:S(2)}, u32[]{:S(2)}) collective-permute-start(f32[2,8,3,128]{3,2,1,0:T(4,128)S(1)} %get-tuple-element.866), channel_id=1, source_target_pairs={{0,32},{32,64},{64,96},{96,128},{128,160},{160,192},{192,224},{224... | collective-permute-start | bytes 73736 | tf_op jit(solution)/shard_map/ppermute | solution.py:27
  37.5 4.2 %collective-permute-done.6 = s32[36,10]{1,0:T(8,128)S(1)} collective-permute-done((s32[36,10]{1,0:T(8,128)S(1)}, s32[36,10]{1,0:T(8,128)S(1)}, u32[]{:S(2)}, u32[]{:S(2)}) %collective-permute-start.6) | collective-permute-done | bytes 1472 | tf_op jit(solution)/shard_map/ppermute | solution.py:27
  42.5 7.3 %collective-permute-start.11 = (f32[2,8,22,3]{3,2,1,0:T(8,128)S(1)}, f32[2,8,22,3]{3,2,1,0:T(8,128)S(1)}, u32[]{:S(2)}, u32[]{:S(2)}) collective-permute-start(f32[2,8,22,3]{3,2,1,0:T(8,128)S(1)} %get-tuple-element.864), channel_id=1, source_target_pairs={{1,0},{2,1},{3,2},{4,3},{5,4},{6,5},{7,6},{8,7},{9,8},{10,9},{11,1... | collective-permute-start | bytes 12680 | tf_op jit(solution)/shard_map/ppermute | solution.py:30
  49.7 1.9 %collective-permute-start.10 = (f32[2,8,22,3]{3,2,1,0:T(8,128)S(1)}, f32[2,8,22,3]{3,2,1,0:T(8,128)S(1)}, u32[]{:S(2)}, u32[]{:S(2)}) collective-permute-start(f32[2,8,22,3]{3,2,1,0:T(8,128)S(1)} %get-tuple-element.863), channel_id=1, source_target_pairs={{0,1},{1,2},{2,3},{3,4},{4,5},{5,6},{6,7},{7,8},{8,9},{9,10},{10,1... | collective-permute-start | bytes 12680 | tf_op jit(solution)/shard_map/ppermute | solution.py:27
  52.3 7.4 %collective-permute-done.10 = f32[2,8,22,3]{3,2,1,0:T(8,128)S(1)} collective-permute-done((f32[2,8,22,3]{3,2,1,0:T(8,128)S(1)}, f32[2,8,22,3]{3,2,1,0:T(8,128)S(1)}, u32[]{:S(2)}, u32[]{:S(2)}) %collective-permute-start.10) | collective-permute-done | bytes 4256 | tf_op jit(solution)/shard_map/ppermute | solution.py:27
  61.5 1.9 %collective-permute-start.3 = (f32[4,8,22,3]{3,2,1,0:T(8,128)S(1)}, f32[4,8,22,3]{3,2,1,0:T(8,128)S(1)}, u32[]{:S(2)}, u32[]{:S(2)}) collective-permute-start(f32[4,8,22,3]{3,2,1,0:T(8,128)S(1)} %get-tuple-element.857), channel_id=1, source_target_pairs={{1,0},{2,1},{3,2},{4,3},{5,4},{6,5},{7,6},{8,7},{9,8},{10,9},{11,1... | collective-permute-start | bytes 25352 | tf_op jit(solution)/shard_map/ppermute | solution.py:30
  63.5 4.9 %collective-permute-start.2 = (f32[4,8,22,3]{3,2,1,0:T(8,128)S(1)}, f32[4,8,22,3]{3,2,1,0:T(8,128)S(1)}, u32[]{:S(2)}, u32[]{:S(2)}) collective-permute-start(f32[4,8,22,3]{3,2,1,0:T(8,128)S(1)} %get-tuple-element.856), channel_id=1, source_target_pairs={{0,1},{1,2},{2,3},{3,4},{4,5},{5,6},{6,7},{7,8},{8,9},{9,10},{10,1... | collective-permute-start | bytes 25352 | tf_op jit(solution)/shard_map/ppermute | solution.py:27
  68.5 7.6 %collective-permute-done.3 = f32[4,8,22,3]{3,2,1,0:T(8,128)S(1)} collective-permute-done((f32[4,8,22,3]{3,2,1,0:T(8,128)S(1)}, f32[4,8,22,3]{3,2,1,0:T(8,128)S(1)}, u32[]{:S(2)}, u32[]{:S(2)}) %collective-permute-start.3) | collective-permute-done | bytes 8480 | tf_op jit(solution)/shard_map/ppermute | solution.py:30
  76.1 2.5 %collective-permute-done.2 = f32[4,8,22,3]{3,2,1,0:T(8,128)S(1)} collective-permute-done((f32[4,8,22,3]{3,2,1,0:T(8,128)S(1)}, f32[4,8,22,3]{3,2,1,0:T(8,128)S(1)}, u32[]{:S(2)}, u32[]{:S(2)}) %collective-permute-start.2) | collective-permute-done | bytes 8480 | tf_op jit(solution)/shard_map/ppermute | solution.py:27
  80.5 8.2 %collective-permute-start.13 = (f32[5,10,128]{2,1,0:T(8,128)S(1)}, f32[5,10,128]{2,1,0:T(8,128)S(1)}, u32[]{:S(2)}, u32[]{:S(2)}) collective-permute-start(f32[5,10,128]{2,1,0:T(8,128)S(1)} %get-tuple-element.884), channel_id=1, source_target_pairs={{32,0},{64,32},{96,64},{128,96},{160,128},{192,160},{224,192},{256... | collective-permute-start | bytes 76808 | tf_op jit(solution)/shard_map/ppermute | solution.py:30
  88.7 1.9 %collective-permute-start.12 = (f32[5,10,128]{2,1,0:T(8,128)S(1)}, f32[5,10,128]{2,1,0:T(8,128)S(1)}, u32[]{:S(2)}, u32[]{:S(2)}) collective-permute-start(f32[5,10,128]{2,1,0:T(8,128)S(1)} %get-tuple-element.883), channel_id=1, source_target_pairs={{0,32},{32,64},{64,96},{96,128},{128,160},{160,192},{192,224},{224... | collective-permute-start | bytes 76808 | tf_op jit(solution)/shard_map/ppermute | solution.py:27
  92.2 6.8 %collective-permute-start.15 = (f32[5,36,10]{2,1,0:T(8,128)S(1)}, f32[5,36,10]{2,1,0:T(8,128)S(1)}, u32[]{:S(2)}, u32[]{:S(2)}) collective-permute-start(f32[5,36,10]{2,1,0:T(8,128)S(1)} %get-tuple-element.875), channel_id=1, source_target_pairs={{1,0},{2,1},{3,2},{4,3},{5,4},{6,5},{7,6},{8,7},{9,8},{10,9},{11,1... | collective-permute-start | bytes 21608 | tf_op jit(solution)/shard_map/ppermute | solution.py:30
  99.0 1.9 %collective-permute-start.14 = (f32[5,36,10]{2,1,0:T(8,128)S(1)}, f32[5,36,10]{2,1,0:T(8,128)S(1)}, u32[]{:S(2)}, u32[]{:S(2)}) collective-permute-start(f32[5,36,10]{2,1,0:T(8,128)S(1)} %get-tuple-element.874), channel_id=1, source_target_pairs={{0,1},{1,2},{2,3},{3,4},{4,5},{5,6},{6,7},{7,8},{8,9},{9,10},{10,1... | collective-permute-start | bytes 21608 | tf_op jit(solution)/shard_map/ppermute | solution.py:27
  101.7 6.3 %collective-permute-done.14 = f32[5,36,10]{2,1,0:T(8,128)S(1)} collective-permute-done((f32[5,36,10]{2,1,0:T(8,128)S(1)}, f32[5,36,10]{2,1,0:T(8,128)S(1)}, u32[]{:S(2)}, u32[]{:S(2)}) %collective-permute-start.14) | collective-permute-done | bytes 7232 | tf_op jit(solution)/shard_map/ppermute | solution.py:27
  108.3 3.4 %while.80 = (s32[]{:T(128)}, f32[36,148]{1,0:T(8,128)S(1)}, f32[36,148]{1,0:T(8,128)S(1)}, f32[36,148]{1,0:T(8,128)S(1)}, f32[36,148]{1,0:T(8,128)S(1)}, /*index...) while((s32[]{:T(128)}, f32[36,148]{1,0:T(8,128)S(1)}, ...), condition=%wide.region_9.10_spmd.clone.clone.clone, body=%wide.region_8.9_spmd.clone.clone.clone.sunk | while | flops 186879 | bytes 576139 | solution.py:313
  111.8 8.3 %collective-permute-start.17 = (f32[3,10,128]{2,1,0:T(8,128)S(1)}, f32[3,10,128]{2,1,0:T(8,128)S(1)}, u32[]{:S(2)}, u32[]{:S(2)}) collective-permute-start(f32[3,10,128]{2,1,0:T(8,128)S(1)} %get-tuple-element.888), channel_id=1, source_target_pairs={{32,0},{64,32},{96,64},{128,96},{160,128},{192,160},{224,192},{256... | collective-permute-start | bytes 46088 | tf_op jit(solution)/shard_map/ppermute | solution.py:30
  120.1 1.9 %collective-permute-start.16 = (f32[3,10,128]{2,1,0:T(8,128)S(1)}, f32[3,10,128]{2,1,0:T(8,128)S(1)}, u32[]{:S(2)}, u32[]{:S(2)}) collective-permute-start(f32[3,10,128]{2,1,0:T(8,128)S(1)} %get-tuple-element.887), channel_id=1, source_target_pairs={{0,32},{32,64},{64,96},{96,128},{128,160},{160,192},{192,224},{224... | collective-permute-start | bytes 46088 | tf_op jit(solution)/shard_map/ppermute | solution.py:27
  125.2 4.9 %collective-permute-start.18 = (f32[3,36,10]{2,1,0:T(8,128)S(1)}, f32[3,36,10]{2,1,0:T(8,128)S(1)}, u32[]{:S(2)}, u32[]{:S(2)}) collective-permute-start(f32[3,36,10]{2,1,0:T(8,128)S(1)} %get-tuple-element.879), channel_id=1, source_target_pairs={{0,1},{1,2},{2,3},{3,4},{4,5},{5,6},{6,7},{7,8},{8,9},{9,10},{10,1... | collective-permute-start | bytes 12968 | tf_op jit(solution)/shard_map/ppermute | solution.py:27
  131.0 2.8 %collective-permute-done.18 = f32[3,36,10]{2,1,0:T(8,128)S(1)} collective-permute-done((f32[3,36,10]{2,1,0:T(8,128)S(1)}, f32[3,36,10]{2,1,0:T(8,128)S(1)}, u32[]{:S(2)}, u32[]{:S(2)}) %collective-permute-start.18) | collective-permute-done | bytes 4352 | tf_op jit(solution)/shard_map/ppermute | solution.py:27
  134.0 3.3 %while.81 = (s32[]{:T(128)}, f32[36,148]{1,0:T(8,128)S(1)}, f32[36,148]{1,0:T(8,128)S(1)}, f32[36,148]{1,0:T(8,128)S(1)}, f32[36,148]{1,0:T(8,128)S(1)}, /*index...) while((s32[]{:T(128)}, f32[36,148]{1,0:T(8,128)S(1)}, ...), condition=%wide.region_11.12_spmd.clone.clone.clone, body=%wide.region_10.11_spmd.clone.clone.clone.sunk | while | flops 186879 | bytes 576139 | solution.py:313
  137.5 7.2 %collective-permute-start.21 = (f32[3,10,128]{2,1,0:T(8,128)S(1)}, f32[3,10,128]{2,1,0:T(8,128)S(1)}, u32[]{:S(2)}, u32[]{:S(2)}) collective-permute-start(f32[3,10,128]{2,1,0:T(8,128)S(1)} %get-tuple-element.886), channel_id=1, source_target_pairs={{32,0},{64,32},{96,64},{128,96},{160,128},{192,160},{224,192},{256... | collective-permute-start | bytes 46088 | tf_op jit(solution)/shard_map/ppermute | solution.py:30
  149.9 4.9 %collective-permute-start.22 = (f32[3,36,10]{2,1,0:T(8,128)S(1)}, f32[3,36,10]{2,1,0:T(8,128)S(1)}, u32[]{:S(2)}, u32[]{:S(2)}) collective-permute-start(f32[3,36,10]{2,1,0:T(8,128)S(1)} %get-tuple-element.877), channel_id=1, source_target_pairs={{0,1},{1,2},{2,3},{3,4},{4,5},{5,6},{6,7},{7,8},{8,9},{9,10},{10,1... | collective-permute-start | bytes 12968 | tf_op jit(solution)/shard_map/ppermute | solution.py:27
  154.8 3.7 %collective-permute-done.22 = f32[3,36,10]{2,1,0:T(8,128)S(1)} collective-permute-done((f32[3,36,10]{2,1,0:T(8,128)S(1)}, f32[3,36,10]{2,1,0:T(8,128)S(1)}, u32[]{:S(2)}, u32[]{:S(2)}) %collective-permute-start.22) | collective-permute-done | bytes 4352 | tf_op jit(solution)/shard_map/ppermute | solution.py:27
  158.6 3.3 %while.82 = (s32[]{:T(128)}, f32[36,148]{1,0:T(8,128)S(1)}, f32[36,148]{1,0:T(8,128)S(1)}, f32[36,148]{1,0:T(8,128)S(1)}, f32[36,148]{1,0:T(8,128)S(1)}, /*index...) while((s32[]{:T(128)}, f32[36,148]{1,0:T(8,128)S(1)}, ...), condition=%wide.region_13.14_spmd.clone.clone.clone, body=%wide.region_12.13_spmd.clone.clone.clone.sunk | while | flops 186879 | bytes 576139 | solution.py:313
  162.7 21.0 %all-gather.1 = f32[16,1,128]{2,1,0:T(1,128)S(1)} all-gather(f32[1,1,128]{2,1,0:T(1,128)S(1)} %bitcast.142), channel_id=2, replica_groups=mesh['lat'=16,'lon'=32] {'lat'}, dimensions={0}, use_global_device_ids=true | all-gather | bytes 8704 | tf_op jit(solution)/shard_map/all_gather | solution.py:37
  (319 shorter events, 29.1 us)
Async XLA Ops:
  0.6 17.4 %copy-start.1 = (f32[2,8,16,128]{3,2,1,0:T(8,128)S(1)}, f32[2,8,16,128]{3,2,1,0:T(8,128)}, u32[]{:S(2)}) copy-start(f32[2,8,16,128]{3,2,1,0:T(8,128)} %param.14) | copy-start | bytes 393220
  0.6 11.8 %copy-start.2 = (s32[16,128]{1,0:T(8,128)S(1)}, s32[16,128]{1,0:T(8,128)}, u32[]{:S(2)}) copy-start(s32[16,128]{1,0:T(8,128)} %param.17) | copy-start | bytes 24580
  1.7 58.8 %collective-permute-start.1 = (f32[4,8,3,128]{3,2,1,0:T(4,128)S(1)}, f32[4,8,3,128]{3,2,1,0:T(4,128)S(1)}, u32[]{:S(2)}, u32[]{:S(2)}) collective-permute-start(f32[4,8,3,128]{3,2,1,0:T(4,128)S(1)} %get-tuple-element.859), channel_id=1, source_target_pairs={{32,0},{64,32},{96,64},{128,96},{160,128},{192,160},{224,192},{256... | collective-permute-start | bytes 147464 | tf_op jit(solution)/shard_map/ppermute | solution.py:30
  10.5 50.0 %collective-permute-start = (f32[4,8,3,128]{3,2,1,0:T(4,128)S(1)}, f32[4,8,3,128]{3,2,1,0:T(4,128)S(1)}, u32[]{:S(2)}, u32[]{:S(2)}) collective-permute-start(f32[4,8,3,128]{3,2,1,0:T(4,128)S(1)} %get-tuple-element.858), channel_id=1, source_target_pairs={{0,32},{32,64},{64,96},{96,128},{128,160},{160,192},{192,224},{224... | collective-permute-start | bytes 147464 | tf_op jit(solution)/shard_map/ppermute | solution.py:27
  12.4 9.8 %collective-permute-start.5 = (s32[10,128]{1,0:T(8,128)S(1)}, s32[10,128]{1,0:T(8,128)S(1)}, u32[]{:S(2)}, u32[]{:S(2)}) collective-permute-start(s32[10,128]{1,0:T(8,128)S(1)} %get-tuple-element.894), channel_id=1, source_target_pairs={{32,0},{64,32},{96,64},{128,96},{160,128},{192,160},{224,192},{256... | collective-permute-start | bytes 15368 | tf_op jit(solution)/shard_map/ppermute | solution.py:30
  14.8 7.4 %collective-permute-start.4 = (s32[10,128]{1,0:T(8,128)S(1)}, s32[10,128]{1,0:T(8,128)S(1)}, u32[]{:S(2)}, u32[]{:S(2)}) collective-permute-start(s32[10,128]{1,0:T(8,128)S(1)} %get-tuple-element.893), channel_id=1, source_target_pairs={{0,32},{32,64},{64,96},{96,128},{128,160},{160,192},{192,224},{224... | collective-permute-start | bytes 15368 | tf_op jit(solution)/shard_map/ppermute | solution.py:27
  18.0 4.1 %copy-start.3 = (f32[2,16,128]{2,1,0:T(8,128)S(1)}, f32[2,16,128]{2,1,0:T(8,128)}, u32[]{:S(2)}) copy-start(f32[2,16,128]{2,1,0:T(8,128)} %param.16) | copy-start | bytes 49156
  18.1 23.8 %collective-permute-start.9 = (f32[2,8,3,128]{3,2,1,0:T(4,128)S(1)}, f32[2,8,3,128]{3,2,1,0:T(4,128)S(1)}, u32[]{:S(2)}, u32[]{:S(2)}) collective-permute-start(f32[2,8,3,128]{3,2,1,0:T(4,128)S(1)} %get-tuple-element.867), channel_id=1, source_target_pairs={{32,0},{64,32},{96,64},{128,96},{160,128},{192,160},{224,192},{256... | collective-permute-start | bytes 73736 | tf_op jit(solution)/shard_map/ppermute | solution.py:30
  22.3 13.3 %collective-permute-start.7 = (s32[36,10]{1,0:T(8,128)S(1)}, s32[36,10]{1,0:T(8,128)S(1)}, u32[]{:S(2)}, u32[]{:S(2)}) collective-permute-start(s32[36,10]{1,0:T(8,128)S(1)} %get-tuple-element.890), channel_id=1, source_target_pairs={{1,0},{2,1},{3,2},{4,3},{5,4},{6,5},{7,6},{8,7},{9,8},{10,9},{11,1... | collective-permute-start | bytes 4328 | tf_op jit(solution)/shard_map/ppermute | solution.py:30
  33.6 8.1 %collective-permute-start.6 = (s32[36,10]{1,0:T(8,128)S(1)}, s32[36,10]{1,0:T(8,128)S(1)}, u32[]{:S(2)}, u32[]{:S(2)}) collective-permute-start(s32[36,10]{1,0:T(8,128)S(1)} %get-tuple-element.889), channel_id=1, source_target_pairs={{0,1},{1,2},{2,3},{3,4},{4,5},{5,6},{6,7},{7,8},{8,9},{9,10},{10,1... | collective-permute-start | bytes 4328 | tf_op jit(solution)/shard_map/ppermute | solution.py:27
  35.6 6.7 %collective-permute-start.8 = (f32[2,8,3,128]{3,2,1,0:T(4,128)S(1)}, f32[2,8,3,128]{3,2,1,0:T(4,128)S(1)}, u32[]{:S(2)}, u32[]{:S(2)}) collective-permute-start(f32[2,8,3,128]{3,2,1,0:T(4,128)S(1)} %get-tuple-element.866), channel_id=1, source_target_pairs={{0,32},{32,64},{64,96},{96,128},{128,160},{160,192},{192,224},{224... | collective-permute-start | bytes 73736 | tf_op jit(solution)/shard_map/ppermute | solution.py:27
  42.5 9.9 %collective-permute-start.11 = (f32[2,8,22,3]{3,2,1,0:T(8,128)S(1)}, f32[2,8,22,3]{3,2,1,0:T(8,128)S(1)}, u32[]{:S(2)}, u32[]{:S(2)}) collective-permute-start(f32[2,8,22,3]{3,2,1,0:T(8,128)S(1)} %get-tuple-element.864), channel_id=1, source_target_pairs={{1,0},{2,1},{3,2},{4,3},{5,4},{6,5},{7,6},{8,7},{9,8},{10,9},{11,1... | collective-permute-start | bytes 12680 | tf_op jit(solution)/shard_map/ppermute | solution.py:30
  49.7 10.0 %collective-permute-start.10 = (f32[2,8,22,3]{3,2,1,0:T(8,128)S(1)}, f32[2,8,22,3]{3,2,1,0:T(8,128)S(1)}, u32[]{:S(2)}, u32[]{:S(2)}) collective-permute-start(f32[2,8,22,3]{3,2,1,0:T(8,128)S(1)} %get-tuple-element.863), channel_id=1, source_target_pairs={{0,1},{1,2},{2,3},{3,4},{4,5},{5,6},{6,7},{7,8},{8,9},{9,10},{10,1... | collective-permute-start | bytes 12680 | tf_op jit(solution)/shard_map/ppermute | solution.py:27
  60.3 1.0 copy-start
  61.5 14.5 %collective-permute-start.3 = (f32[4,8,22,3]{3,2,1,0:T(8,128)S(1)}, f32[4,8,22,3]{3,2,1,0:T(8,128)S(1)}, u32[]{:S(2)}, u32[]{:S(2)}) collective-permute-start(f32[4,8,22,3]{3,2,1,0:T(8,128)S(1)} %get-tuple-element.857), channel_id=1, source_target_pairs={{1,0},{2,1},{3,2},{4,3},{5,4},{6,5},{7,6},{8,7},{9,8},{10,9},{11,1... | collective-permute-start | bytes 25352 | tf_op jit(solution)/shard_map/ppermute | solution.py:30
  63.5 15.1 %collective-permute-start.2 = (f32[4,8,22,3]{3,2,1,0:T(8,128)S(1)}, f32[4,8,22,3]{3,2,1,0:T(8,128)S(1)}, u32[]{:S(2)}, u32[]{:S(2)}) collective-permute-start(f32[4,8,22,3]{3,2,1,0:T(8,128)S(1)} %get-tuple-element.856), channel_id=1, source_target_pairs={{0,1},{1,2},{2,3},{3,4},{4,5},{5,6},{6,7},{7,8},{8,9},{9,10},{10,1... | collective-permute-start | bytes 25352 | tf_op jit(solution)/shard_map/ppermute | solution.py:27
  79.8 0.7 copy-start.4
  80.5 10.3 %collective-permute-start.13 = (f32[5,10,128]{2,1,0:T(8,128)S(1)}, f32[5,10,128]{2,1,0:T(8,128)S(1)}, u32[]{:S(2)}, u32[]{:S(2)}) collective-permute-start(f32[5,10,128]{2,1,0:T(8,128)S(1)} %get-tuple-element.884), channel_id=1, source_target_pairs={{32,0},{64,32},{96,64},{128,96},{160,128},{192,160},{224,192},{256... | collective-permute-start | bytes 76808 | tf_op jit(solution)/shard_map/ppermute | solution.py:30
  88.7 3.3 %collective-permute-start.12 = (f32[5,10,128]{2,1,0:T(8,128)S(1)}, f32[5,10,128]{2,1,0:T(8,128)S(1)}, u32[]{:S(2)}, u32[]{:S(2)}) collective-permute-start(f32[5,10,128]{2,1,0:T(8,128)S(1)} %get-tuple-element.883), channel_id=1, source_target_pairs={{0,32},{32,64},{64,96},{96,128},{128,160},{160,192},{192,224},{224... | collective-permute-start | bytes 76808 | tf_op jit(solution)/shard_map/ppermute | solution.py:27
  92.2 9.5 %collective-permute-start.15 = (f32[5,36,10]{2,1,0:T(8,128)S(1)}, f32[5,36,10]{2,1,0:T(8,128)S(1)}, u32[]{:S(2)}, u32[]{:S(2)}) collective-permute-start(f32[5,36,10]{2,1,0:T(8,128)S(1)} %get-tuple-element.875), channel_id=1, source_target_pairs={{1,0},{2,1},{3,2},{4,3},{5,4},{6,5},{7,6},{8,7},{9,8},{10,9},{11,1... | collective-permute-start | bytes 21608 | tf_op jit(solution)/shard_map/ppermute | solution.py:30
  99.0 9.0 %collective-permute-start.14 = (f32[5,36,10]{2,1,0:T(8,128)S(1)}, f32[5,36,10]{2,1,0:T(8,128)S(1)}, u32[]{:S(2)}, u32[]{:S(2)}) collective-permute-start(f32[5,36,10]{2,1,0:T(8,128)S(1)} %get-tuple-element.874), channel_id=1, source_target_pairs={{0,1},{1,2},{2,3},{3,4},{4,5},{5,6},{6,7},{7,8},{8,9},{9,10},{10,1... | collective-permute-start | bytes 21608 | tf_op jit(solution)/shard_map/ppermute | solution.py:27
  111.8 10.9 %collective-permute-start.17 = (f32[3,10,128]{2,1,0:T(8,128)S(1)}, f32[3,10,128]{2,1,0:T(8,128)S(1)}, u32[]{:S(2)}, u32[]{:S(2)}) collective-permute-start(f32[3,10,128]{2,1,0:T(8,128)S(1)} %get-tuple-element.888), channel_id=1, source_target_pairs={{32,0},{64,32},{96,64},{128,96},{160,128},{192,160},{224,192},{256... | collective-permute-start | bytes 46088 | tf_op jit(solution)/shard_map/ppermute | solution.py:30
  120.1 3.1 %collective-permute-start.16 = (f32[3,10,128]{2,1,0:T(8,128)S(1)}, f32[3,10,128]{2,1,0:T(8,128)S(1)}, u32[]{:S(2)}, u32[]{:S(2)}) collective-permute-start(f32[3,10,128]{2,1,0:T(8,128)S(1)} %get-tuple-element.887), channel_id=1, source_target_pairs={{0,32},{32,64},{64,96},{96,128},{128,160},{160,192},{192,224},{224... | collective-permute-start | bytes 46088 | tf_op jit(solution)/shard_map/ppermute | solution.py:27
  123.3 7.7 %collective-permute-start.19 = (f32[3,36,10]{2,1,0:T(8,128)S(1)}, f32[3,36,10]{2,1,0:T(8,128)S(1)}, u32[]{:S(2)}, u32[]{:S(2)}) collective-permute-start(f32[3,36,10]{2,1,0:T(8,128)S(1)} %get-tuple-element.880), channel_id=1, source_target_pairs={{1,0},{2,1},{3,2},{4,3},{5,4},{6,5},{7,6},{8,7},{9,8},{10,9},{11,1... | collective-permute-start | bytes 12968 | tf_op jit(solution)/shard_map/ppermute | solution.py:30
  125.2 8.6 %collective-permute-start.18 = (f32[3,36,10]{2,1,0:T(8,128)S(1)}, f32[3,36,10]{2,1,0:T(8,128)S(1)}, u32[]{:S(2)}, u32[]{:S(2)}) collective-permute-start(f32[3,36,10]{2,1,0:T(8,128)S(1)} %get-tuple-element.879), channel_id=1, source_target_pairs={{0,1},{1,2},{2,3},{3,4},{4,5},{5,6},{6,7},{7,8},{8,9},{9,10},{10,1... | collective-permute-start | bytes 12968 | tf_op jit(solution)/shard_map/ppermute | solution.py:27
  137.5 9.2 %collective-permute-start.21 = (f32[3,10,128]{2,1,0:T(8,128)S(1)}, f32[3,10,128]{2,1,0:T(8,128)S(1)}, u32[]{:S(2)}, u32[]{:S(2)}) collective-permute-start(f32[3,10,128]{2,1,0:T(8,128)S(1)} %get-tuple-element.886), channel_id=1, source_target_pairs={{32,0},{64,32},{96,64},{128,96},{160,128},{192,160},{224,192},{256... | collective-permute-start | bytes 46088 | tf_op jit(solution)/shard_map/ppermute | solution.py:30
  144.8 3.1 %collective-permute-start.20 = (f32[3,10,128]{2,1,0:T(8,128)S(1)}, f32[3,10,128]{2,1,0:T(8,128)S(1)}, u32[]{:S(2)}, u32[]{:S(2)}) collective-permute-start(f32[3,10,128]{2,1,0:T(8,128)S(1)} %get-tuple-element.885), channel_id=1, source_target_pairs={{0,32},{32,64},{64,96},{96,128},{128,160},{160,192},{192,224},{224... | collective-permute-start | bytes 46088 | tf_op jit(solution)/shard_map/ppermute | solution.py:27
  148.0 6.8 %collective-permute-start.23 = (f32[3,36,10]{2,1,0:T(8,128)S(1)}, f32[3,36,10]{2,1,0:T(8,128)S(1)}, u32[]{:S(2)}, u32[]{:S(2)}) collective-permute-start(f32[3,36,10]{2,1,0:T(8,128)S(1)} %get-tuple-element.878), channel_id=1, source_target_pairs={{1,0},{2,1},{3,2},{4,3},{5,4},{6,5},{7,6},{8,7},{9,8},{10,9},{11,1... | collective-permute-start | bytes 12968 | tf_op jit(solution)/shard_map/ppermute | solution.py:30
  149.9 8.6 %collective-permute-start.22 = (f32[3,36,10]{2,1,0:T(8,128)S(1)}, f32[3,36,10]{2,1,0:T(8,128)S(1)}, u32[]{:S(2)}, u32[]{:S(2)}) collective-permute-start(f32[3,36,10]{2,1,0:T(8,128)S(1)} %get-tuple-element.877), channel_id=1, source_target_pairs={{0,1},{1,2},{2,3},{3,4},{4,5},{5,6},{6,7},{7,8},{8,9},{9,10},{10,1... | collective-permute-start | bytes 12968 | tf_op jit(solution)/shard_map/ppermute | solution.py:27
where the time goes:
time: 186 us; the launch traced here: 185 us
  starting transfers between devices  103 us (55%)
  waiting for transfers between devices  38.4 us (21%)
  blocking collectives  21 us (11%)
  other arithmetic  14.7 us (8%)
  local copies, waits for them, and re-layouts  4.75 us (3%)
  loops' own time  2.01 us (1%)
    ppermute x12, starting transfers between devices, padded_2(): lax.ppermute(lax.slice_in_dim(block, 0, width, axis=dim), axis, backward)  70 us
    ppermute x12, starting transfers between devices, padded_2(): lax.ppermute(lax.slice_in_dim(block, block.shape[dim] - width, None, axis...  33.1 us
    ppermute x12, waiting for transfers between devices, padded_2(): lax.ppermute(lax.slice_in_dim(block, block.shape[dim] - width, None, axis...  30.2 us
    all_gather x1, blocking collectives, prefix(): gathered = lax.all_gather(part, axis)  21 us
    ppermute x12, waiting for transfers between devices, padded_2(): lax.ppermute(lax.slice_in_dim(block, 0, width, axis=dim), axis, backward)  8.25 us
    add x30, other arithmetic, advance(): north_sum + north_now  4.36 us
  transfers between devices with their start and end apart: 24, of which 12 were waited for; matrix products, arithmetic and copies ran while one was open for 2% of the time, Pallas kernels for 0%

commit v1 on v0

v1 whole, which is shorter than its diff:
```python
import jax
import jax.numpy as jnp
from jax import lax
from jax.experimental import pallas as pl
from jax.experimental.pallas import tpu as pltpu
from jax.sharding import PartitionSpec as P

TRACERS = 4
LEVELS = 8
SUBSTEPS = 30
ROWS = 16
COLS = 128
MEMBERS = 16
HALO = 32
SLAB = 72
NLAT = ROWS * MEMBERS

time_step = 0.2
tracer_diffusion = 0.2
viscosity = 0.2
thermal_expansion = 2.0
haline_contraction = 1.5
coriolis_base = 1.0
gravity = 140.0
surface_scale = 40.0
thickness = 1.0 / LEVELS
f32 = jnp.float32

PRESSURE, EAST, NORTH, WIND, SURFACE, BOTTOM = 0, 8, 16, 24, 26, 27
PLANES = 28
MAIL_N, MAIL_S, EDGE, CHUNK = SLAB, SLAB + 8, SLAB + 16, SLAB + 24
BACK = 24


def at(values, step, axis):
    size = values.shape[axis]
    step %= size
    return values if step == 0 else pltpu.roll(values, size - step, axis)


def ids(shape, axis):
    return lax.broadcasted_iota(jnp.int32, shape, axis)


def wide(own, beside):
    return jnp.concatenate([own, beside], axis=1)


def tracer_planes(tracers_ref, bottom):
    return [
        [jnp.where(bottom > k, tracers_ref[t, k], 0.0) for k in range(LEVELS)]
        for t in range(TRACERS)
    ]


def pressures(salt, heat):
    total, out = None, []
    for k in range(LEVELS):
        density = haline_contraction * salt[k] - thermal_expansion * heat[k]
        total = density if total is None else total + density
        out.append(thickness * total)
    return out


def pack_kernel(tracers_ref, velocity_ref, surface_ref, wind_ref, bottom_ref, right_ref, left_ref):
    bottom = bottom_ref[...]
    c = tracer_planes(tracers_ref, bottom)
    planes = pressures(c[1], c[0])
    planes += [velocity_ref[d, k] for d in range(2) for k in range(LEVELS)]
    planes += [wind_ref[0], wind_ref[1], surface_ref[...], bottom.astype(f32)]
    lane = ids((ROWS, COLS), 1)
    for q in range(PLANES // 4):
        right = left = jnp.zeros((ROWS, COLS), f32)
        for s in range(4):
            moved = at(planes[4 * q + s], -32 * s, 1)
            right = jnp.where(lane // 32 == (s + 3) % 4, moved, right)
            left = jnp.where(lane // 32 == s, moved, left)
        right_ref[q] = right
        left_ref[q] = left
    right = left = jnp.zeros((ROWS, COLS), f32)
    for n in range(TRACERS * LEVELS):
        moved = at(c[n // LEVELS][n % LEVELS], -4 * n, 1)
        right = jnp.where(lane // 4 == (n + 31) % 32, moved, right)
        left = jnp.where(lane // 4 == n, moved, left)
    right_ref[PLANES // 4] = right
    left_ref[PLANES // 4] = left


def beside_plane(west_ref, east_ref, plane):
    q, s = divmod(plane, 4)
    block = ids((ROWS, COLS), 1) // 32
    both = jnp.where(
        block == s, east_ref[q], jnp.where(block == (s + 3) % 4, west_ref[q], 0.0)
    )
    return at(both, 32 * s, 1)


def beside_tracer(west_ref, east_ref, n):
    block = ids((ROWS, COLS), 1) // 4
    last = PLANES // 4
    both = jnp.where(
        block == n, east_ref[last], jnp.where(block == (n + 31) % 32, west_ref[last], 0.0)
    )
    return at(both, 4 * n, 1)


def momentum(k, u, v, p, wind, east, north, f_u, f_v, up, down):
    pair_v = v + down(v)
    pair_u = u + at(u, -1, 1)
    tend_u = (
        (0.25 * f_u) * (pair_v + at(pair_v, 1, 1))
        - (at(p, 1, 1) - p)
        + viscosity * (at(u, 1, 1) + at(u, -1, 1) + up(u) + down(u) - 4.0 * u)
    )
    tend_v = (
        (-0.25 * f_v) * (pair_u + up(pair_u))
        - (up(p) - p)
        + viscosity * (at(v, 1, 1) + at(v, -1, 1) + up(v) + down(v) - 4.0 * v)
    )
    if k == 0:
        tend_u = tend_u + wind[0]
        tend_v = tend_v + wind[1]
    return jnp.where(east, tend_u, 0.0), jnp.where(north, tend_v, 0.0)


def coriolis(rows, offset):
    return coriolis_base * (0.5 + (rows.astype(f32) + offset) / NLAT)


def send_kernel(
    place_ref, tracers_ref, velocity_ref, surface_ref, wind_ref, bottom_ref, west_ref, east_ref,
    out_ref, stack_ref, edge_ref, turned_ref,
):
    place = place_ref[0]
    bottom_own = bottom_ref[...]
    c = tracer_planes(tracers_ref, bottom_own)
    p_own = pressures(c[1], c[0])

    def whole(own, plane):
        return wide(own, beside_plane(west_ref, east_ref, plane))

    shape = (ROWS, 2 * COLS)
    row = ids(shape, 0)
    bottom = whole(bottom_own.astype(f32), BOTTOM)
    wind = [whole(wind_ref[d], WIND + d) for d in range(2)]

    def up(x):
        return jnp.where(row == ROWS - 1, 0.0, at(x, 1, 0))

    def down(x):
        return jnp.where(row == 0, 0.0, at(x, -1, 0))

    count_u = jnp.minimum(bottom, at(bottom, 1, 1))
    count_v = jnp.minimum(bottom, up(bottom))
    f_u = coriolis(place * ROWS + row, 0.5)
    f_v = coriolis(place * ROWS + row, 1.0)
    sums = [jnp.zeros(shape, f32) for _ in range(4)]
    us, vs, raws = [], [], []
    for k in range(LEVELS):
        east, north = count_u > k, count_v > k
        u = jnp.where(east, whole(velocity_ref[0, k], EAST + k), 0.0)
        raw = jnp.where(bottom > k, whole(velocity_ref[1, k], NORTH + k), 0.0)
        v = jnp.where(north, raw, 0.0)
        p = whole(p_own[k], PRESSURE + k)
        tend_u, tend_v = momentum(k, u, v, p, wind, east, north, f_u, f_v, up, down)
        sums = [a + b for a, b in zip(sums, (u, v, tend_u, tend_v))]
        us.append(u)
        vs.append(v)
        raws.append(raw)
        pair = u + at(u, -1, 1)
        last = p[8:] + (-0.25 * f_v[8:]) * pair[8:] + viscosity * at(v, -1, 0)[8:]
        if k == 0:
            last = last + wind[1][8:]
        first = (-0.25 * (f_v[:8] - 1.0 / NLAT)) * pair[:8] - p[:8] + viscosity * v[:8]
        edge_ref[k : k + 1] = u[15:16]
        edge_ref[8 + k : 9 + k] = raw[15:16]
        edge_ref[16 + k : 17 + k] = last[7:8]
        edge_ref[24 + k : 25 + k] = u[0:1]
        edge_ref[32 + k : 33 + k] = first[0:1]
    surface = whole(surface_ref[...], SURFACE)
    blocks = [surface, *sums, bottom, edge_ref[0:16], edge_ref[16:32]]
    for n, block in enumerate(blocks):
        spot = pl.multiple_of(lax.rem(n + place, 8) * ROWS, ROWS)
        stack_ref[pl.ds(spot, ROWS)] = block
    turned_ref[HALO : HALO + COLS] = stack_ref[:, :COLS].T
    beyond = stack_ref[:, COLS:].T
    turned_ref[:HALO] = beyond[COLS - HALO :]
    turned_ref[HALO + COLS :] = beyond[:HALO]
    edge = edge_ref[32:40]
    for d in range(MEMBERS):
        out_ref[d, :SLAB] = turned_ref[8 * d : 8 * d + SLAB]
        out_ref[d, EDGE:CHUNK] = at(edge, 8 * d - HALO, 1)[:, :COLS]

    sub = ids((8, COLS), 0)

    def spare(n):
        t, k = divmod(n, LEVELS)
        if t == 0:
            return us[k][:, :COLS], us[k][:, :COLS]
        if t == 1:
            return raws[k][:, :COLS], vs[k][:, :COLS]
        if t == 2:
            return raws[k][:, COLS:], us[k][:, COLS:]
        if k < 2:
            own = bottom[:, COLS * k : COLS * (k + 1)]
            return own, own
        return None

    def tops(n):
        own = c[n // LEVELS][n % LEVELS][8:]
        more = spare(n)
        return own if more is None else jnp.where(sub == 4, at(more[0][8:], 3, 0), own)

    def bottoms(n):
        own = c[n // LEVELS][n % LEVELS][:8]
        more = spare(n)
        return own if more is None else jnp.where(sub == 3, at(more[1][:8], -3, 0), own)

    for m in range(MEMBERS):
        out_ref[m, MAIL_N:MAIL_S] = jnp.where(sub >= 4, tops(2 * m), at(tops(2 * m + 1), 4, 0))
        out_ref[m, MAIL_S:EDGE] = jnp.where(sub < 4, bottoms(2 * m), at(bottoms(2 * m + 1), 4, 0))


def slab_kernel(in_ref, out_ref, edge_ref):
    shape = (SLAB, 2 * COLS)
    block = ids((SLAB, COLS), 1) // ROWS

    def plane(n):
        halves = []
        for h in range(2):
            half = in_ref[8 * h, :SLAB]
            for a in range(1, 8):
                half = jnp.where(block == (n + a) % 8, in_ref[8 * h + a, :SLAB], half)
            halves.append(at(half, 16 * n, 1))
        return jnp.concatenate(halves, axis=1)

    surface, start_u, start_v, force_u, force_v, bottom, first, second = map(plane, range(8))
    zeros = jnp.zeros((8, COLS), f32)
    for a in range(MEMBERS):
        edge_ref[ROWS * a : ROWS * a + 8] = in_ref[a + 1, EDGE:CHUNK] if a < MEMBERS - 1 else zeros
        edge_ref[ROWS * a + 8 : ROWS * a + 16] = zeros
    third = jnp.concatenate([edge_ref[:COLS].T[:SLAB], edge_ref[COLS:].T[:SLAB]], axis=1)

    lane = ids(shape, 1)
    r = lane % ROWS
    count_u = jnp.minimum(bottom, at(bottom, 1, 0))
    count_v = jnp.where(lane == NLAT - 1, 0.0, jnp.minimum(bottom, at(bottom, 1, 1)))

    def levels_of(values, row):
        one = at(jnp.where(r == row % ROWS, values, 0.0), row - 7, 1)
        for step in (1, 2, 4):
            one = one + at(one, step, 1)
        return one

    def summed(values, row):
        one = jnp.where(r < 8, values, 0.0)
        for step in (1, 2, 4):
            one = one + at(one, -step, 1)
        one = at(one, 7 - row, 1)
        return jnp.where(r == row % ROWS, one, 0.0)

    level = r.astype(f32)
    count_ua = levels_of(count_u, 15)
    count_ub = levels_of(count_u, 16)
    count_va = levels_of(count_v, 15)
    count_vb = levels_of(count_v, 16)
    count_vc = levels_of(count_v, 14)
    top = lane >= NLAT - ROWS
    v_a = jnp.where(count_va > level, at(first, 8, 1), 0.0)
    u_a = jnp.where(top, 0.0, first)
    u_b = jnp.where(top, 0.0, at(second, 24, 1))
    f_a = 0.25 * coriolis(lane - r + 15, 0.5)
    f_b = f_a + 0.25 * coriolis_base / NLAT
    pair = v_a + at(v_a, 1, 0)
    force_u = (
        force_u
        + summed(jnp.where(count_ua > level, f_a * pair + viscosity * u_b, 0.0), 15)
        + summed(jnp.where(count_ub > level, f_b * pair + viscosity * u_a, 0.0), 16)
    )
    spread = viscosity * (at(v_a, 1, 0) + at(v_a, -1, 0) - 4.0 * v_a)
    force_v = (
        force_v
        + summed(jnp.where(count_vc > level, viscosity * v_a, 0.0), 14)
        + summed(jnp.where(count_va > level, second + third + spread, 0.0), 15)
        + summed(jnp.where(count_vb > level, viscosity * v_a, 0.0), 16)
    )
    start_v = start_v + summed(v_a, 15)

    sub_step = time_step / SUBSTEPS
    per_u = 1.0 / jnp.maximum(count_u, 1.0)
    per_v = 1.0 / jnp.maximum(count_v, 1.0)
    open_u = jnp.where(count_u > 0.0, sub_step, 0.0)
    open_v = jnp.where(count_v > 0.0, sub_step, 0.0)
    flux_u = (sub_step * surface_scale * thickness) * count_u
    flux_v = (sub_step * surface_scale * thickness) * count_v
    held = (
        flux_u,
        at(flux_u, -1, 0),
        flux_v,
        at(flux_v, -1, 1),
        (0.25 * open_u) * coriolis(lane, 0.5),
        gravity * open_u,
        open_u * (force_u * per_u),
        (-0.25 * open_v) * coriolis(lane, 1.0),
        gravity * open_v,
        open_v * (force_v * per_v),
    )
    state = (surface, start_u * per_u, start_v * per_v)
    total_u = total_v = jnp.zeros((8, 2 * COLS), f32)
    low = 0
    for low, steps in ((0, 6), (8, 8), (16, 8), (24, 8)):
        high = SLAB - low
        cut = 8 if low else 0
        state = tuple(x[cut : x.shape[0] - cut] for x in state)
        du, du_w, dv, dv_s, cu, gu, fu, cv, gv, fv = (x[low:high] for x in held)
        centre = HALO - low

        def advance(_, carry):
            height, u, v, sum_u, sum_v = carry
            u_w = at(u, -1, 0)
            v_s = at(v, -1, 1)
            height = height - ((du * u - du_w * u_w) + (dv * v - dv_s * v_s))
            pair_v = v + v_s
            pair_u = u + u_w
            u_new = u + (cu * (pair_v + at(pair_v, 1, 0)) - gu * (at(height, 1, 0) - height) + fu)
            v_new = v + (cv * (pair_u + at(pair_u, 1, 1)) - gv * (at(height, 1, 1) - height) + fv)
            sum_u = sum_u + u_new[centre : centre + 8]
            sum_v = sum_v + v_new[centre : centre + 8]
            return height, u_new, v_new, sum_u, sum_v

        *state, total_u, total_v = lax.fori_loop(0, steps, advance, (*state, total_u, total_v))
    height = state[0][8:16]
    average_u = total_u * (1.0 / SUBSTEPS)
    average_v = total_v * (1.0 / SUBSTEPS)
    stream = (-thickness * count_u[HALO : HALO + 8]) * average_u
    lane_own = ids((8, 2 * COLS), 1)
    step = 1
    while step < NLAT:
        stream = stream + jnp.where(lane_own >= step, at(stream, -step, 1), 0.0)
        step *= 2
    block_own = ids((8, COLS), 1) // ROWS
    results = (height, stream, average_u, average_v)
    for e in range(MEMBERS):
        half = COLS * (e // 8)
        packed = zeros
        for n, values in enumerate(results):
            moved = at(values[:, half : half + COLS], -ROWS * n, 1)
            packed = jnp.where(block_own == (e + n) % 8, moved, packed)
        out_ref[e, 0:8] = packed
        out_ref[e, 8:16] = in_ref[(e + 15) % MEMBERS, MAIL_N:MAIL_S]
        out_ref[e, 16:24] = in_ref[(e + 1) % MEMBERS, MAIL_S:EDGE]


def finish_kernel(
    place_ref, in_ref, tracers_ref, velocity_ref, wind_ref, bottom_ref, west_ref, east_ref,
    tracers_out, velocity_out, height_out, stream_out, turned_ref,
):
    place = place_ref[0]
    turned_ref[...] = in_ref[:, 0:8].reshape(COLS, COLS).T

    def result(n):
        spot = pl.multiple_of(lax.rem(n + place, 8) * ROWS, ROWS)
        return turned_ref[pl.ds(spot, ROWS)]

    height_out[...] = result(0)
    stream_out[...] = result(1)
    average_u, average_v = result(2), result(3)

    sub = ids((8, COLS), 0)
    tall = (ROWS + 8, 2 * COLS)
    row = ids(tall, 0)
    first, last = place == 0, place == MEMBERS - 1

    def lat_tile(n):
        south = jnp.where(first, 0.0, in_ref[n // 2, 8:16])
        north = jnp.where(last, 0.0, in_ref[n // 2, 16:24])
        if n % 2 == 0:
            return jnp.where(sub < 4, north, south)
        return at(jnp.where(sub < 4, south, north), 4, 0)

    def spare_north(tile):
        return jnp.where(sub == 0, at(tile, 3, 0), 0.0)

    def spare_south(tile):
        return jnp.where(sub == 7, at(tile, -3, 0), 0.0)

    def tallen(own, tile):
        return jnp.concatenate([own, tile], axis=0)

    def whole(own, plane):
        return wide(own, beside_plane(west_ref, east_ref, plane))

    tiles = [[lat_tile(LEVELS * t + k) for k in range(LEVELS)] for t in range(TRACERS)]
    bottom_own = bottom_ref[...]
    c = tracer_planes(tracers_ref, bottom_own)
    p_own = pressures(c[1], c[0])
    p_tile = pressures(tiles[1], tiles[0])
    both = wide(
        spare_north(tiles[3][0]) + spare_south(tiles[3][0]),
        spare_north(tiles[3][1]) + spare_south(tiles[3][1]),
    )
    bottom = tallen(whole(bottom_own.astype(f32), BOTTOM), both)
    count_u = jnp.minimum(bottom, at(bottom, 1, 1))
    count_v = jnp.minimum(bottom, at(bottom, 1, 0))
    f_u = coriolis(place * ROWS + row, 0.5)
    f_v = coriolis(place * ROWS + row, 1.0)
    none = jnp.zeros((8, COLS), f32)
    wind = [tallen(wide(wind_ref[d], jnp.zeros((ROWS, COLS), f32)), jnp.zeros((8, 2 * COLS), f32)) for d in range(2)]

    def up(x):
        return at(x, 1, 0)

    def down(x):
        return at(x, -1, 0)

    stars_u, stars_v = [], []
    own_u, own_v = count_u[:ROWS, :COLS], count_v[:ROWS, :COLS]
    mean_u = mean_v = jnp.zeros((ROWS, COLS), f32)
    for k in range(LEVELS):
        east, north = count_u > k, count_v > k
        t0, t1, t2 = tiles[0][k], tiles[1][k], tiles[2][k]
        u_lat = wide(spare_north(t0) + spare_south(t0), spare_north(t2))
        v_lat = wide(spare_north(t1) + spare_south(t1), spare_south(t2))
        u = tallen(whole(velocity_ref[0, k], EAST + k), u_lat)
        u = jnp.where(east | (row >= ROWS), u, 0.0)
        v = tallen(whole(velocity_ref[1, k], NORTH + k), v_lat)
        v = jnp.where(north | (row == ROWS), v, 0.0)
        p = tallen(whole(p_own[k], PRESSURE + k), wide(p_tile[k], none))
        tend_u, tend_v = momentum(k, u, v, p, wind, east, north, f_u, f_v, up, down)
        star_u = (u + time_step * tend_u)[:ROWS, :COLS]
        star_v = (v + time_step * tend_v)[:ROWS, :COLS]
        stars_u.append(star_u)
        stars_v.append(star_v)
        mean_u = mean_u + star_u
        mean_v = mean_v + star_v

        u_own, v_own = u[:ROWS], v[:, :COLS]
        diff_e = jnp.where(east[:ROWS], tracer_diffusion, 0.0)
        diff_n = jnp.where(north[:, :COLS], tracer_diffusion, 0.0)
        for t in range(TRACERS):
            ce = wide(c[t][k], beside_tracer(west_ref, east_ref, LEVELS * t + k))
            cn = tallen(c[t][k], tiles[t][k])
            change = None
            for values, axis, flow, diffusion in ((ce, 1, u_own, diff_e), (cn, 0, v_own, diff_n)):
                ahead = at(values, 1, axis)
                face = (
                    37.0 * (values + ahead)
                    - 8.0 * (at(values, -1, axis) + at(values, 2, axis))
                    + (at(values, -2, axis) + at(values, 3, axis))
                ) * (1.0 / 60.0)
                flux = diffusion * (ahead - values) - flow * face
                gain = (flux - at(flux, -1, axis))[:ROWS, :COLS]
                change = gain if change is None else change + gain
            tracers_out[t, k] = jnp.where(bottom_own > k, c[t][k] + time_step * change, 0.0)
    shift_u = average_u - mean_u / jnp.maximum(own_u, 1.0)
    shift_v = average_v - mean_v / jnp.maximum(own_v, 1.0)
    for k in range(LEVELS):
        velocity_out[0, k] = jnp.where(own_u > k, stars_u[k] + shift_u, 0.0)
        velocity_out[1, k] = jnp.where(own_v > k, stars_v[k] + shift_v, 0.0)


def ring(axis, step):
    count = lax.axis_size(axis)
    return [(i, (i + step) % count) for i in range(count)]


def struct(*shape):
    return jax.ShapeDtypeStruct(shape, f32)


def vmem(*shape):
    return pltpu.VMEM(shape, f32)


def specs(count, scalars=0):
    return [pl.BlockSpec(memory_space=pltpu.SMEM)] * scalars + [
        pl.BlockSpec(memory_space=pltpu.VMEM)
    ] * count


PARAMS = pltpu.CompilerParams(vmem_limit_bytes=32 * 1024 * 1024)


def shards(tracers, velocity, surface, wind, bottom):
    place = lax.axis_index("lat").astype(jnp.int32).reshape(1)
    payload = struct(PLANES // 4 + 1, ROWS, COLS)
    to_right, to_left = pl.pallas_call(
        pack_kernel,
        out_shape=(payload, payload),
        in_specs=specs(5),
        out_specs=tuple(specs(2)),
        compiler_params=PARAMS,
        name="pack",
    )(tracers, velocity, surface, wind, bottom)
    west = lax.ppermute(to_right, "lon", ring("lon", 1))
    east = lax.ppermute(to_left, "lon", ring("lon", -1))
    chunks = pl.pallas_call(
        send_kernel,
        out_shape=struct(MEMBERS, CHUNK, COLS),
        in_specs=specs(7, 1),
        out_specs=specs(1)[0],
        scratch_shapes=[vmem(8 * ROWS, 2 * COLS), vmem(40, 2 * COLS), vmem(COLS + 2 * HALO, COLS)],
        compiler_params=PARAMS,
        name="columns",
    )(place, tracers, velocity, surface, wind, bottom, west, east)
    slabs = lax.all_to_all(chunks, "lat", 0, 0, tiled=True)
    answers = pl.pallas_call(
        slab_kernel,
        out_shape=struct(MEMBERS, BACK, COLS),
        in_specs=specs(1),
        out_specs=specs(1)[0],
        scratch_shapes=[vmem(2 * COLS, COLS)],
        compiler_params=PARAMS,
        name="substeps",
    )(slabs)
    home = lax.all_to_all(answers, "lat", 0, 0, tiled=True)
    return pl.pallas_call(
        finish_kernel,
        out_shape=(
            struct(TRACERS, LEVELS, ROWS, COLS),
            struct(2, LEVELS, ROWS, COLS),
            struct(ROWS, COLS),
            struct(ROWS, COLS),
        ),
        in_specs=specs(7, 1),
        out_specs=tuple(specs(4)),
        scratch_shapes=[vmem(COLS, COLS)],
        compiler_params=PARAMS,
        name="finish",
    )(place, home, tracers, velocity, wind, bottom, west, east)


def solution(mesh):
    placed = (
        P(None, None, "lat", "lon"),
        P(None, None, "lat", "lon"),
        P("lat", "lon"),
        P(None, "lat", "lon"),
        P("lat", "lon"),
    )
    return jax.shard_map(
        shards,
        mesh=mesh,
        in_specs=placed,
        out_specs=(
            P(None, None, "lat", "lon"),
            P(None, None, "lat", "lon"),
            P("lat", "lon"),
            P("lat", "lon"),
        ),
        check_vma=False,
    )
```

time: 186 us -> 67.3 us (0.36)
  starting transfers between devices: 103 us -> 16.5 us
  waiting for transfers between devices: 38.4 us -> 1.3 us
  Pallas kernels: 0 us -> 15.9 us
  other arithmetic: 14.7 us -> 0 us
  blocking collectives: 21 us -> 28.5 us
  loops' own time: 2.01 us -> 0 us
    ppermute x24 -> x2, starting transfers between devices: 103 us -> 16.5 us  [the longest x1 10.9 us: shards(): east = lax.ppermute(to_left, 'lon', ring('lon', -1))]
    ppermute x24 -> x2, waiting for transfers between devices: 38.4 us -> 1.3 us  [the longest x1 1.3 us: shards(): east = lax.ppermute(to_left, 'lon', ring('lon', -1))]
    all_to_all x0 -> x2, blocking collectives: none -> 28.5 us  [the longest x1 18.5 us: shards(): slabs = lax.all_to_all(chunks, 'lat', 0, 0, tiled=True)]
    all_gather x1 -> x0, blocking collectives: 21 us -> none  [prefix(): gathered = lax.all_gather(part, axis)]
    pallas_call x0 -> x4, Pallas kernels: none -> 15.9 us  [the longest x1 9.02 us: shards(): pl.pallas_call(slab_kernel, out_shape=struct(MEMBERS, BACK, COLS), in_spe...]
    add x31 -> x0, other arithmetic: 4.38 us -> none  [the longest x30 4.36 us: advance(): north_sum + north_now]
    sub x32 -> x0, other arithmetic: 3.98 us -> none  [the longest x30 2.55 us: substep(): height - sub_step * surface_scale * (flux_u - neighbour(flux_u, 0, -1) +...]
    mul x97 -> x0, other arithmetic: 2.9 us -> none  [the longest x1 0.93 us: baroclinic(): (tracer_win(0, row_count, 0, col_count) + time_step * tendency) * wet_inner]
  transfers between devices with their start and end apart: 24 -> 2, of which waited for: 12 -> 1; matrix products, arithmetic and copies ran while one was open for 2% -> 0% of each run, Pallas kernels for 0% -> 0%
where the time goes in v1:
time: 67.3 us; the launch traced here: 66.9 us
  blocking collectives  28.5 us (42%)
  starting transfers between devices  16.5 us (25%)
  Pallas kernels  15.9 us (24%)
  local copies, waits for them, and re-layouts  3.98 us (6%)
  waiting for transfers between devices  1.3 us (2%)
  between operations  0.72 us (1%)
    all_to_all x1, blocking collectives, shards(): slabs = lax.all_to_all(chunks, 'lat', 0, 0, tiled=True)  18.5 us
    ppermute x1, starting transfers between devices, shards(): east = lax.ppermute(to_left, 'lon', ring('lon', -1))  10.9 us
    all_to_all x1, blocking collectives, shards(): home = lax.all_to_all(answers, 'lat', 0, 0, tiled=True)  9.94 us
    pallas_call x1, Pallas kernels, shards(): pl.pallas_call(slab_kernel, out_shape=struct(MEMBERS, BACK, COLS), in_spe...  9.02 us
    pallas_call x1, Pallas kernels, shards(): pl.pallas_call(finish_kernel, out_shape=(struct(TRACERS, LEVELS, ROWS, CO...  5.93 us
    ppermute x1, starting transfers between devices, shards(): west = lax.ppermute(to_right, 'lon', ring('lon', 1))  5.65 us
    unnamed x20, local copies, waits for them, and re-layouts  3.98 us
  transfers between devices with their start and end apart: 2, of which 1 were waited for; matrix products, arithmetic and copies ran while one was open for 0% of the time, Pallas kernels for 0%

profile of v1, /device:TPU:1, one launch (start us, length us, event | category | flops | bytes accessed | tf_op | source)
XLA Modules:
  0.0 66.9 jit_solution(707631527262956217)
XLA Ops:
  0.6 0.0 copy-start
  0.6 0.9 %copy-done = f32[4,8,16,128]{3,2,1,0:T(8,128)S(1)} copy-done((f32[4,8,16,128]{3,2,1,0:T(8,128)S(1)}, f32[4,8,16,128]{3,2,1,0:T(8,128)}, u32[]{:S(2)}) %copy-start) | copy-done | bytes 262168
  1.6 0.0 copy-start.2
  1.6 0.9 %copy-done.2 = f32[2,8,16,128]{3,2,1,0:T(8,128)S(1)} copy-done((f32[2,8,16,128]{3,2,1,0:T(8,128)S(1)}, f32[2,8,16,128]{3,2,1,0:T(8,128)}, u32[]{:S(2)}) %copy-start.2) | copy-done | bytes 131096
  2.5 0.0 copy-start.4
  2.5 0.7 %copy-done.4 = f32[2,16,128]{2,1,0:T(8,128)S(1)} copy-done((f32[2,16,128]{2,1,0:T(8,128)S(1)}, f32[2,16,128]{2,1,0:T(8,128)}, u32[]{:S(2)}) %copy-start.4) | copy-done | bytes 16408
  3.2 0.0 copy-start.6
  3.2 0.7 %copy-done.6 = s32[16,128]{1,0:T(8,128)S(1)} copy-done((s32[16,128]{1,0:T(8,128)S(1)}, s32[16,128]{1,0:T(8,128)}, u32[]{:S(2)}) %copy-start.6) | copy-done | bytes 8216
  3.9 0.0 copy-start.8
  3.9 0.7 %copy-done.8 = f32[16,128]{1,0:T(8,128)S(1)} copy-done((f32[16,128]{1,0:T(8,128)S(1)}, f32[16,128]{1,0:T(8,128)}, u32[]{:S(2)}) %copy-start.8) | copy-done | bytes 8216
  4.6 0.0 copy-start.1
  4.6 0.0 copy-start.3
  4.6 0.0 copy-start.5
  4.6 0.0 copy-start.9
  4.6 0.2 pack.1
  4.8 0.0 copy-start.7
  4.8 5.7 %collective-permute-start = (f32[8,16,128]{2,1,0:T(8,128)S(1)}, f32[8,16,128]{2,1,0:T(8,128)S(1)}, u32[]{:S(2)}, u32[]{:S(2)}) collective-permute-start(f32[8,16,128]{2,1,0:T(8,128)S(1)} %get-tuple-element.6), channel_id=1, source_target_pairs={{0,1},{1,2},{2,3},{3,4},{4,5},{5,6},{6,7},{7,8},{8,9},{9,10},{10,1... | collective-permute-start | bytes 196616 | tf_op jit(solution)/shard_map/ppermute | solution.py:495
  10.5 10.9 %collective-permute-start.1 = (f32[8,16,128]{2,1,0:T(8,128)S(1)}, f32[8,16,128]{2,1,0:T(8,128)S(1)}, u32[]{:S(2)}, u32[]{:S(2)}) collective-permute-start(f32[8,16,128]{2,1,0:T(8,128)S(1)} %get-tuple-element.7), channel_id=1, source_target_pairs={{0,31},{1,0},{2,1},{3,2},{4,3},{5,4},{6,5},{7,6},{8,7},{9,8},{10,9... | collective-permute-start | bytes 196616 | tf_op jit(solution)/shard_map/ppermute | solution.py:496
  21.3 0.0 collective-permute-done.west_ref
  21.3 1.3 %collective-permute-done.1.east_ref = f32[8,16,128]{2,1,0:T(8,128)S(1)} collective-permute-done((f32[8,16,128]{2,1,0:T(8,128)S(1)}, f32[8,16,128]{2,1,0:T(8,128)S(1)}, u32[]{:S(2)}, u32[]{:S(2)}) %collective-permute-start.1) | collective-permute-done | bytes 65568 | tf_op jit(solution)/shard_map/ppermute | solution.py:496
  22.6 0.0 copy-done.1
  22.6 0.0 copy-done.3
  22.6 0.0 copy-done.5
  22.7 0.0 copy-done.9
  22.7 0.0 copy-done.7
  22.7 0.8 %columns.1 = f32[16,96,128]{2,1,0:T(8,128)S(1)} custom-call(s32[1]{0:T(128)} %bitcast.place_ref, f32[4,8,16,128]{3,2,1,0:T(8,128)S(1)} %copy-done.1, f32[2,8,16,128]{3,2,1,0:T(8,128)S(1)} %copy-done.3, f32[16,128]{1,0:T(8,128)S(1)} %copy-done.9, f32[2,16,128]{2,1,0:T(8,128)S(1)} %copy-done.5, s32[16,128]{1,0:T(8,128)S(1)} %copy-done.7, ...), custom_call_target="tpu_custom_call" | custom-call | tf_op jit(solution)/shard_map/columns/pallas_call | solution.py:497
  23.4 18.5 %all_to_all.10.in_ref = f32[16,96,128]{2,1,0:T(8,128)S(1)} all-to-all(f32[16,96,128]{2,1,0:T(8,128)S(1)} %columns.1), channel_id=1, replica_groups=mesh['lat'=16,'lon'=32] {'lat'}, dimensions={0} | all-to-all | bytes 1572864 | tf_op jit(solution)/shard_map/all_to_all | solution.py:506
  42.0 9.0 %substeps.1 = f32[16,24,128]{2,1,0:T(8,128)S(1)} custom-call(f32[16,96,128]{2,1,0:T(8,128)S(1)} %all_to_all.10.in_ref), custom_call_target="tpu_custom_call" | custom-call | tf_op jit(solution)/shard_map/substeps/pallas_call | solution.py:507
  51.0 9.9 %all_to_all.11.in_ref = f32[16,24,128]{2,1,0:T(8,128)S(1)} all-to-all(f32[16,24,128]{2,1,0:T(8,128)S(1)} %substeps.1), channel_id=1, replica_groups=mesh['lat'=16,'lon'=32] {'lat'}, dimensions={0} | all-to-all | bytes 393216 | tf_op jit(solution)/shard_map/all_to_all | solution.py:516
  60.9 5.9 %finish.1 = (f32[4,8,16,128]{3,2,1,0:T(8,128)}, f32[2,8,16,128]{3,2,1,0:T(8,128)}, f32[16,128]{1,0:T(8,128)}, f32[16,128]{1,0:T(8,128)}) custom-call(s32[1]{0:T(128)} %bitcast.place_ref, f32[16,24,128]{2,1,0:T(8,128)S(1)} %all_to_all.11.in_ref, f32[4,8,16,128]{3,2,1,0:T(8,128)S(1)} %copy-done.1, f32[2,8,16,128]{3,2,1,0:T(8,128)S(1)} %copy-done.3, ...), custom_call_target="tpu_custom_call" | custom-call | tf_op jit(solution)/shard_map/finish/pallas_call | solution.py:517
Async XLA Ops:
  0.6 1.0 %copy-start = (f32[4,8,16,128]{3,2,1,0:T(8,128)S(1)}, f32[4,8,16,128]{3,2,1,0:T(8,128)}, u32[]{:S(2)}) copy-start(f32[4,8,16,128]{3,2,1,0:T(8,128)} %tracers_ref.5) | copy-start | bytes 786436
  1.6 0.9 %copy-start.2 = (f32[2,8,16,128]{3,2,1,0:T(8,128)S(1)}, f32[2,8,16,128]{3,2,1,0:T(8,128)}, u32[]{:S(2)}) copy-start(f32[2,8,16,128]{3,2,1,0:T(8,128)} %velocity_ref.5) | copy-start | bytes 393220
  2.5 0.7 %copy-start.4 = (f32[2,16,128]{2,1,0:T(8,128)S(1)}, f32[2,16,128]{2,1,0:T(8,128)}, u32[]{:S(2)}) copy-start(f32[2,16,128]{2,1,0:T(8,128)} %wind_ref.5) | copy-start | bytes 49156
  3.2 0.7 %copy-start.6 = (s32[16,128]{1,0:T(8,128)S(1)}, s32[16,128]{1,0:T(8,128)}, u32[]{:S(2)}) copy-start(s32[16,128]{1,0:T(8,128)} %bottom_ref.5) | copy-start | bytes 24580
  3.9 0.7 %copy-start.8 = (f32[16,128]{1,0:T(8,128)S(1)}, f32[16,128]{1,0:T(8,128)}, u32[]{:S(2)}) copy-start(f32[16,128]{1,0:T(8,128)} %surface_ref.3) | copy-start | bytes 24580
  4.6 18.0 %copy-start.1 = (f32[4,8,16,128]{3,2,1,0:T(8,128)S(1)}, f32[4,8,16,128]{3,2,1,0:T(8,128)}, u32[]{:S(2)}) copy-start(f32[4,8,16,128]{3,2,1,0:T(8,128)} %tracers_ref.5) | copy-start | bytes 786436
  4.6 18.0 %copy-start.3 = (f32[2,8,16,128]{3,2,1,0:T(8,128)S(1)}, f32[2,8,16,128]{3,2,1,0:T(8,128)}, u32[]{:S(2)}) copy-start(f32[2,8,16,128]{3,2,1,0:T(8,128)} %velocity_ref.5) | copy-start | bytes 393220
  4.6 18.0 %copy-start.5 = (f32[2,16,128]{2,1,0:T(8,128)S(1)}, f32[2,16,128]{2,1,0:T(8,128)}, u32[]{:S(2)}) copy-start(f32[2,16,128]{2,1,0:T(8,128)} %wind_ref.5) | copy-start | bytes 49156
  4.6 18.0 %copy-start.9 = (f32[16,128]{1,0:T(8,128)S(1)}, f32[16,128]{1,0:T(8,128)}, u32[]{:S(2)}) copy-start(f32[16,128]{1,0:T(8,128)} %surface_ref.3) | copy-start | bytes 24580
  4.8 17.9 %copy-start.7 = (s32[16,128]{1,0:T(8,128)S(1)}, s32[16,128]{1,0:T(8,128)}, u32[]{:S(2)}) copy-start(s32[16,128]{1,0:T(8,128)} %bottom_ref.5) | copy-start | bytes 24580
  4.8 16.5 %collective-permute-start = (f32[8,16,128]{2,1,0:T(8,128)S(1)}, f32[8,16,128]{2,1,0:T(8,128)S(1)}, u32[]{:S(2)}, u32[]{:S(2)}) collective-permute-start(f32[8,16,128]{2,1,0:T(8,128)S(1)} %get-tuple-element.6), channel_id=1, source_target_pairs={{0,1},{1,2},{2,3},{3,4},{4,5},{5,6},{6,7},{7,8},{8,9},{9,10},{10,1... | collective-permute-start | bytes 196616 | tf_op jit(solution)/shard_map/ppermute | solution.py:495
  10.5 12.2 %collective-permute-start.1 = (f32[8,16,128]{2,1,0:T(8,128)S(1)}, f32[8,16,128]{2,1,0:T(8,128)S(1)}, u32[]{:S(2)}, u32[]{:S(2)}) collective-permute-start(f32[8,16,128]{2,1,0:T(8,128)S(1)} %get-tuple-element.7), channel_id=1, source_target_pairs={{0,31},{1,0},{2,1},{3,2},{4,3},{5,4},{6,5},{7,6},{8,7},{9,8},{10,9... | collective-permute-start | bytes 196616 | tf_op jit(solution)/shard_map/ppermute | solution.py:496

commit v2 on v1

v2 whole, which is shorter than its diff:
```python
import jax
import jax.numpy as jnp
from jax import lax
from jax.experimental import pallas as pl
from jax.experimental.pallas import tpu as pltpu
from jax.sharding import PartitionSpec as P

TRACERS = 4
LEVELS = 8
SUBSTEPS = 30
ROWS = 16
COLS = 128
MEMBERS = 16
HALO = 32
SLAB = 72
NLAT = ROWS * MEMBERS

time_step = 0.2
tracer_diffusion = 0.2
viscosity = 0.2
thermal_expansion = 2.0
haline_contraction = 1.5
coriolis_base = 1.0
gravity = 140.0
surface_scale = 40.0
thickness = 1.0 / LEVELS
f32 = jnp.float32

PRESSURE, EAST, NORTH, WIND, SURFACE, BOTTOM = 0, 8, 16, 24, 26, 27
PLANES = 28
OWN_EAST, OWN_NORTH, OWN_SURFACE, OWN_WIND, OWN_BOTTOM, OWN = 32, 40, 48, 49, 51, 52
MAIL_N, MAIL_S, EDGE, CHUNK = SLAB, SLAB + 8, SLAB + 16, SLAB + 24
BACK = 24


def at(values, step, axis):
    size = values.shape[axis]
    step %= size
    return values if step == 0 else pltpu.roll(values, size - step, axis)


def ids(shape, axis):
    return lax.broadcasted_iota(jnp.int32, shape, axis)


def wide(own, beside):
    return jnp.concatenate([own, beside], axis=1)


def tracer_planes(own_ref):
    bottom = own_ref[OWN_BOTTOM]
    return [
        [jnp.where(bottom > k, own_ref[LEVELS * t + k], 0.0) for k in range(LEVELS)]
        for t in range(TRACERS)
    ]


def pressures(salt, heat):
    total, out = None, []
    for k in range(LEVELS):
        density = haline_contraction * salt[k] - thermal_expansion * heat[k]
        total = density if total is None else total + density
        out.append(thickness * total)
    return out


def pack_kernel(own_ref, right_ref, left_ref):
    c = tracer_planes(own_ref)
    planes = pressures(c[1], c[0])
    planes += [own_ref[n] for n in range(OWN_EAST, OWN_SURFACE)]
    planes += [own_ref[n] for n in (OWN_WIND, OWN_WIND + 1, OWN_SURFACE, OWN_BOTTOM)]
    lane = ids((ROWS, COLS), 1)
    for q in range(PLANES // 4):
        right = left = jnp.zeros((ROWS, COLS), f32)
        for s in range(4):
            moved = at(planes[4 * q + s], -32 * s, 1)
            right = jnp.where(lane // 32 == (s + 3) % 4, moved, right)
            left = jnp.where(lane // 32 == s, moved, left)
        right_ref[q] = right
        left_ref[q] = left
    right = left = jnp.zeros((ROWS, COLS), f32)
    for n in range(TRACERS * LEVELS):
        moved = at(c[n // LEVELS][n % LEVELS], -4 * n, 1)
        right = jnp.where(lane // 4 == (n + 31) % 32, moved, right)
        left = jnp.where(lane // 4 == n, moved, left)
    right_ref[PLANES // 4] = right
    left_ref[PLANES // 4] = left


def beside_plane(west_ref, east_ref, plane):
    q, s = divmod(plane, 4)
    block = ids((ROWS, COLS), 1) // 32
    both = jnp.where(
        block == s, east_ref[q], jnp.where(block == (s + 3) % 4, west_ref[q], 0.0)
    )
    return at(both, 32 * s, 1)


def beside_tracer(west_ref, east_ref, n):
    block = ids((ROWS, COLS), 1) // 4
    last = PLANES // 4
    both = jnp.where(
        block == n, east_ref[last], jnp.where(block == (n + 31) % 32, west_ref[last], 0.0)
    )
    return at(both, 4 * n, 1)


def momentum(k, u, v, p, wind, east, north, f_u, f_v, up, down):
    pair_v = v + down(v)
    pair_u = u + at(u, -1, 1)
    tend_u = (
        (0.25 * f_u) * (pair_v + at(pair_v, 1, 1))
        - (at(p, 1, 1) - p)
        + viscosity * (at(u, 1, 1) + at(u, -1, 1) + up(u) + down(u) - 4.0 * u)
    )
    tend_v = (
        (-0.25 * f_v) * (pair_u + up(pair_u))
        - (up(p) - p)
        + viscosity * (at(v, 1, 1) + at(v, -1, 1) + up(v) + down(v) - 4.0 * v)
    )
    if k == 0:
        tend_u = tend_u + wind[0]
        tend_v = tend_v + wind[1]
    return jnp.where(east, tend_u, 0.0), jnp.where(north, tend_v, 0.0)


def coriolis(rows, offset):
    return coriolis_base * (0.5 + (rows.astype(f32) + offset) / NLAT)


def send_kernel(
    place_ref, own_ref, west_ref, east_ref,
    out_ref, split_ref, stack_ref, edge_ref, turned_ref,
):
    place = place_ref[0]
    c = tracer_planes(own_ref)
    p_own = pressures(c[1], c[0])

    def whole(own, plane):
        return wide(own, beside_plane(west_ref, east_ref, plane))

    shape = (ROWS, 2 * COLS)
    row = ids(shape, 0)
    bottom = whole(own_ref[OWN_BOTTOM], BOTTOM)
    wind = [whole(own_ref[OWN_WIND + d], WIND + d) for d in range(2)]

    def up(x):
        return jnp.where(row == ROWS - 1, 0.0, at(x, 1, 0))

    def down(x):
        return jnp.where(row == 0, 0.0, at(x, -1, 0))

    count_u = jnp.minimum(bottom, at(bottom, 1, 1))
    count_v = jnp.minimum(bottom, up(bottom))
    f_u = coriolis(place * ROWS + row, 0.5)
    f_v = coriolis(place * ROWS + row, 1.0)
    sums = [jnp.zeros(shape, f32) for _ in range(4)]
    us, vs, raws = [], [], []
    for k in range(LEVELS):
        east, north = count_u > k, count_v > k
        u = jnp.where(east, whole(own_ref[OWN_EAST + k], EAST + k), 0.0)
        raw = jnp.where(bottom > k, whole(own_ref[OWN_NORTH + k], NORTH + k), 0.0)
        v = jnp.where(north, raw, 0.0)
        p = whole(p_own[k], PRESSURE + k)
        tend_u, tend_v = momentum(k, u, v, p, wind, east, north, f_u, f_v, up, down)
        sums = [a + b for a, b in zip(sums, (u, v, tend_u, tend_v))]
        us.append(u)
        vs.append(v)
        raws.append(raw)
        pair = u + at(u, -1, 1)
        last = p[8:] + (-0.25 * f_v[8:]) * pair[8:] + viscosity * at(v, -1, 0)[8:]
        if k == 0:
            last = last + wind[1][8:]
        first = (-0.25 * (f_v[:8] - 1.0 / NLAT)) * pair[:8] - p[:8] + viscosity * v[:8]
        edge_ref[k : k + 1] = u[15:16]
        edge_ref[8 + k : 9 + k] = raw[15:16]
        edge_ref[16 + k : 17 + k] = last[7:8]
        edge_ref[24 + k : 25 + k] = u[0:1]
        edge_ref[32 + k : 33 + k] = first[0:1]
    surface = whole(own_ref[OWN_SURFACE], SURFACE)
    for n, values in enumerate((surface, *sums, bottom)):
        split_ref[ROWS * n : ROWS * (n + 1)] = values[:, :COLS]
        split_ref[ROWS * (6 + n) : ROWS * (7 + n)] = values[:, COLS:]
    for q in range(16):
        spot = pl.multiple_of(lax.rem(q + place, 16) * 8, 8)
        for half in range(2):
            if q < 12:
                rows = split_ref[pl.ds(ROWS * (6 * half + q // 2) + q % 2, 8, 2), :]
            else:
                rows = edge_ref[8 * (q - 12) : 8 * (q - 11), COLS * half : COLS * (half + 1)]
            stack_ref[half, pl.ds(spot, 8)] = rows
    turned_ref[HALO : HALO + COLS] = stack_ref[0].T
    beyond = stack_ref[1].T
    turned_ref[:HALO] = beyond[COLS - HALO :]
    turned_ref[HALO + COLS :] = beyond[:HALO]
    edge = edge_ref[32:40]
    for d in range(MEMBERS):
        out_ref[d, :SLAB] = turned_ref[8 * d : 8 * d + SLAB]
        out_ref[d, EDGE:CHUNK] = at(edge, 8 * d - HALO, 1)[:, :COLS]

    sub = ids((8, COLS), 0)

    def spare(n):
        t, k = divmod(n, LEVELS)
        if t == 0:
            return us[k][:, :COLS], us[k][:, :COLS]
        if t == 1:
            return raws[k][:, :COLS], vs[k][:, :COLS]
        if t == 2:
            return raws[k][:, COLS:], us[k][:, COLS:]
        if k < 2:
            own = bottom[:, COLS * k : COLS * (k + 1)]
            return own, own
        return None

    def tops(n):
        own = c[n // LEVELS][n % LEVELS][8:]
        more = spare(n)
        return own if more is None else jnp.where(sub == 4, at(more[0][8:], 3, 0), own)

    def bottoms(n):
        own = c[n // LEVELS][n % LEVELS][:8]
        more = spare(n)
        return own if more is None else jnp.where(sub == 3, at(more[1][:8], -3, 0), own)

    for m in range(MEMBERS):
        out_ref[m, MAIL_N:MAIL_S] = jnp.where(sub >= 4, tops(2 * m), at(tops(2 * m + 1), 4, 0))
        out_ref[m, MAIL_S:EDGE] = jnp.where(sub < 4, bottoms(2 * m), at(bottoms(2 * m + 1), 4, 0))


def slab_kernel(in_ref, out_ref, edge_ref):
    shape = (SLAB, COLS)
    lane = ids(shape, 1)
    r = lane % 8
    block = ids((8, COLS), 1) // 8

    tiles = []
    for t in range(SLAB // 8):
        now = [in_ref[a, 8 * t : 8 * t + 8] for a in range(MEMBERS)]
        for bit in (1, 2, 4, 8):
            odd = (block & bit) > 0
            now = [jnp.where(odd, now[(a + bit) % MEMBERS], now[a]) for a in range(MEMBERS)]
        tiles.append([at(now[-q % MEMBERS], 8 * q, 1) for q in range(16)])
    blocks = [jnp.concatenate([tile[q] for tile in tiles], axis=0) for q in range(16)]
    surface, start_u, start_v, force_u, force_v, bottom = (blocks[2 * n : 2 * n + 2] for n in range(6))
    u_a, v_raw, near, u_next = blocks[12:]
    zeros = jnp.zeros((8, COLS), f32)
    for a in range(MEMBERS):
        edge_ref[8 * a : 8 * a + 8] = in_ref[a + 1, EDGE:CHUNK] if a < MEMBERS - 1 else zeros
    far = edge_ref[...].T[:SLAB]

    top = lane == COLS - 1
    count_u = [jnp.minimum(b, at(b, 1, 0)) for b in bottom]
    count_v = [
        jnp.minimum(*bottom),
        jnp.where(top, 0.0, jnp.minimum(bottom[1], at(bottom[0], 1, 1))),
    ]

    ahead = jnp.concatenate([count_u[0], count_v[0]], axis=0)
    first = (ids(ahead.shape, 1) % 8 == 0) & (ids(ahead.shape, 1) > 0)
    counts = jnp.concatenate(
        [
            jnp.where(r == 7, count_u[1], 0.0),
            jnp.where(r == 7, count_v[1], 0.0),
            jnp.where(r == 7, count_v[0], 0.0),
            at(jnp.where(first, ahead, 0.0), 1, 1),
        ],
        axis=0,
    )
    for step in (1, 2, 4):
        counts = counts + at(counts, step, 1)
    count_ua, count_va, count_vc, count_ub, count_vb = (
        counts[SLAB * n : SLAB * (n + 1)] for n in range(5)
    )
    level = r.astype(f32)
    last = lane >= COLS - 8
    v_a = jnp.where(count_va > level, v_raw, 0.0)
    u_a = jnp.where(last, 0.0, u_a)
    u_b = jnp.where(last, 0.0, at(u_next, 8, 1))
    f_a = 0.25 * coriolis(lane // 8 * ROWS + 15, 0.5)
    f_b = f_a + 0.25 * coriolis_base / NLAT
    pair = v_a + at(v_a, 1, 0)
    spread = viscosity * (at(v_a, 1, 0) + at(v_a, -1, 0) - 4.0 * v_a)
    terms = jnp.concatenate(
        [
            jnp.where(count_ua > level, f_a * pair + viscosity * u_b, 0.0),
            jnp.where(count_ub > level, f_b * pair + viscosity * u_a, 0.0),
            jnp.where(count_vb > level, viscosity * v_a, 0.0),
            jnp.where(count_vc > level, viscosity * v_a, 0.0),
            jnp.where(count_va > level, near + far + spread, 0.0),
            v_a,
        ],
        axis=0,
    )
    for step in (1, 2, 4):
        terms = terms + at(terms, -step, 1)
    shifted = at(terms[SLAB : 3 * SLAB], -1, 1)
    u_15, v_14, v_15, begin_15 = (
        jnp.where(r == 7, terms[SLAB * n : SLAB * (n + 1)], 0.0) for n in (0, 3, 4, 5)
    )
    u_16, v_16 = (jnp.where(r == 0, shifted[SLAB * n : SLAB * (n + 1)], 0.0) for n in range(2))
    force_u = [force_u[0] + u_16, force_u[1] + u_15]
    force_v = [force_v[0] + (v_14 + v_16), force_v[1] + v_15]
    start_v = [start_v[0], start_v[1] + begin_15]

    sub_step = time_step / SUBSTEPS
    held_u, held_v, flux_u, flux_v, begin_u, begin_v = [], [], [], [], [], []
    for i in range(2):
        per = 1.0 / jnp.maximum(count_u[i], 1.0)
        open_face = jnp.where(count_u[i] > 0.0, sub_step, 0.0)
        flux_u.append((sub_step * surface_scale * thickness) * count_u[i])
        held_u.append(
            (
                (0.25 * open_face) * coriolis(2 * lane + i, 0.5),
                gravity * open_face,
                open_face * (force_u[i] * per),
            )
        )
        begin_u.append(start_u[i] * per)
        per = 1.0 / jnp.maximum(count_v[i], 1.0)
        open_face = jnp.where(count_v[i] > 0.0, sub_step, 0.0)
        flux_v.append((sub_step * surface_scale * thickness) * count_v[i])
        held_v.append(
            (
                (-0.25 * open_face) * coriolis(2 * lane + i, 1.0),
                gravity * open_face,
                open_face * (force_v[i] * per),
            )
        )
        begin_v.append(start_v[i] * per)
    held = (
        *flux_u, at(flux_u[0], 1, 1), *flux_v, at(flux_v[0], 1, 1), at(flux_v[1], -1, 1),
        *held_u[0], *held_u[1], *held_v[0], *held_v[1],
    )
    state = (*surface, at(surface[0], 1, 1), *begin_u, *begin_v)
    total = (zeros,) * 4
    for low, steps in ((0, 6), (8, 8), (16, 8), (24, 8)):
        cut = 8 if low else 0
        state = tuple(x[cut : x.shape[0] - cut] for x in state)
        (
            du0, du1, du2, dv0, dv1, dv2, dv_, cu0, gu0, fu0, cu1, gu1, fu1,
            cv0, gv0, fv0, cv1, gv1, fv1,
        ) = (x[low : SLAB - low] for x in held)
        centre = HALO - low

        def advance(_, carry):
            h0, h1, h2, u0, u1, v0, v1, *sums = carry
            v_ = at(v1, -1, 1)
            u2 = at(u0, 1, 1)
            v2 = at(v0, 1, 1)
            x0, x1, x2 = du0 * u0, du1 * u1, du2 * u2
            y0, y1 = dv0 * v0, dv1 * v1
            h1 = h1 - ((x1 - at(x1, -1, 0)) + (y1 - y0))
            h0 = h0 - ((x0 - at(x0, -1, 0)) + (y0 - dv_ * v_))
            h2 = h2 - ((x2 - at(x2, -1, 0)) + (dv2 * v2 - y1))
            p0, p1, p2 = u0 + at(u0, -1, 0), u1 + at(u1, -1, 0), u2 + at(u2, -1, 0)
            q0, q1 = v0 + v_, v1 + v0
            u0 = (u0 + fu0) + (cu0 * (q0 + at(q0, 1, 0)) - gu0 * (at(h0, 1, 0) - h0))
            u1 = (u1 + fu1) + (cu1 * (q1 + at(q1, 1, 0)) - gu1 * (at(h1, 1, 0) - h1))
            v0 = (v0 + fv0) + (cv0 * (p0 + p1) - gv0 * (h1 - h0))
            v1 = (v1 + fv1) + (cv1 * (p1 + p2) - gv1 * (h2 - h1))
            sums = [a + b[centre : centre + 8] for a, b in zip(sums, (u0, u1, v0, v1))]
            return (h0, h1, h2, u0, u1, v0, v1, *sums)

        *state, a0, a1, a2, a3 = lax.fori_loop(0, steps, advance, (*state, *total))
        total = (a0, a1, a2, a3)
    height = [x[8:16] for x in state[:2]]
    average = [x * (1.0 / SUBSTEPS) for x in total]
    transport = [
        (-thickness * count_u[i][HALO : HALO + 8]) * average[i] for i in range(2)
    ]
    square = (COLS, COLS)
    before = (ids(square, 0) < ids(square, 1)).astype(f32)
    south = jnp.dot(
        transport[0] + transport[1],
        before,
        precision=lax.Precision.HIGHEST,
        preferred_element_type=f32,
    )
    stream = [south + transport[0], south + (transport[0] + transport[1])]
    results = [*height, *stream, *average]
    moved = [at(values, -8 * n, 1) for n, values in enumerate(results)]
    for e in range(MEMBERS):
        packed = moved[0]
        for n in range(1, 8):
            packed = jnp.where(block == (e + n) % 16, moved[n], packed)
        out_ref[e, 0:8] = packed
        out_ref[e, 8:16] = in_ref[(e + 15) % MEMBERS, MAIL_N:MAIL_S]
        out_ref[e, 16:24] = in_ref[(e + 1) % MEMBERS, MAIL_S:EDGE]


def gain(values, axis, flow, diffusion):
    ahead = at(values, 1, axis)
    sides = at(values, -1, axis) + at(values, 2, axis)
    far = at(values, -2, axis) + at(values, 3, axis)
    face = (37.0 * (values + ahead) - 8.0 * sides + far) * (1.0 / 60.0)
    flux = diffusion * (ahead - values) - flow * face
    return flux - at(flux, -1, axis)


def finish_kernel(
    place_ref, in_ref, own_ref, west_ref, east_ref,
    tracers_out, velocity_out, height_out, stream_out, turned_ref, rows_ref,
):
    place = place_ref[0]
    turned_ref[...] = in_ref[:, 0:8].reshape(COLS, COLS).T

    for q in range(8):
        spot = pl.multiple_of(lax.rem(q + place, 16) * 8, 8)
        rows_ref[pl.ds(ROWS * (q // 2) + q % 2, 8, 2), :] = turned_ref[pl.ds(spot, 8)]
    height_out[...] = rows_ref[:ROWS]
    stream_out[...] = rows_ref[ROWS : 2 * ROWS]
    average_u, average_v = rows_ref[2 * ROWS : 3 * ROWS], rows_ref[3 * ROWS :]

    sub = ids((8, COLS), 0)
    tall = (ROWS + 8, 2 * COLS)
    row = ids(tall, 0)
    first, last = place == 0, place == MEMBERS - 1

    def lat_tile(n):
        south = jnp.where(first, 0.0, in_ref[n // 2, 8:16])
        north = jnp.where(last, 0.0, in_ref[n // 2, 16:24])
        if n % 2 == 0:
            return jnp.where(sub < 4, north, south)
        return at(jnp.where(sub < 4, south, north), 4, 0)

    def spare_north(tile):
        return jnp.where(sub == 0, at(tile, 3, 0), 0.0)

    def spare_south(tile):
        return jnp.where(sub == 7, at(tile, -3, 0), 0.0)

    def tallen(own, tile):
        return jnp.concatenate([own, tile], axis=0)

    def whole(own, plane):
        return wide(own, beside_plane(west_ref, east_ref, plane))

    tiles = [[lat_tile(LEVELS * t + k) for k in range(LEVELS)] for t in range(TRACERS)]
    bottom_own = own_ref[OWN_BOTTOM]
    c = tracer_planes(own_ref)
    p_own = pressures(c[1], c[0])
    p_tile = pressures(tiles[1], tiles[0])
    both = wide(
        spare_north(tiles[3][0]) + spare_south(tiles[3][0]),
        spare_north(tiles[3][1]) + spare_south(tiles[3][1]),
    )
    bottom = tallen(whole(bottom_own, BOTTOM), both)
    count_u = jnp.minimum(bottom, at(bottom, 1, 1))
    count_v = jnp.minimum(bottom, at(bottom, 1, 0))
    f_u = coriolis(place * ROWS + row, 0.5)
    f_v = coriolis(place * ROWS + row, 1.0)
    none = jnp.zeros((8, COLS), f32)
    wind = [tallen(wide(own_ref[OWN_WIND + d], jnp.zeros((ROWS, COLS), f32)), jnp.zeros((8, 2 * COLS), f32)) for d in range(2)]

    def up(x):
        return at(x, 1, 0)

    def down(x):
        return at(x, -1, 0)

    stars_u, stars_v, flows, gains = [], [], [], [None] * (TRACERS * LEVELS)
    own_u, own_v = count_u[:ROWS, :COLS], count_v[:ROWS, :COLS]
    mean_u = mean_v = jnp.zeros((ROWS, COLS), f32)
    for k in range(LEVELS):
        east, north = count_u > k, count_v > k
        t0, t1, t2 = tiles[0][k], tiles[1][k], tiles[2][k]
        u_lat = wide(spare_north(t0) + spare_south(t0), spare_north(t2))
        v_lat = wide(spare_north(t1) + spare_south(t1), spare_south(t2))
        u = tallen(whole(own_ref[OWN_EAST + k], EAST + k), u_lat)
        u = jnp.where(east | (row >= ROWS), u, 0.0)
        v = tallen(whole(own_ref[OWN_NORTH + k], NORTH + k), v_lat)
        v = jnp.where(north | (row == ROWS), v, 0.0)
        p = tallen(whole(p_own[k], PRESSURE + k), wide(p_tile[k], none))
        tend_u, tend_v = momentum(k, u, v, p, wind, east, north, f_u, f_v, up, down)
        star_u = (u + time_step * tend_u)[:ROWS, :COLS]
        star_v = (v + time_step * tend_v)[:ROWS, :COLS]
        stars_u.append(star_u)
        stars_v.append(star_v)
        mean_u = mean_u + star_u
        mean_v = mean_v + star_v

        flows.append((u[:ROWS], jnp.where(east[:ROWS], tracer_diffusion, 0.0)))
        diffusion = jnp.where(north[:, :COLS], tracer_diffusion, 0.0)
        for t in range(TRACERS):
            cn = tallen(c[t][k], tiles[t][k])
            gains[LEVELS * t + k] = gain(cn, 0, v[:, :COLS], diffusion)[:ROWS]
    planes = range(TRACERS * LEVELS)
    beside = [beside_tracer(west_ref, east_ref, n) for n in planes]
    values = jnp.concatenate([wide(c[n // LEVELS][n % LEVELS], beside[n]) for n in planes], axis=0)
    flow, diffusion = (
        jnp.concatenate([flows[n % LEVELS][i] for n in planes], axis=0) for i in range(2)
    )
    along = gain(values, 1, flow, diffusion)[:, :COLS]
    for n in planes:
        t, k = divmod(n, LEVELS)
        change = along[ROWS * n : ROWS * (n + 1)] + gains[n]
        tracers_out[t, k] = jnp.where(bottom_own > k, c[t][k] + time_step * change, 0.0)
    shift_u = average_u - mean_u / jnp.maximum(own_u, 1.0)
    shift_v = average_v - mean_v / jnp.maximum(own_v, 1.0)
    for k in range(LEVELS):
        velocity_out[0, k] = jnp.where(own_u > k, stars_u[k] + shift_u, 0.0)
        velocity_out[1, k] = jnp.where(own_v > k, stars_v[k] + shift_v, 0.0)


def ring(axis, step):
    count = lax.axis_size(axis)
    return [(i, (i + step) % count) for i in range(count)]


def struct(*shape):
    return jax.ShapeDtypeStruct(shape, f32)


def vmem(*shape):
    return pltpu.VMEM(shape, f32)


def specs(count, scalars=0):
    return [pl.BlockSpec(memory_space=pltpu.SMEM)] * scalars + [
        pl.BlockSpec(memory_space=pltpu.VMEM)
    ] * count


PARAMS = pltpu.CompilerParams(vmem_limit_bytes=32 * 1024 * 1024)


def stacked(tracers, velocity, surface, wind, bottom):
    def put(values, first):
        values = values.reshape(-1, ROWS, COLS)
        after = OWN - first - values.shape[0]
        return lax.pad(
            values, jnp.zeros((), values.dtype), ((first, after, 0), (0, 0, 0), (0, 0, 0))
        )

    return (
        put(tracers, 0)
        + put(velocity, OWN_EAST)
        + put(surface, OWN_SURFACE)
        + put(wind, OWN_WIND)
        + put(bottom, OWN_BOTTOM).astype(f32)
    )


def shards(tracers, velocity, surface, wind, bottom):
    place = lax.axis_index("lat").astype(jnp.int32).reshape(1)
    own = stacked(tracers, velocity, surface, wind, bottom)
    payload = struct(PLANES // 4 + 1, ROWS, COLS)
    to_right, to_left = pl.pallas_call(
        pack_kernel,
        out_shape=(payload, payload),
        in_specs=specs(1),
        out_specs=tuple(specs(2)),
        compiler_params=PARAMS,
        name="pack",
    )(own)
    west = lax.ppermute(to_right, "lon", ring("lon", 1))
    east = lax.ppermute(to_left, "lon", ring("lon", -1))
    chunks = pl.pallas_call(
        send_kernel,
        out_shape=struct(MEMBERS, CHUNK, COLS),
        in_specs=specs(3, 1),
        out_specs=specs(1)[0],
        scratch_shapes=[
            vmem(12 * ROWS, COLS),
            vmem(2, COLS, COLS),
            vmem(40, 2 * COLS),
            vmem(COLS + 2 * HALO, COLS),
        ],
        compiler_params=PARAMS,
        name="columns",
    )(place, own, west, east)
    slabs = lax.all_to_all(chunks, "lat", 0, 0, tiled=True)
    answers = pl.pallas_call(
        slab_kernel,
        out_shape=struct(MEMBERS, BACK, COLS),
        in_specs=specs(1),
        out_specs=specs(1)[0],
        scratch_shapes=[vmem(COLS, COLS)],
        compiler_params=PARAMS,
        name="substeps",
    )(slabs)
    home = lax.all_to_all(answers, "lat", 0, 0, tiled=True)
    return pl.pallas_call(
        finish_kernel,
        out_shape=(
            struct(TRACERS, LEVELS, ROWS, COLS),
            struct(2, LEVELS, ROWS, COLS),
            struct(ROWS, COLS),
            struct(ROWS, COLS),
        ),
        in_specs=specs(4, 1),
        out_specs=tuple(specs(4)),
        scratch_shapes=[vmem(COLS, COLS), vmem(4 * ROWS, COLS)],
        compiler_params=PARAMS,
        name="finish",
    )(place, home, own, west, east)


def solution(mesh):
    placed = (
        P(None, None, "lat", "lon"),
        P(None, None, "lat", "lon"),
        P("lat", "lon"),
        P(None, "lat", "lon"),
        P("lat", "lon"),
    )
    return jax.shard_map(
        shards,
        mesh=mesh,
        in_specs=placed,
        out_specs=(
            P(None, None, "lat", "lon"),
            P(None, None, "lat", "lon"),
            P("lat", "lon"),
            P("lat", "lon"),
        ),
        check_vma=False,
    )
```

time: 67.3 us -> 56.4 us (0.84)
  Pallas kernels: 15.9 us -> 8.11 us
  local copies, waits for them, and re-layouts: 3.98 us -> 0 us
  other arithmetic: 0 us -> 1.09 us
    pallas_call x1, Pallas kernels: 9.02 us -> 4.48 us  [shards(): pl.pallas_call(slab_kernel, out_shape=struct(MEMBERS, BACK, COLS), in_spe...]
    unnamed x20 -> x0, local copies, waits for them, and re-layouts: 3.98 us -> none
    pallas_call x1, Pallas kernels: 5.93 us -> 2.72 us  [shards(): pl.pallas_call(finish_kernel, out_shape=(struct(TRACERS, LEVELS, ROWS, CO...]
    add x0 -> x1, other arithmetic: none -> 1.09 us  [stacked(): put(tracers, 0) + put(velocity, OWN_EAST) + put(surface, OWN_SURFACE)]
where the time goes in v2:
time: 56.4 us; the launch traced here: 56.2 us
  blocking collectives  28.5 us (51%)
  starting transfers between devices  16.5 us (29%)
  Pallas kernels  8.11 us (14%)
  waiting for transfers between devices  1.3 us (2%)
  other arithmetic  1.09 us (2%)
  between operations  0.69 us (1%)
    all_to_all x1, blocking collectives, shards(): slabs = lax.all_to_all(chunks, 'lat', 0, 0, tiled=True)  18.5 us
    ppermute x1, starting transfers between devices, shards(): east = lax.ppermute(to_left, 'lon', ring('lon', -1))  10.9 us
    all_to_all x1, blocking collectives, shards(): home = lax.all_to_all(answers, 'lat', 0, 0, tiled=True)  9.94 us
    ppermute x1, starting transfers between devices, shards(): west = lax.ppermute(to_right, 'lon', ring('lon', 1))  5.65 us
    pallas_call x1, Pallas kernels, shards(): pl.pallas_call(slab_kernel, out_shape=struct(MEMBERS, BACK, COLS), in_spe...  4.48 us
    pallas_call x1, Pallas kernels, shards(): pl.pallas_call(finish_kernel, out_shape=(struct(TRACERS, LEVELS, ROWS, CO...  2.72 us
    ppermute x1, waiting for transfers between devices, shards(): east = lax.ppermute(to_left, 'lon', ring('lon', -1))  1.3 us
  transfers between devices with their start and end apart: 2, of which 1 were waited for; matrix products, arithmetic and copies ran while one was open for 0% of the time, Pallas kernels for 0%

profile of v2, /device:TPU:1, one launch (start us, length us, event | category | flops | bytes accessed | tf_op | source)
XLA Modules:
  0.0 56.2 jit_solution(17067548404130626574)
XLA Ops:
  0.6 1.1 %convert_add_fusion.own_ref = f32[52,16,128]{2,1,0:T(8,128)S(1)} fusion(s32[1,16,128]{2,1,0:T(8,128)} %bitcast.7, f32[2,16,128]{2,1,0:T(8,128)} %param.8, f32[1,16,128]{2,1,0:T(8,128)} %bitcast.8, f32[16,16,128]{2,1,0:T(8,128)} %bitcast.6, f32[32,16,128]{2,1,0:T(8,128)} %bitcast.5), kind=kLoop, calls=%fused_computation | loop fusion | flops 532480 | bytes 851968 | tf_op jit(solution)/shard_map/add | solution.py:537
  1.7 0.2 pack.1
  1.9 5.7 %collective-permute-start = (f32[8,16,128]{2,1,0:T(8,128)S(1)}, f32[8,16,128]{2,1,0:T(8,128)S(1)}, u32[]{:S(2)}, u32[]{:S(2)}) collective-permute-start(f32[8,16,128]{2,1,0:T(8,128)S(1)} %get-tuple-element.6), channel_id=1, source_target_pairs={{0,1},{1,2},{2,3},{3,4},{4,5},{5,6},{6,7},{7,8},{8,9},{9,10},{10,1... | collective-permute-start | bytes 196616 | tf_op jit(solution)/shard_map/ppermute | solution.py:557
  7.6 10.9 %collective-permute-start.1 = (f32[8,16,128]{2,1,0:T(8,128)S(1)}, f32[8,16,128]{2,1,0:T(8,128)S(1)}, u32[]{:S(2)}, u32[]{:S(2)}) collective-permute-start(f32[8,16,128]{2,1,0:T(8,128)S(1)} %get-tuple-element.7), channel_id=1, source_target_pairs={{0,31},{1,0},{2,1},{3,2},{4,3},{5,4},{6,5},{7,6},{8,7},{9,8},{10,9... | collective-permute-start | bytes 196616 | tf_op jit(solution)/shard_map/ppermute | solution.py:558
  18.4 0.0 collective-permute-done.west_ref
  18.5 1.3 %collective-permute-done.1.east_ref = f32[8,16,128]{2,1,0:T(8,128)S(1)} collective-permute-done((f32[8,16,128]{2,1,0:T(8,128)S(1)}, f32[8,16,128]{2,1,0:T(8,128)S(1)}, u32[]{:S(2)}, u32[]{:S(2)}) %collective-permute-start.1) | collective-permute-done | bytes 65568 | tf_op jit(solution)/shard_map/ppermute | solution.py:558
  19.7 0.7 %columns.1 = f32[16,96,128]{2,1,0:T(8,128)S(1)} custom-call(s32[1]{0:T(128)} %bitcast.place_ref, f32[52,16,128]{2,1,0:T(8,128)S(1)} %convert_add_fusion.own_ref, f32[8,16,128]{2,1,0:T(8,128)S(1)} %collective-permute-done.west_ref, f32[8,16,128]{2,1,0:T(8,128)S(1)} %collective-permute-done.1.east_ref), custom_call_target="tpu_custom_call" | custom-call | tf_op jit(solution)/shard_map/columns/pallas_call | solution.py:559
  20.5 18.5 %all_to_all.10.in_ref = f32[16,96,128]{2,1,0:T(8,128)S(1)} all-to-all(f32[16,96,128]{2,1,0:T(8,128)S(1)} %columns.1), channel_id=1, replica_groups=mesh['lat'=16,'lon'=32] {'lat'}, dimensions={0} | all-to-all | bytes 1572864 | tf_op jit(solution)/shard_map/all_to_all | solution.py:573
  39.0 4.5 %substeps.1 = f32[16,24,128]{2,1,0:T(8,128)S(1)} custom-call(f32[16,96,128]{2,1,0:T(8,128)S(1)} %all_to_all.10.in_ref), custom_call_target="tpu_custom_call" | custom-call | tf_op jit(solution)/shard_map/substeps/pallas_call | solution.py:574
  43.5 9.9 %all_to_all.11.in_ref = f32[16,24,128]{2,1,0:T(8,128)S(1)} all-to-all(f32[16,24,128]{2,1,0:T(8,128)S(1)} %substeps.1), channel_id=1, replica_groups=mesh['lat'=16,'lon'=32] {'lat'}, dimensions={0} | all-to-all | bytes 393216 | tf_op jit(solution)/shard_map/all_to_all | solution.py:583
  53.4 2.7 %finish.1 = (f32[4,8,16,128]{3,2,1,0:T(8,128)}, f32[2,8,16,128]{3,2,1,0:T(8,128)}, f32[16,128]{1,0:T(8,128)}, f32[16,128]{1,0:T(8,128)}) custom-call(s32[1]{0:T(128)} %bitcast.place_ref, f32[16,24,128]{2,1,0:T(8,128)S(1)} %all_to_all.11.in_ref, f32[52,16,128]{2,1,0:T(8,128)S(1)} %convert_add_fusion.own_ref, f32[8,16,128]{2,1,0:T(8,128)S(1)} %collective-permute-done.west_ref, ...), custom_call_target="tpu_custom_call" | custom-call | tf_op jit(solution)/shard_map/finish/pallas_call | solution.py:584
Async XLA Ops:
  1.9 16.5 %collective-permute-start = (f32[8,16,128]{2,1,0:T(8,128)S(1)}, f32[8,16,128]{2,1,0:T(8,128)S(1)}, u32[]{:S(2)}, u32[]{:S(2)}) collective-permute-start(f32[8,16,128]{2,1,0:T(8,128)S(1)} %get-tuple-element.6), channel_id=1, source_target_pairs={{0,1},{1,2},{2,3},{3,4},{4,5},{5,6},{6,7},{7,8},{8,9},{9,10},{10,1... | collective-permute-start | bytes 196616 | tf_op jit(solution)/shard_map/ppermute | solution.py:557
  7.6 12.2 %collective-permute-start.1 = (f32[8,16,128]{2,1,0:T(8,128)S(1)}, f32[8,16,128]{2,1,0:T(8,128)S(1)}, u32[]{:S(2)}, u32[]{:S(2)}) collective-permute-start(f32[8,16,128]{2,1,0:T(8,128)S(1)} %get-tuple-element.7), channel_id=1, source_target_pairs={{0,31},{1,0},{2,1},{3,2},{4,3},{5,4},{6,5},{7,6},{8,7},{9,8},{10,9... | collective-permute-start | bytes 196616 | tf_op jit(solution)/shard_map/ppermute | solution.py:558

commit v3 on v2

--- a/solution.py
+++ b/solution.py
@@ -94,15 +94,6 @@
         block == s, east_ref[q], jnp.where(block == (s + 3) % 4, west_ref[q], 0.0)
     )
     return at(both, 32 * s, 1)
-
-
-def beside_tracer(west_ref, east_ref, n):
-    block = ids((ROWS, COLS), 1) // 4
-    last = PLANES // 4
-    both = jnp.where(
-        block == n, east_ref[last], jnp.where(block == (n + 31) % 32, west_ref[last], 0.0)
-    )
-    return at(both, 4 * n, 1)
 
 
 def momentum(k, u, v, p, wind, east, north, f_u, f_v, up, down):
@@ -362,7 +353,9 @@
             sums = [a + b[centre : centre + 8] for a, b in zip(sums, (u0, u1, v0, v1))]
             return (h0, h1, h2, u0, u1, v0, v1, *sums)
 
-        *state, a0, a1, a2, a3 = lax.fori_loop(0, steps, advance, (*state, *total))
+        *state, a0, a1, a2, a3 = lax.fori_loop(
+            0, steps, advance, (*state, *total), unroll=True
+        )
         total = (a0, a1, a2, a3)
     height = [x[8:16] for x in state[:2]]
     average = [x * (1.0 / SUBSTEPS) for x in total]
@@ -398,8 +391,48 @@
     return flux - at(flux, -1, axis)
 
 
+def inner_kernel(own_ref, out_ref):
+    bottom = own_ref[OWN_BOTTOM]
+    c = tracer_planes(own_ref)
+    count = jnp.minimum(bottom, at(bottom, 1, 1))
+    values = jnp.concatenate([plane for tracer in c for plane in tracer], axis=0)
+    flow, diffusion = [], []
+    for k in range(LEVELS):
+        flow.append(jnp.where(count > k, own_ref[OWN_EAST + k], 0.0))
+        diffusion.append(jnp.where(count > k, tracer_diffusion, 0.0))
+    flow, diffusion = (jnp.concatenate(x * TRACERS, axis=0) for x in (flow, diffusion))
+    lane = ids(values.shape, 1)
+
+    def moved(step):
+        inside = lane < COLS - step if step > 0 else lane >= -step
+        return jnp.where(inside, at(values, step, 1), 0.0)
+
+    ahead = moved(1)
+    face = (37.0 * (values + ahead) - 8.0 * (moved(-1) + moved(2)) + (moved(-2) + moved(3))) * (
+        1.0 / 60.0
+    )
+    flux = jnp.where(lane < COLS - 1, diffusion * (ahead - values) - flow * face, 0.0)
+    out_ref[...] = flux - at(flux, -1, 1)
+
+
+def outer(west, east, left, right, flow_w, flow_l, flow_r, diff_w, diff_r):
+    q = ids((ROWS, COLS), 1) % 4
+    sixtieth = 1.0 / 60.0
+    w1, w2, w3 = at(west, 3, 1), at(west, 2, 1), at(west, 1, 1)
+    face = 37.0 * (w1 + left) - 8.0 * (w2 + at(left, 1, 1)) + (w3 + at(left, 2, 1))
+    through = at(diff_w, 3, 1) * (left - w1) - at(flow_w, 3, 1) * (face * sixtieth)
+    flux = jnp.where(q == 0, w2 - 8.0 * w1, jnp.where(q == 1, w2, 0.0)) * (-sixtieth) * flow_l
+    low = flux - at(flux, -1, 1) - jnp.where(q == 0, through, 0.0)
+    e1, e2, e3 = at(east, -3, 1), at(east, -2, 1), at(east, -1, 1)
+    face = 37.0 * (right + e1) - 8.0 * (at(right, -1, 1) + e2) + (at(right, -2, 1) + e3)
+    through = diff_r * (e1 - right) - flow_r * (face * sixtieth)
+    flux = jnp.where(q == 2, e3 - 8.0 * e2, jnp.where(q == 1, e3, 0.0)) * (-sixtieth) * flow_r
+    high = flux - at(flux, -1, 1) + jnp.where(q == 3, through, 0.0)
+    return low, high
+
+
 def finish_kernel(
-    place_ref, in_ref, own_ref, west_ref, east_ref,
+    place_ref, in_ref, own_ref, west_ref, east_ref, right_ref, left_ref, inner_ref,
     tracers_out, velocity_out, height_out, stream_out, turned_ref, rows_ref,
 ):
     place = place_ref[0]
@@ -485,16 +518,31 @@
         for t in range(TRACERS):
             cn = tallen(c[t][k], tiles[t][k])
             gains[LEVELS * t + k] = gain(cn, 0, v[:, :COLS], diffusion)[:ROWS]
+    block = ids((ROWS, COLS), 1) // 4
+
+    def packed(which, half, ahead):
+        tile = jnp.zeros((ROWS, COLS), f32)
+        for k in range(LEVELS):
+            values = flows[k][which][:, COLS * half : COLS * (half + 1)]
+            tile = jnp.where(block % LEVELS == k, at(values, -4 * (k + ahead), 1), tile)
+        for step in (32, 64):
+            tile = jnp.where(block * 4 % (2 * step) < step, tile, at(tile, -step, 1))
+        return tile
+
+    last = PLANES // 4
+    low, high = outer(
+        at(west_ref[last], -4, 1), east_ref[last], left_ref[last], at(right_ref[last], -4, 1),
+        packed(0, 1, 1), packed(0, 0, 0), packed(0, 0, 1), packed(1, 1, 1), packed(1, 0, 1),
+    )
+    high = at(high, 4, 1)
     planes = range(TRACERS * LEVELS)
-    beside = [beside_tracer(west_ref, east_ref, n) for n in planes]
-    values = jnp.concatenate([wide(c[n // LEVELS][n % LEVELS], beside[n]) for n in planes], axis=0)
-    flow, diffusion = (
-        jnp.concatenate([flows[n % LEVELS][i] for n in planes], axis=0) for i in range(2)
-    )
-    along = gain(values, 1, flow, diffusion)[:, :COLS]
+    sides = [
+        at(jnp.where(block == n, low, jnp.where(block == (n + 31) % 32, high, 0.0)), 4 * n, 1)
+        for n in planes
+    ]
     for n in planes:
         t, k = divmod(n, LEVELS)
-        change = along[ROWS * n : ROWS * (n + 1)] + gains[n]
+        change = inner_ref[ROWS * n : ROWS * (n + 1)] + sides[n] + gains[n]
         tracers_out[t, k] = jnp.where(bottom_own > k, c[t][k] + time_step * change, 0.0)
     shift_u = average_u - mean_u / jnp.maximum(own_u, 1.0)
     shift_v = average_v - mean_v / jnp.maximum(own_v, 1.0)
@@ -556,6 +604,15 @@
     )(own)
     west = lax.ppermute(to_right, "lon", ring("lon", 1))
     east = lax.ppermute(to_left, "lon", ring("lon", -1))
+    inner = pl.pallas_call(
+        inner_kernel,
+        out_shape=struct(TRACERS * LEVELS * ROWS, COLS),
+        in_specs=specs(1),
+        out_specs=specs(1)[0],
+        compiler_params=PARAMS,
+        cost_estimate=pl.CostEstimate(flops=1500000, bytes_accessed=3000000, transcendentals=0),
+        name="inner",
+    )(own)
     chunks = pl.pallas_call(
         send_kernel,
         out_shape=struct(MEMBERS, CHUNK, COLS),
@@ -589,12 +646,12 @@
             struct(ROWS, COLS),
             struct(ROWS, COLS),
         ),
-        in_specs=specs(4, 1),
+        in_specs=specs(7, 1),
         out_specs=tuple(specs(4)),
         scratch_shapes=[vmem(COLS, COLS), vmem(4 * ROWS, COLS)],
         compiler_params=PARAMS,
         name="finish",
-    )(place, home, own, west, east)
+    )(place, home, own, west, east, to_right, to_left, inner)
 
 
 def solution(mesh):

time: 56.4 us -> 56.7 us (level)
  blocking collectives: 28.5 us -> 18.5 us
  waiting for transfers between devices: 1.3 us -> 7.52 us
  starting transfers between devices: 16.5 us -> 20.6 us
    all_to_all x1 -> x0, blocking collectives: 9.94 us -> none  [shards(): home = lax.all_to_all(answers, 'lat', 0, 0, tiled=True)]
    all_to_all x0 -> x1, waiting for transfers between devices: none -> 6.22 us  [shards(): home = lax.all_to_all(answers, 'lat', 0, 0, tiled=True)]
    all_to_all x0 -> x1, starting transfers between devices: none -> 4.11 us  [shards(): home = lax.all_to_all(answers, 'lat', 0, 0, tiled=True)]
    pallas_call x1, Pallas kernels: 2.72 us -> 2.13 us  [shards(): pl.pallas_call(finish_kernel, out_shape=(struct(TRACERS, LEVELS, ROWS, CO...]
  transfers between devices with their start and end apart: 2 -> 3, of which waited for: 1 -> 2; matrix products, arithmetic and copies ran while one was open for 0% -> 0% of each run, Pallas kernels for 0% -> 1%
where the time goes in v3:
time: 56.7 us; the launch traced here: 56.3 us
  starting transfers between devices  20.6 us (36%)
  blocking collectives  18.5 us (33%)
  Pallas kernels  7.88 us (14%)
  waiting for transfers between devices  7.52 us (13%)
  other arithmetic  1.09 us (2%)
  between operations  0.69 us (1%)
    all_to_all x1, blocking collectives, shards(): slabs = lax.all_to_all(chunks, 'lat', 0, 0, tiled=True)  18.5 us
    ppermute x1, starting transfers between devices, shards(): east = lax.ppermute(to_left, 'lon', ring('lon', -1))  10.9 us
    all_to_all x1, waiting for transfers between devices, shards(): home = lax.all_to_all(answers, 'lat', 0, 0, tiled=True)  6.22 us
    ppermute x1, starting transfers between devices, shards(): west = lax.ppermute(to_right, 'lon', ring('lon', 1))  5.65 us
    pallas_call x1, Pallas kernels, shards(): pl.pallas_call(slab_kernel, out_shape=struct(MEMBERS, BACK, COLS), in_spe...  4.35 us
    all_to_all x1, starting transfers between devices, shards(): home = lax.all_to_all(answers, 'lat', 0, 0, tiled=True)  4.11 us
    pallas_call x1, Pallas kernels, shards(): pl.pallas_call(finish_kernel, out_shape=(struct(TRACERS, LEVELS, ROWS, CO...  2.13 us
    ppermute x1, waiting for transfers between devices, shards(): east = lax.ppermute(to_left, 'lon', ring('lon', -1))  1.3 us
  transfers between devices with their start and end apart: 3, of which 2 were waited for; matrix products, arithmetic and copies ran while one was open for 0% of the time, Pallas kernels for 1%

profile of v3, /device:TPU:1, one launch (start us, length us, event | category | flops | bytes accessed | tf_op | source)
XLA Modules:
  0.0 56.3 jit_solution(11051668196507210486)
XLA Ops:
  0.6 1.1 %convert_add_fusion.own_ref = f32[52,16,128]{2,1,0:T(8,128)S(1)} fusion(s32[1,16,128]{2,1,0:T(8,128)} %bitcast.7, f32[2,16,128]{2,1,0:T(8,128)} %param.8, f32[1,16,128]{2,1,0:T(8,128)} %bitcast.8, f32[16,16,128]{2,1,0:T(8,128)} %bitcast.6, f32[32,16,128]{2,1,0:T(8,128)} %bitcast.5), kind=kLoop, calls=%fused_computation | loop fusion | flops 532480 | bytes 851968 | tf_op jit(solution)/shard_map/add | solution.py:585
  1.7 0.2 pack.1
  1.9 5.7 %collective-permute-start = (f32[8,16,128]{2,1,0:T(8,128)S(1)}, f32[8,16,128]{2,1,0:T(8,128)S(1)}, u32[]{:S(2)}, u32[]{:S(2)}) collective-permute-start(f32[8,16,128]{2,1,0:T(8,128)S(1)} %get-tuple-element.6.right_ref), channel_id=1, source_target_pairs={{0,1},{1,2},{2,3},{3,4},{4,5},{5,6},{6,7},{7,8},{8,9},{9,10},{10,1... | collective-permute-start | bytes 196616 | tf_op jit(solution)/shard_map/ppermute | solution.py:605
  7.6 10.9 %collective-permute-start.1 = (f32[8,16,128]{2,1,0:T(8,128)S(1)}, f32[8,16,128]{2,1,0:T(8,128)S(1)}, u32[]{:S(2)}, u32[]{:S(2)}) collective-permute-start(f32[8,16,128]{2,1,0:T(8,128)S(1)} %get-tuple-element.7.left_ref), channel_id=1, source_target_pairs={{0,31},{1,0},{2,1},{3,2},{4,3},{5,4},{6,5},{7,6},{8,7},{9,8},{10,9... | collective-permute-start | bytes 196616 | tf_op jit(solution)/shard_map/ppermute | solution.py:606
  18.4 0.0 collective-permute-done.west_ref
  18.5 1.3 %collective-permute-done.1.east_ref = f32[8,16,128]{2,1,0:T(8,128)S(1)} collective-permute-done((f32[8,16,128]{2,1,0:T(8,128)S(1)}, f32[8,16,128]{2,1,0:T(8,128)S(1)}, u32[]{:S(2)}, u32[]{:S(2)}) %collective-permute-start.1) | collective-permute-done | bytes 65568 | tf_op jit(solution)/shard_map/ppermute | solution.py:606
  19.7 0.7 %columns.1 = f32[16,96,128]{2,1,0:T(8,128)S(1)} custom-call(s32[1]{0:T(128)} %bitcast.place_ref, f32[52,16,128]{2,1,0:T(8,128)S(1)} %convert_add_fusion.own_ref, f32[8,16,128]{2,1,0:T(8,128)S(1)} %collective-permute-done.west_ref, f32[8,16,128]{2,1,0:T(8,128)S(1)} %collective-permute-done.1.east_ref), custom_call_target="tpu_custom_call" | custom-call | tf_op jit(solution)/shard_map/columns/pallas_call | solution.py:616
  20.5 18.5 %all_to_all.10.in_ref = f32[16,96,128]{2,1,0:T(8,128)S(1)} all-to-all(f32[16,96,128]{2,1,0:T(8,128)S(1)} %columns.1), channel_id=1, replica_groups=mesh['lat'=16,'lon'=32] {'lat'}, dimensions={0} | all-to-all | bytes 1572864 | tf_op jit(solution)/shard_map/all_to_all | solution.py:630
  39.0 4.4 %substeps.1 = f32[16,24,128]{2,1,0:T(8,128)} custom-call(f32[16,96,128]{2,1,0:T(8,128)S(1)} %all_to_all.10.in_ref), custom_call_target="tpu_custom_call" | custom-call | tf_op jit(solution)/shard_map/substeps/pallas_call | solution.py:631
  43.4 4.1 %all-to-all-start.1 = ((f32[16,24,128]{2,1,0:T(8,128)}), f32[16,24,128]{2,1,0:T(8,128)S(1)}, u32[]{:S(2)}, u32[]{:S(2)}) async-start(f32[16,24,128]{2,1,0:T(8,128)} %substeps.1), calls=%async_computation.1 | async-start | bytes 393216 | tf_op jit(solution)/shard_map/all_to_all | solution.py:640
  47.5 0.5 inner.1.inner_ref
  48.0 6.2 %all-to-all-done.1.in_ref = f32[16,24,128]{2,1,0:T(8,128)S(1)} async-done(((f32[16,24,128]{2,1,0:T(8,128)}), f32[16,24,128]{2,1,0:T(8,128)S(1)}, u32[]{:S(2)}, u32[]{:S(2)}) %all-to-all-start.1) | async-done | bytes 196640 | tf_op jit(solution)/shard_map/all_to_all | solution.py:640
  54.2 2.1 %finish.1 = (f32[4,8,16,128]{3,2,1,0:T(8,128)}, f32[2,8,16,128]{3,2,1,0:T(8,128)}, f32[16,128]{1,0:T(8,128)}, f32[16,128]{1,0:T(8,128)}) custom-call(s32[1]{0:T(128)} %bitcast.place_ref, f32[16,24,128]{2,1,0:T(8,128)S(1)} %all-to-all-done.1.in_ref, f32[52,16,128]{2,1,0:T(8,128)S(1)} %convert_add_fusion.own_ref, ...), custom_call_target="tpu_custom_call" | custom-call | tf_op jit(solution)/shard_map/finish/pallas_call | solution.py:641
Async XLA Ops:
  1.9 16.5 %collective-permute-start = (f32[8,16,128]{2,1,0:T(8,128)S(1)}, f32[8,16,128]{2,1,0:T(8,128)S(1)}, u32[]{:S(2)}, u32[]{:S(2)}) collective-permute-start(f32[8,16,128]{2,1,0:T(8,128)S(1)} %get-tuple-element.6.right_ref), channel_id=1, source_target_pairs={{0,1},{1,2},{2,3},{3,4},{4,5},{5,6},{6,7},{7,8},{8,9},{9,10},{10,1... | collective-permute-start | bytes 196616 | tf_op jit(solution)/shard_map/ppermute | solution.py:605
  7.6 12.2 %collective-permute-start.1 = (f32[8,16,128]{2,1,0:T(8,128)S(1)}, f32[8,16,128]{2,1,0:T(8,128)S(1)}, u32[]{:S(2)}, u32[]{:S(2)}) collective-permute-start(f32[8,16,128]{2,1,0:T(8,128)S(1)} %get-tuple-element.7.left_ref), channel_id=1, source_target_pairs={{0,31},{1,0},{2,1},{3,2},{4,3},{5,4},{6,5},{7,6},{8,7},{9,8},{10,9... | collective-permute-start | bytes 196616 | tf_op jit(solution)/shard_map/ppermute | solution.py:606
  43.4 10.8 %all-to-all-start.1 = ((f32[16,24,128]{2,1,0:T(8,128)}), f32[16,24,128]{2,1,0:T(8,128)S(1)}, u32[]{:S(2)}, u32[]{:S(2)}) async-start(f32[16,24,128]{2,1,0:T(8,128)} %substeps.1), calls=%async_computation.1 | async-start | bytes 393216 | tf_op jit(solution)/shard_map/all_to_all | solution.py:640

commit v4 on v3

--- a/solution.py
+++ b/solution.py
@@ -64,7 +64,8 @@
     return out
 
 
-def pack_kernel(own_ref, right_ref, left_ref):
+def pack_kernel(even_ref, own_ref, first_ref, second_ref):
+    even = even_ref[0] > 0
     c = tracer_planes(own_ref)
     planes = pressures(c[1], c[0])
     planes += [own_ref[n] for n in range(OWN_EAST, OWN_SURFACE)]
@@ -76,15 +77,22 @@
             moved = at(planes[4 * q + s], -32 * s, 1)
             right = jnp.where(lane // 32 == (s + 3) % 4, moved, right)
             left = jnp.where(lane // 32 == s, moved, left)
-        right_ref[q] = right
-        left_ref[q] = left
+        first_ref[q] = jnp.where(even, right, left)
+        second_ref[q] = jnp.where(even, left, right)
     right = left = jnp.zeros((ROWS, COLS), f32)
     for n in range(TRACERS * LEVELS):
         moved = at(c[n // LEVELS][n % LEVELS], -4 * n, 1)
         right = jnp.where(lane // 4 == (n + 31) % 32, moved, right)
         left = jnp.where(lane // 4 == n, moved, left)
-    right_ref[PLANES // 4] = right
-    left_ref[PLANES // 4] = left
+    first_ref[PLANES // 4] = jnp.where(even, right, left)
+    second_ref[PLANES // 4] = jnp.where(even, left, right)
+
+
+def sort_sides(even_ref, first_ref, second_ref, west_ref, east_ref):
+    even = even_ref[0] > 0
+    for q in range(PLANES // 4 + 1):
+        west_ref[q] = jnp.where(even, second_ref[q], first_ref[q])
+        east_ref[q] = jnp.where(even, first_ref[q], second_ref[q])
 
 
 def beside_plane(west_ref, east_ref, plane):
@@ -120,10 +128,11 @@
 
 
 def send_kernel(
-    place_ref, own_ref, west_ref, east_ref,
-    out_ref, split_ref, stack_ref, edge_ref, turned_ref,
+    place_ref, even_ref, own_ref, first_ref, second_ref, _,
+    out_ref, split_ref, stack_ref, edge_ref, turned_ref, west_ref, east_ref,
 ):
     place = place_ref[0]
+    sort_sides(even_ref, first_ref, second_ref, west_ref, east_ref)
     c = tracer_planes(own_ref)
     p_own = pressures(c[1], c[0])
 
@@ -432,10 +441,11 @@
 
 
 def finish_kernel(
-    place_ref, in_ref, own_ref, west_ref, east_ref, right_ref, left_ref, inner_ref,
-    tracers_out, velocity_out, height_out, stream_out, turned_ref, rows_ref,
+    place_ref, even_ref, in_ref, own_ref, first_ref, second_ref, one_ref, two_ref, inner_ref,
+    tracers_out, velocity_out, height_out, stream_out, turned_ref, rows_ref, west_ref, east_ref,
 ):
     place = place_ref[0]
+    sort_sides(even_ref, first_ref, second_ref, west_ref, east_ref)
     turned_ref[...] = in_ref[:, 0:8].reshape(COLS, COLS).T
 
     for q in range(8):
@@ -530,8 +540,11 @@
         return tile
 
     last = PLANES // 4
+    even = even_ref[0] > 0
+    left = jnp.where(even, two_ref[last], one_ref[last])
+    right = jnp.where(even, one_ref[last], two_ref[last])
     low, high = outer(
-        at(west_ref[last], -4, 1), east_ref[last], left_ref[last], at(right_ref[last], -4, 1),
+        at(west_ref[last], -4, 1), east_ref[last], left, at(right, -4, 1),
         packed(0, 1, 1), packed(0, 0, 0), packed(0, 0, 1), packed(1, 1, 1), packed(1, 0, 1),
     )
     high = at(high, 4, 1)
@@ -551,9 +564,10 @@
         velocity_out[1, k] = jnp.where(own_v > k, stars_v[k] + shift_v, 0.0)
 
 
-def ring(axis, step):
+def swaps(axis, first):
     count = lax.axis_size(axis)
-    return [(i, (i + step) % count) for i in range(count)]
+    pairs = [((i + first) % count, (i + first + 1) % count) for i in range(0, count, 2)]
+    return pairs + [(b, a) for a, b in pairs]
 
 
 def struct(*shape):
@@ -592,18 +606,19 @@
 
 def shards(tracers, velocity, surface, wind, bottom):
     place = lax.axis_index("lat").astype(jnp.int32).reshape(1)
+    even = (1 - lax.axis_index("lon") % 2).astype(jnp.int32).reshape(1)
     own = stacked(tracers, velocity, surface, wind, bottom)
     payload = struct(PLANES // 4 + 1, ROWS, COLS)
-    to_right, to_left = pl.pallas_call(
+    one, two = pl.pallas_call(
         pack_kernel,
         out_shape=(payload, payload),
-        in_specs=specs(1),
+        in_specs=specs(1, 1),
         out_specs=tuple(specs(2)),
         compiler_params=PARAMS,
         name="pack",
-    )(own)
-    west = lax.ppermute(to_right, "lon", ring("lon", 1))
-    east = lax.ppermute(to_left, "lon", ring("lon", -1))
+    )(even, own)
+    second = lax.ppermute(two, "lon", swaps("lon", 1))
+    first = lax.ppermute(one, "lon", swaps("lon", 0))
     inner = pl.pallas_call(
         inner_kernel,
         out_shape=struct(TRACERS * LEVELS * ROWS, COLS),
@@ -616,17 +631,19 @@
     chunks = pl.pallas_call(
         send_kernel,
         out_shape=struct(MEMBERS, CHUNK, COLS),
-        in_specs=specs(3, 1),
+        in_specs=specs(3, 2) + [pl.BlockSpec(memory_space=pl.ANY)],
         out_specs=specs(1)[0],
         scratch_shapes=[
             vmem(12 * ROWS, COLS),
             vmem(2, COLS, COLS),
             vmem(40, 2 * COLS),
             vmem(COLS + 2 * HALO, COLS),
+            vmem(PLANES // 4 + 1, ROWS, COLS),
+            vmem(PLANES // 4 + 1, ROWS, COLS),
         ],
         compiler_params=PARAMS,
         name="columns",
-    )(place, own, west, east)
+    )(place, even, own, first, second, inner)
     slabs = lax.all_to_all(chunks, "lat", 0, 0, tiled=True)
     answers = pl.pallas_call(
         slab_kernel,
@@ -646,12 +663,17 @@
             struct(ROWS, COLS),
             struct(ROWS, COLS),
         ),
-        in_specs=specs(7, 1),
+        in_specs=specs(7, 2),
         out_specs=tuple(specs(4)),
-        scratch_shapes=[vmem(COLS, COLS), vmem(4 * ROWS, COLS)],
+        scratch_shapes=[
+            vmem(COLS, COLS),
+            vmem(4 * ROWS, COLS),
+            vmem(PLANES // 4 + 1, ROWS, COLS),
+            vmem(PLANES // 4 + 1, ROWS, COLS),
+        ],
         compiler_params=PARAMS,
         name="finish",
-    )(place, home, own, west, east, to_right, to_left, inner)
+    )(place, even, home, own, first, second, one, two, inner)
 
 
 def solution(mesh):

time: 56.7 us -> 57.4 us (1.012)
  blocking collectives: 18.5 us -> 29.7 us
  waiting for transfers between devices: 7.52 us -> 1.12 us
  starting transfers between devices: 20.6 us -> 16.5 us
  local copies, waits for them, and re-layouts: 0 us -> 0.7 us
  Pallas kernels: 7.88 us -> 7.21 us
    all_to_all x0 -> x1, blocking collectives: none -> 9.94 us  [shards(): home = lax.all_to_all(answers, 'lat', 0, 0, tiled=True)]
    all_to_all x1 -> x0, waiting for transfers between devices: 6.22 us -> none  [shards(): home = lax.all_to_all(answers, 'lat', 0, 0, tiled=True)]
    all_to_all x1 -> x0, starting transfers between devices: 4.11 us -> none  [shards(): home = lax.all_to_all(answers, 'lat', 0, 0, tiled=True)]
    all_to_all x1, blocking collectives: 18.5 us -> 19.7 us  [shards(): slabs = lax.all_to_all(chunks, 'lat', 0, 0, tiled=True)]
    unnamed x0 -> x6, local copies, waits for them, and re-layouts: none -> 0.7 us
    pallas_call x1, Pallas kernels: 4.35 us -> 3.67 us  [shards(): pl.pallas_call(slab_kernel, out_shape=struct(MEMBERS, BACK, COLS), in_spe...]
  transfers between devices with their start and end apart: 3 -> 2, of which waited for: 2 -> 1; matrix products, arithmetic and copies ran while one was open for 0% -> 0% of each run, Pallas kernels for 1% -> 1%
where the time goes in v4:
time: 57.4 us; the launch traced here: 57 us
  blocking collectives  29.7 us (52%)
  starting transfers between devices  16.5 us (29%)
  Pallas kernels  7.21 us (13%)
  waiting for transfers between devices  1.12 us (2%)
  other arithmetic  1.05 us (2%)
  between operations  0.73 us (1%)
  local copies, waits for them, and re-layouts  0.7 us (1%)
    all_to_all x1, blocking collectives, shards(): slabs = lax.all_to_all(chunks, 'lat', 0, 0, tiled=True)  19.7 us
    ppermute x1, starting transfers between devices, shards(): second = lax.ppermute(two, 'lon', swaps('lon', 1))  10.9 us
    all_to_all x1, blocking collectives, shards(): home = lax.all_to_all(answers, 'lat', 0, 0, tiled=True)  9.94 us
    ppermute x1, starting transfers between devices, shards(): first = lax.ppermute(one, 'lon', swaps('lon', 0))  5.65 us
    pallas_call x1, Pallas kernels, shards(): pl.pallas_call(slab_kernel, out_shape=struct(MEMBERS, BACK, COLS), in_spe...  3.67 us
    pallas_call x1, Pallas kernels, shards(): pl.pallas_call(finish_kernel, out_shape=(struct(TRACERS, LEVELS, ROWS, CO...  2.14 us
  transfers between devices with their start and end apart: 2, of which 1 were waited for; matrix products, arithmetic and copies ran while one was open for 0% of the time, Pallas kernels for 1%

profile of v4, /device:TPU:1, one launch (start us, length us, event | category | flops | bytes accessed | tf_op | source)
XLA Modules:
  0.0 57.0 jit_solution(15743302454890439688)
XLA Ops:
  0.6 0.0 copy-start
  0.6 0.0 copy-start.2
  0.7 0.0 copy-start.1
  0.7 0.7 %copy-done = f32[2,16,128]{2,1,0:T(8,128)S(1)} copy-done((f32[2,16,128]{2,1,0:T(8,128)S(1)}, f32[2,16,128]{2,1,0:T(8,128)}, u32[]{:S(2)}) %copy-start) | copy-done | bytes 16408
  1.4 0.0 copy-done.2
  1.4 0.0 copy-done.1
  1.4 1.1 %convert_add_fusion.own_ref = f32[52,16,128]{2,1,0:T(8,128)S(1)} fusion(s32[1,16,128]{2,1,0:T(8,128)S(1)} %bitcast.8, f32[2,16,128]{2,1,0:T(8,128)S(1)} %copy-done, f32[1,16,128]{2,1,0:T(8,128)S(1)} %bitcast.9, f32[16,16,128]{2,1,0:T(8,128)} %bitcast.7, f32[32,16,128]{2,1,0:T(8,128)} %bitcast.6), kind=kLoop, calls=%fused_computation | loop fusion | flops 532480 | bytes 851968 | tf_op jit(solution)/shard_map/add | solution.py:599
  2.4 0.2 pack.1
  2.6 5.7 %collective-permute-start = (f32[8,16,128]{2,1,0:T(8,128)S(1)}, f32[8,16,128]{2,1,0:T(8,128)S(1)}, u32[]{:S(2)}, u32[]{:S(2)}) collective-permute-start(f32[8,16,128]{2,1,0:T(8,128)S(1)} %get-tuple-element.6.one_ref), channel_id=1, source_target_pairs={{0,1},{2,3},{4,5},{6,7},{8,9},{10,11},{12,13},{14,15},{16,17},{18,... | collective-permute-start | bytes 196616 | tf_op jit(solution)/shard_map/ppermute | solution.py:621
  8.3 10.9 %collective-permute-start.1 = (f32[8,16,128]{2,1,0:T(8,128)S(1)}, f32[8,16,128]{2,1,0:T(8,128)S(1)}, u32[]{:S(2)}, u32[]{:S(2)}) collective-permute-start(f32[8,16,128]{2,1,0:T(8,128)S(1)} %get-tuple-element.7.two_ref), channel_id=1, source_target_pairs={{1,2},{3,4},{5,6},{7,8},{9,10},{11,12},{13,14},{15,16},{17,18},{19... | collective-permute-start | bytes 196616 | tf_op jit(solution)/shard_map/ppermute | solution.py:620
  19.2 0.5 inner.1._.inner_ref
  19.7 0.0 collective-permute-done.first_ref
  19.7 1.1 %collective-permute-done.1.second_ref = f32[8,16,128]{2,1,0:T(8,128)S(1)} collective-permute-done((f32[8,16,128]{2,1,0:T(8,128)S(1)}, f32[8,16,128]{2,1,0:T(8,128)S(1)}, u32[]{:S(2)}, u32[]{:S(2)}) %collective-permute-start.1) | collective-permute-done | bytes 65568 | tf_op jit(solution)/shard_map/ppermute | solution.py:620
  20.8 0.7 %columns.1 = f32[16,96,128]{2,1,0:T(8,128)S(1)} custom-call(s32[1]{0:T(128)} %bitcast.place_ref, s32[1]{0:T(128)} %bitcast.1.even_ref, f32[52,16,128]{2,1,0:T(8,128)S(1)} %convert_add_fusion.own_ref, f32[8,16,128]{2,1,0:T(8,128)S(1)} %collective-permute-done.first_ref, f32[8,16,128]{2,1,0:T(8,128)S(1)} %collective-permute-done.1.second_ref, ...), custom_call_target="tpu_custom_call" | custom-call | tf_op jit(solution)/shard_map/columns/pallas_call | solution.py:631
  21.5 19.7 %all_to_all.10.in_ref = f32[16,96,128]{2,1,0:T(8,128)S(1)} all-to-all(f32[16,96,128]{2,1,0:T(8,128)S(1)} %columns.1), channel_id=1, replica_groups=mesh['lat'=16,'lon'=32] {'lat'}, dimensions={0} | all-to-all | bytes 1572864 | tf_op jit(solution)/shard_map/all_to_all | solution.py:647
  41.3 3.7 %substeps.1 = f32[16,24,128]{2,1,0:T(8,128)S(1)} custom-call(f32[16,96,128]{2,1,0:T(8,128)S(1)} %all_to_all.10.in_ref), custom_call_target="tpu_custom_call" | custom-call | tf_op jit(solution)/shard_map/substeps/pallas_call | solution.py:648
  45.0 9.9 %all_to_all.11.in_ref = f32[16,24,128]{2,1,0:T(8,128)S(1)} all-to-all(f32[16,24,128]{2,1,0:T(8,128)S(1)} %substeps.1), channel_id=1, replica_groups=mesh['lat'=16,'lon'=32] {'lat'}, dimensions={0} | all-to-all | bytes 393216 | tf_op jit(solution)/shard_map/all_to_all | solution.py:657
  54.9 2.1 %finish.1 = (f32[4,8,16,128]{3,2,1,0:T(8,128)}, f32[2,8,16,128]{3,2,1,0:T(8,128)}, f32[16,128]{1,0:T(8,128)}, f32[16,128]{1,0:T(8,128)}) custom-call(s32[1]{0:T(128)} %bitcast.place_ref, s32[1]{0:T(128)} %bitcast.1.even_ref, f32[16,24,128]{2,1,0:T(8,128)S(1)} %all_to_all.11.in_ref, f32[52,16,128]{2,1,0:T(8,128)S(1)} %convert_add_fusion.own_ref, ...), custom_call_target="tpu_custom_call" | custom-call | tf_op jit(solution)/shard_map/finish/pallas_call | solution.py:658
Async XLA Ops:
  0.6 0.7 %copy-start = (f32[2,16,128]{2,1,0:T(8,128)S(1)}, f32[2,16,128]{2,1,0:T(8,128)}, u32[]{:S(2)}) copy-start(f32[2,16,128]{2,1,0:T(8,128)} %param.8) | copy-start | bytes 49156
  0.6 0.7 %copy-start.2 = (f32[16,128]{1,0:T(8,128)S(1)}, f32[16,128]{1,0:T(8,128)}, u32[]{:S(2)}) copy-start(f32[16,128]{1,0:T(8,128)} %param.7) | copy-start | bytes 24580
  0.7 0.7 %copy-start.1 = (s32[16,128]{1,0:T(8,128)S(1)}, s32[16,128]{1,0:T(8,128)}, u32[]{:S(2)}) copy-start(s32[16,128]{1,0:T(8,128)} %param.9) | copy-start | bytes 24580
  2.6 17.1 %collective-permute-start = (f32[8,16,128]{2,1,0:T(8,128)S(1)}, f32[8,16,128]{2,1,0:T(8,128)S(1)}, u32[]{:S(2)}, u32[]{:S(2)}) collective-permute-start(f32[8,16,128]{2,1,0:T(8,128)S(1)} %get-tuple-element.6.one_ref), channel_id=1, source_target_pairs={{0,1},{2,3},{4,5},{6,7},{8,9},{10,11},{12,13},{14,15},{16,17},{18,... | collective-permute-start | bytes 196616 | tf_op jit(solution)/shard_map/ppermute | solution.py:621
  8.3 12.5 %collective-permute-start.1 = (f32[8,16,128]{2,1,0:T(8,128)S(1)}, f32[8,16,128]{2,1,0:T(8,128)S(1)}, u32[]{:S(2)}, u32[]{:S(2)}) collective-permute-start(f32[8,16,128]{2,1,0:T(8,128)S(1)} %get-tuple-element.7.two_ref), channel_id=1, source_target_pairs={{1,2},{3,4},{5,6},{7,8},{9,10},{11,12},{13,14},{15,16},{17,18},{19... | collective-permute-start | bytes 196616 | tf_op jit(solution)/shard_map/ppermute | solution.py:620

commit v5 on v3

--- a/solution.py
+++ b/solution.py
@@ -120,8 +120,8 @@
 
 
 def send_kernel(
-    place_ref, own_ref, west_ref, east_ref,
-    out_ref, split_ref, stack_ref, edge_ref, turned_ref,
+    place_ref, own_ref, west_ref, east_ref, right_ref, left_ref, inner_ref,
+    out_ref, along_ref, split_ref, stack_ref, edge_ref, turned_ref,
 ):
     place = place_ref[0]
     c = tracer_planes(own_ref)
@@ -189,6 +189,29 @@
         out_ref[d, :SLAB] = turned_ref[8 * d : 8 * d + SLAB]
         out_ref[d, EDGE:CHUNK] = at(edge, 8 * d - HALO, 1)[:, :COLS]
 
+    block = ids((ROWS, COLS), 1) // 4
+    flows = [(us[k], jnp.where(count_u > k, tracer_diffusion, 0.0)) for k in range(LEVELS)]
+
+    def packed(which, half, ahead):
+        tile = jnp.zeros((ROWS, COLS), f32)
+        for k in range(LEVELS):
+            values = flows[k][which][:, COLS * half : COLS * (half + 1)]
+            tile = jnp.where(block % LEVELS == k, at(values, -4 * (k + ahead), 1), tile)
+        for step in (32, 64):
+            tile = jnp.where(block * 4 % (2 * step) < step, tile, at(tile, -step, 1))
+        return tile
+
+    last = PLANES // 4
+    low, high = outer(
+        at(west_ref[last], -4, 1), east_ref[last], left_ref[last], at(right_ref[last], -4, 1),
+        packed(0, 1, 1), packed(0, 0, 0), packed(0, 0, 1), packed(1, 1, 1), packed(1, 0, 1),
+    )
+    high = at(high, 4, 1)
+    for n in range(TRACERS * LEVELS):
+        both = jnp.where(block == n, low, jnp.where(block == (n + 31) % 32, high, 0.0))
+        rows = slice(ROWS * n, ROWS * (n + 1))
+        along_ref[rows] = inner_ref[rows] + at(both, 4 * n, 1)
+
     sub = ids((8, COLS), 0)
 
     def spare(n):
@@ -432,7 +455,7 @@
 
 
 def finish_kernel(
-    place_ref, in_ref, own_ref, west_ref, east_ref, right_ref, left_ref, inner_ref,
+    place_ref, in_ref, own_ref, west_ref, east_ref, along_ref,
     tracers_out, velocity_out, height_out, stream_out, turned_ref, rows_ref,
 ):
     place = place_ref[0]
@@ -492,7 +515,7 @@
     def down(x):
         return at(x, -1, 0)
 
-    stars_u, stars_v, flows, gains = [], [], [], [None] * (TRACERS * LEVELS)
+    stars_u, stars_v, gains = [], [], [None] * (TRACERS * LEVELS)
     own_u, own_v = count_u[:ROWS, :COLS], count_v[:ROWS, :COLS]
     mean_u = mean_v = jnp.zeros((ROWS, COLS), f32)
     for k in range(LEVELS):
@@ -513,36 +536,13 @@
         mean_u = mean_u + star_u
         mean_v = mean_v + star_v
 
-        flows.append((u[:ROWS], jnp.where(east[:ROWS], tracer_diffusion, 0.0)))
         diffusion = jnp.where(north[:, :COLS], tracer_diffusion, 0.0)
         for t in range(TRACERS):
             cn = tallen(c[t][k], tiles[t][k])
             gains[LEVELS * t + k] = gain(cn, 0, v[:, :COLS], diffusion)[:ROWS]
-    block = ids((ROWS, COLS), 1) // 4
-
-    def packed(which, half, ahead):
-        tile = jnp.zeros((ROWS, COLS), f32)
-        for k in range(LEVELS):
-            values = flows[k][which][:, COLS * half : COLS * (half + 1)]
-            tile = jnp.where(block % LEVELS == k, at(values, -4 * (k + ahead), 1), tile)
-        for step in (32, 64):
-            tile = jnp.where(block * 4 % (2 * step) < step, tile, at(tile, -step, 1))
-        return tile
-
-    last = PLANES // 4
-    low, high = outer(
-        at(west_ref[last], -4, 1), east_ref[last], left_ref[last], at(right_ref[last], -4, 1),
-        packed(0, 1, 1), packed(0, 0, 0), packed(0, 0, 1), packed(1, 1, 1), packed(1, 0, 1),
-    )
-    high = at(high, 4, 1)
-    planes = range(TRACERS * LEVELS)
-    sides = [
-        at(jnp.where(block == n, low, jnp.where(block == (n + 31) % 32, high, 0.0)), 4 * n, 1)
-        for n in planes
-    ]
-    for n in planes:
+    for n in range(TRACERS * LEVELS):
         t, k = divmod(n, LEVELS)
-        change = inner_ref[ROWS * n : ROWS * (n + 1)] + sides[n] + gains[n]
+        change = along_ref[ROWS * n : ROWS * (n + 1)] + gains[n]
         tracers_out[t, k] = jnp.where(bottom_own > k, c[t][k] + time_step * change, 0.0)
     shift_u = average_u - mean_u / jnp.maximum(own_u, 1.0)
     shift_v = average_v - mean_v / jnp.maximum(own_v, 1.0)
@@ -613,11 +613,14 @@
         cost_estimate=pl.CostEstimate(flops=1500000, bytes_accessed=3000000, transcendentals=0),
         name="inner",
     )(own)
-    chunks = pl.pallas_call(
+    chunks, along = pl.pallas_call(
         send_kernel,
-        out_shape=struct(MEMBERS, CHUNK, COLS),
-        in_specs=specs(3, 1),
-        out_specs=specs(1)[0],
+        out_shape=(
+            struct(MEMBERS, CHUNK, COLS),
+            struct(TRACERS * LEVELS * ROWS, COLS),
+        ),
+        in_specs=specs(6, 1),
+        out_specs=tuple(specs(2)),
         scratch_shapes=[
             vmem(12 * ROWS, COLS),
             vmem(2, COLS, COLS),
@@ -626,7 +629,7 @@
         ],
         compiler_params=PARAMS,
         name="columns",
-    )(place, own, west, east)
+    )(place, own, west, east, to_right, to_left, inner)
     slabs = lax.all_to_all(chunks, "lat", 0, 0, tiled=True)
     answers = pl.pallas_call(
         slab_kernel,
@@ -646,12 +649,12 @@
             struct(ROWS, COLS),
             struct(ROWS, COLS),
         ),
-        in_specs=specs(7, 1),
+        in_specs=specs(5, 1),
         out_specs=tuple(specs(4)),
         scratch_shapes=[vmem(COLS, COLS), vmem(4 * ROWS, COLS)],
         compiler_params=PARAMS,
         name="finish",
-    )(place, home, own, west, east, to_right, to_left, inner)
+    )(place, home, own, west, east, along)
 
 
 def solution(mesh):

time: 56.7 us -> 54.8 us (0.966)
  blocking collectives: 18.5 us -> 28.5 us
  waiting for transfers between devices: 7.52 us -> 0.79 us
  starting transfers between devices: 20.6 us -> 16.5 us
  Pallas kernels: 7.88 us -> 6.94 us
    all_to_all x0 -> x1, blocking collectives: none -> 9.94 us  [shards(): home = lax.all_to_all(answers, 'lat', 0, 0, tiled=True)]
    all_to_all x1 -> x0, waiting for transfers between devices: 6.22 us -> none  [shards(): home = lax.all_to_all(answers, 'lat', 0, 0, tiled=True)]
    all_to_all x1 -> x0, starting transfers between devices: 4.11 us -> none  [shards(): home = lax.all_to_all(answers, 'lat', 0, 0, tiled=True)]
    pallas_call x1, Pallas kernels: 2.13 us -> 1.37 us  [shards(): pl.pallas_call(finish_kernel, out_shape=(struct(TRACERS, LEVELS, ROWS, CO...]
    pallas_call x1, Pallas kernels: 4.35 us -> 3.67 us  [shards(): pl.pallas_call(slab_kernel, out_shape=struct(MEMBERS, BACK, COLS), in_spe...]
  transfers between devices with their start and end apart: 3 -> 2, of which waited for: 2 -> 1; matrix products, arithmetic and copies ran while one was open for 0% -> 0% of each run, Pallas kernels for 1% -> 1%
where the time goes in v5:
time: 54.8 us; the launch traced here: 54.5 us
  blocking collectives  28.5 us (52%)
  starting transfers between devices  16.5 us (30%)
  Pallas kernels  6.94 us (13%)
  other arithmetic  1.09 us (2%)
  waiting for transfers between devices  0.79 us (1%)
  between operations  0.7 us (1%)
    all_to_all x1, blocking collectives, shards(): slabs = lax.all_to_all(chunks, 'lat', 0, 0, tiled=True)  18.5 us
    ppermute x1, starting transfers between devices, shards(): east = lax.ppermute(to_left, 'lon', ring('lon', -1))  10.9 us
    all_to_all x1, blocking collectives, shards(): home = lax.all_to_all(answers, 'lat', 0, 0, tiled=True)  9.94 us
    ppermute x1, starting transfers between devices, shards(): west = lax.ppermute(to_right, 'lon', ring('lon', 1))  5.65 us
    pallas_call x1, Pallas kernels, shards(): pl.pallas_call(slab_kernel, out_shape=struct(MEMBERS, BACK, COLS), in_spe...  3.67 us
    pallas_call x1, Pallas kernels, shards(): pl.pallas_call(finish_kernel, out_shape=(struct(TRACERS, LEVELS, ROWS, CO...  1.37 us
    pallas_call x1, Pallas kernels, shards(): pl.pallas_call(send_kernel, out_shape=(struct(MEMBERS, CHUNK, COLS), stru...  1.22 us
  transfers between devices with their start and end apart: 2, of which 1 were waited for; matrix products, arithmetic and copies ran while one was open for 0% of the time, Pallas kernels for 1%

profile of v5, /device:TPU:1, one launch (start us, length us, event | category | flops | bytes accessed | tf_op | source)
XLA Modules:
  0.0 54.5 jit_solution(12326904549332121172)
XLA Ops:
  0.6 1.1 %convert_add_fusion.own_ref = f32[52,16,128]{2,1,0:T(8,128)S(1)} fusion(s32[1,16,128]{2,1,0:T(8,128)} %bitcast.7, f32[2,16,128]{2,1,0:T(8,128)} %param.8, f32[1,16,128]{2,1,0:T(8,128)} %bitcast.8, f32[16,16,128]{2,1,0:T(8,128)} %bitcast.6, f32[32,16,128]{2,1,0:T(8,128)} %bitcast.5), kind=kLoop, calls=%fused_computation | loop fusion | flops 532480 | bytes 851968 | tf_op jit(solution)/shard_map/add | solution.py:585
  1.7 0.2 pack.1
  1.9 5.7 %collective-permute-start = (f32[8,16,128]{2,1,0:T(8,128)S(1)}, f32[8,16,128]{2,1,0:T(8,128)S(1)}, u32[]{:S(2)}, u32[]{:S(2)}) collective-permute-start(f32[8,16,128]{2,1,0:T(8,128)S(1)} %get-tuple-element.8.right_ref), channel_id=1, source_target_pairs={{0,1},{1,2},{2,3},{3,4},{4,5},{5,6},{6,7},{7,8},{8,9},{9,10},{10,1... | collective-permute-start | bytes 196616 | tf_op jit(solution)/shard_map/ppermute | solution.py:605
  7.6 10.9 %collective-permute-start.1 = (f32[8,16,128]{2,1,0:T(8,128)S(1)}, f32[8,16,128]{2,1,0:T(8,128)S(1)}, u32[]{:S(2)}, u32[]{:S(2)}) collective-permute-start(f32[8,16,128]{2,1,0:T(8,128)S(1)} %get-tuple-element.9.left_ref), channel_id=1, source_target_pairs={{0,31},{1,0},{2,1},{3,2},{4,3},{5,4},{6,5},{7,6},{8,7},{9,8},{10,9... | collective-permute-start | bytes 196616 | tf_op jit(solution)/shard_map/ppermute | solution.py:606
  18.4 0.5 inner.1.inner_ref
  18.9 0.0 collective-permute-done.west_ref
  19.0 0.8 %collective-permute-done.1.east_ref = f32[8,16,128]{2,1,0:T(8,128)S(1)} collective-permute-done((f32[8,16,128]{2,1,0:T(8,128)S(1)}, f32[8,16,128]{2,1,0:T(8,128)S(1)}, u32[]{:S(2)}, u32[]{:S(2)}) %collective-permute-start.1) | collective-permute-done | bytes 65568 | tf_op jit(solution)/shard_map/ppermute | solution.py:606
  19.7 1.2 %columns.1 = (f32[16,96,128]{2,1,0:T(8,128)S(1)}, f32[512,128]{1,0:T(8,128)S(1)}) custom-call(s32[1]{0:T(128)} %bitcast.place_ref, f32[52,16,128]{2,1,0:T(8,128)S(1)} %convert_add_fusion.own_ref, f32[8,16,128]{2,1,0:T(8,128)S(1)} %collective-permute-done.west_ref, f32[8,16,128]{2,1,0:T(8,128)S(1)} %collective-permute-done.1.east_ref, ...), custom_call_target="tpu_custom_call" | custom-call | tf_op jit(solution)/shard_map/columns/pallas_call | solution.py:616
  21.0 18.5 %all_to_all.10.in_ref = f32[16,96,128]{2,1,0:T(8,128)S(1)} all-to-all(f32[16,96,128]{2,1,0:T(8,128)S(1)} %get-tuple-element.10), channel_id=1, replica_groups=mesh['lat'=16,'lon'=32] {'lat'}, dimensions={0} | all-to-all | bytes 1572864 | tf_op jit(solution)/shard_map/all_to_all | solution.py:633
  39.5 3.7 %substeps.1 = f32[16,24,128]{2,1,0:T(8,128)S(1)} custom-call(f32[16,96,128]{2,1,0:T(8,128)S(1)} %all_to_all.10.in_ref), custom_call_target="tpu_custom_call" | custom-call | tf_op jit(solution)/shard_map/substeps/pallas_call | solution.py:634
  43.2 9.9 %all_to_all.11.in_ref = f32[16,24,128]{2,1,0:T(8,128)S(1)} all-to-all(f32[16,24,128]{2,1,0:T(8,128)S(1)} %substeps.1), channel_id=1, replica_groups=mesh['lat'=16,'lon'=32] {'lat'}, dimensions={0} | all-to-all | bytes 393216 | tf_op jit(solution)/shard_map/all_to_all | solution.py:643
  53.1 1.4 %finish.1 = (f32[4,8,16,128]{3,2,1,0:T(8,128)}, f32[2,8,16,128]{3,2,1,0:T(8,128)}, f32[16,128]{1,0:T(8,128)}, f32[16,128]{1,0:T(8,128)}) custom-call(s32[1]{0:T(128)} %bitcast.place_ref, f32[16,24,128]{2,1,0:T(8,128)S(1)} %all_to_all.11.in_ref, f32[52,16,128]{2,1,0:T(8,128)S(1)} %convert_add_fusion.own_ref, f32[8,16,128]{2,1,0:T(8,128)S(1)} %collective-permute-done.west_ref, ...), custom_call_target="tpu_custom_call" | custom-call | tf_op jit(solution)/shard_map/finish/pallas_call | solution.py:644
Async XLA Ops:
  1.9 17.0 %collective-permute-start = (f32[8,16,128]{2,1,0:T(8,128)S(1)}, f32[8,16,128]{2,1,0:T(8,128)S(1)}, u32[]{:S(2)}, u32[]{:S(2)}) collective-permute-start(f32[8,16,128]{2,1,0:T(8,128)S(1)} %get-tuple-element.8.right_ref), channel_id=1, source_target_pairs={{0,1},{1,2},{2,3},{3,4},{4,5},{5,6},{6,7},{7,8},{8,9},{9,10},{10,1... | collective-permute-start | bytes 196616 | tf_op jit(solution)/shard_map/ppermute | solution.py:605
  7.6 12.2 %collective-permute-start.1 = (f32[8,16,128]{2,1,0:T(8,128)S(1)}, f32[8,16,128]{2,1,0:T(8,128)S(1)}, u32[]{:S(2)}, u32[]{:S(2)}) collective-permute-start(f32[8,16,128]{2,1,0:T(8,128)S(1)} %get-tuple-element.9.left_ref), channel_id=1, source_target_pairs={{0,31},{1,0},{2,1},{3,2},{4,3},{5,4},{6,5},{7,6},{8,7},{9,8},{10,9... | collective-permute-start | bytes 196616 | tf_op jit(solution)/shard_map/ppermute | solution.py:606

commit v6 on v5

--- a/solution.py
+++ b/solution.py
@@ -29,7 +29,7 @@
 PRESSURE, EAST, NORTH, WIND, SURFACE, BOTTOM = 0, 8, 16, 24, 26, 27
 PLANES = 28
 OWN_EAST, OWN_NORTH, OWN_SURFACE, OWN_WIND, OWN_BOTTOM, OWN = 32, 40, 48, 49, 51, 52
-MAIL_N, MAIL_S, EDGE, CHUNK = SLAB, SLAB + 8, SLAB + 16, SLAB + 24
+MAIL_N, MAIL_S, CHUNK = SLAB, SLAB + 8, SLAB + 16
 BACK = 24
 
 
@@ -185,9 +185,23 @@
     turned_ref[:HALO] = beyond[COLS - HALO :]
     turned_ref[HALO + COLS :] = beyond[:HALO]
     edge = edge_ref[32:40]
+    sub = ids((8, COLS), 0)
+    tile_lane = ids((8, COLS), 1)
+    spare_block = tile_lane // 8 == lax.rem(6 + place, 16)
     for d in range(MEMBERS):
-        out_ref[d, :SLAB] = turned_ref[8 * d : 8 * d + SLAB]
-        out_ref[d, EDGE:CHUNK] = at(edge, 8 * d - HALO, 1)[:, :COLS]
+        moved = at(edge, 8 * d - HALO + 4, 1)[:, :COLS]
+        pairs = jnp.where(tile_lane < 64, moved, at(at(moved, 64, 1), 1, 0))
+        rest = jnp.where(tile_lane % 8 == sub, moved[:, 64:65], 0.0)
+        for step in (1, 2, 4):
+            rest = rest + at(rest, step, 0)
+        out_ref[d, :8] = jnp.where(
+            sub == 0, pairs, jnp.where(sub == 1, at(pairs, 1, 0), turned_ref[8 * d : 8 * d + 8])
+        )
+        out_ref[d, 8 : SLAB - 8] = turned_ref[8 * d + 8 : 8 * d + SLAB - 8]
+        end = turned_ref[8 * d + SLAB - 8 : 8 * d + SLAB]
+        end = jnp.where((sub == 5) & spare_block, rest, end)
+        end = jnp.where(sub == 6, at(pairs, -2, 0), end)
+        out_ref[d, SLAB - 8 : SLAB] = jnp.where(sub == 7, at(pairs, -1, 0), end)
 
     block = ids((ROWS, COLS), 1) // 4
     flows = [(us[k], jnp.where(count_u > k, tracer_diffusion, 0.0)) for k in range(LEVELS)]
@@ -212,7 +226,6 @@
         rows = slice(ROWS * n, ROWS * (n + 1))
         along_ref[rows] = inner_ref[rows] + at(both, 4 * n, 1)
 
-    sub = ids((8, COLS), 0)
 
     def spare(n):
         t, k = divmod(n, LEVELS)
@@ -239,7 +252,7 @@
 
     for m in range(MEMBERS):
         out_ref[m, MAIL_N:MAIL_S] = jnp.where(sub >= 4, tops(2 * m), at(tops(2 * m + 1), 4, 0))
-        out_ref[m, MAIL_S:EDGE] = jnp.where(sub < 4, bottoms(2 * m), at(bottoms(2 * m + 1), 4, 0))
+        out_ref[m, MAIL_S:CHUNK] = jnp.where(sub < 4, bottoms(2 * m), at(bottoms(2 * m + 1), 4, 0))
 
 
 def slab_kernel(in_ref, out_ref, edge_ref):
@@ -259,9 +272,18 @@
     surface, start_u, start_v, force_u, force_v, bottom = (blocks[2 * n : 2 * n + 2] for n in range(6))
     u_a, v_raw, near, u_next = blocks[12:]
     zeros = jnp.zeros((8, COLS), f32)
-    for a in range(MEMBERS):
-        edge_ref[8 * a : 8 * a + 8] = in_ref[a + 1, EDGE:CHUNK] if a < MEMBERS - 1 else zeros
-    far = edge_ref[...].T[:SLAB]
+    sub = ids((8, COLS), 0)
+    edge_ref[COLS - 8 :] = zeros
+    for a in range(1, MEMBERS):
+        begin, end = in_ref[a, :8], in_ref[a, SLAB - 8 : SLAB]
+        rows = jnp.where(sub < 2, begin, at(begin, -1, 0))
+        rows = jnp.where(sub < 4, rows, jnp.where(sub < 6, at(end, 2, 0), at(end, 1, 0)))
+        edge_ref[8 * a - 8 : 8 * a] = jnp.where(sub % 2 == 0, rows, at(at(rows, 64, 1), -1, 0))
+    column = ids(shape, 0)
+    far = at(edge_ref[...].T[:SLAB], -4, 0)
+    far = jnp.where(column == 68, at(at(force_u[0], 1, 0), 8, 1), far)
+    unused = (column < 2) | (column >= SLAB - 2)
+    bottom = [jnp.where(unused, float(LEVELS), b) for b in bottom]
 
     top = lane == COLS - 1
     count_u = [jnp.minimum(b, at(b, 1, 0)) for b in bottom]
@@ -402,7 +424,7 @@
             packed = jnp.where(block == (e + n) % 16, moved[n], packed)
         out_ref[e, 0:8] = packed
         out_ref[e, 8:16] = in_ref[(e + 15) % MEMBERS, MAIL_N:MAIL_S]
-        out_ref[e, 16:24] = in_ref[(e + 1) % MEMBERS, MAIL_S:EDGE]
+        out_ref[e, 16:24] = in_ref[(e + 1) % MEMBERS, MAIL_S:CHUNK]
 
 
 def gain(values, axis, flow, diffusion):

time: 54.8 us -> 55 us (level)
  Pallas kernels: 6.94 us -> 7.96 us
  blocking collectives: 28.5 us -> 27.7 us
    pallas_call x1, Pallas kernels: 1.22 us -> 2.31 us  [shards(): pl.pallas_call(send_kernel, out_shape=(struct(MEMBERS, CHUNK, COLS), stru...]
where the time goes in v6:
time: 55 us; the launch traced here: 54.7 us
  blocking collectives  27.7 us (50%)
  starting transfers between devices  16.5 us (30%)
  Pallas kernels  7.96 us (14%)
  other arithmetic  1.09 us (2%)
  waiting for transfers between devices  0.79 us (1%)
  between operations  0.7 us (1%)
    all_to_all x1, blocking collectives, shards(): slabs = lax.all_to_all(chunks, 'lat', 0, 0, tiled=True)  18 us
    ppermute x1, starting transfers between devices, shards(): east = lax.ppermute(to_left, 'lon', ring('lon', -1))  10.9 us
    all_to_all x1, blocking collectives, shards(): home = lax.all_to_all(answers, 'lat', 0, 0, tiled=True)  9.68 us
    ppermute x1, starting transfers between devices, shards(): west = lax.ppermute(to_right, 'lon', ring('lon', 1))  5.65 us
    pallas_call x1, Pallas kernels, shards(): pl.pallas_call(slab_kernel, out_shape=struct(MEMBERS, BACK, COLS), in_spe...  3.6 us
    pallas_call x1, Pallas kernels, shards(): pl.pallas_call(send_kernel, out_shape=(struct(MEMBERS, CHUNK, COLS), stru...  2.31 us
    pallas_call x1, Pallas kernels, shards(): pl.pallas_call(finish_kernel, out_shape=(struct(TRACERS, LEVELS, ROWS, CO...  1.37 us
  transfers between devices with their start and end apart: 2, of which 1 were waited for; matrix products, arithmetic and copies ran while one was open for 0% of the time, Pallas kernels for 1%

profile of v6, /device:TPU:1, one launch (start us, length us, event | category | flops | bytes accessed | tf_op | source)
XLA Modules:
  0.0 54.7 jit_solution(12227624339948542589)
XLA Ops:
  0.6 1.1 %convert_add_fusion.own_ref = f32[52,16,128]{2,1,0:T(8,128)S(1)} fusion(s32[1,16,128]{2,1,0:T(8,128)} %bitcast.7, f32[2,16,128]{2,1,0:T(8,128)} %param.8, f32[1,16,128]{2,1,0:T(8,128)} %bitcast.8, f32[16,16,128]{2,1,0:T(8,128)} %bitcast.6, f32[32,16,128]{2,1,0:T(8,128)} %bitcast.5), kind=kLoop, calls=%fused_computation | loop fusion | flops 532480 | bytes 851968 | tf_op jit(solution)/shard_map/add | solution.py:607
  1.7 0.2 pack.1
  1.9 5.7 %collective-permute-start = (f32[8,16,128]{2,1,0:T(8,128)S(1)}, f32[8,16,128]{2,1,0:T(8,128)S(1)}, u32[]{:S(2)}, u32[]{:S(2)}) collective-permute-start(f32[8,16,128]{2,1,0:T(8,128)S(1)} %get-tuple-element.8.right_ref), channel_id=1, source_target_pairs={{0,1},{1,2},{2,3},{3,4},{4,5},{5,6},{6,7},{7,8},{8,9},{9,10},{10,1... | collective-permute-start | bytes 196616 | tf_op jit(solution)/shard_map/ppermute | solution.py:627
  7.6 10.9 %collective-permute-start.1 = (f32[8,16,128]{2,1,0:T(8,128)S(1)}, f32[8,16,128]{2,1,0:T(8,128)S(1)}, u32[]{:S(2)}, u32[]{:S(2)}) collective-permute-start(f32[8,16,128]{2,1,0:T(8,128)S(1)} %get-tuple-element.9.left_ref), channel_id=1, source_target_pairs={{0,31},{1,0},{2,1},{3,2},{4,3},{5,4},{6,5},{7,6},{8,7},{9,8},{10,9... | collective-permute-start | bytes 196616 | tf_op jit(solution)/shard_map/ppermute | solution.py:628
  18.4 0.5 inner.1.inner_ref
  18.9 0.0 collective-permute-done.west_ref
  19.0 0.8 %collective-permute-done.1.east_ref = f32[8,16,128]{2,1,0:T(8,128)S(1)} collective-permute-done((f32[8,16,128]{2,1,0:T(8,128)S(1)}, f32[8,16,128]{2,1,0:T(8,128)S(1)}, u32[]{:S(2)}, u32[]{:S(2)}) %collective-permute-start.1) | collective-permute-done | bytes 65568 | tf_op jit(solution)/shard_map/ppermute | solution.py:628
  19.7 2.3 %columns.1 = (f32[16,88,128]{2,1,0:T(8,128)S(1)}, f32[512,128]{1,0:T(8,128)S(1)}) custom-call(s32[1]{0:T(128)} %bitcast.place_ref, f32[52,16,128]{2,1,0:T(8,128)S(1)} %convert_add_fusion.own_ref, f32[8,16,128]{2,1,0:T(8,128)S(1)} %collective-permute-done.west_ref, f32[8,16,128]{2,1,0:T(8,128)S(1)} %collective-permute-done.1.east_ref, ...), custom_call_target="tpu_custom_call" | custom-call | tf_op jit(solution)/shard_map/columns/pallas_call | solution.py:638
  22.1 18.0 %all_to_all.10.in_ref = f32[16,88,128]{2,1,0:T(8,128)S(1)} all-to-all(f32[16,88,128]{2,1,0:T(8,128)S(1)} %get-tuple-element.10), channel_id=1, replica_groups=mesh['lat'=16,'lon'=32] {'lat'}, dimensions={0} | all-to-all | bytes 1441792 | tf_op jit(solution)/shard_map/all_to_all | solution.py:655
  40.1 3.6 %substeps.1 = f32[16,24,128]{2,1,0:T(8,128)S(1)} custom-call(f32[16,88,128]{2,1,0:T(8,128)S(1)} %all_to_all.10.in_ref), custom_call_target="tpu_custom_call" | custom-call | tf_op jit(solution)/shard_map/substeps/pallas_call | solution.py:656
  43.7 9.7 %all_to_all.11.in_ref = f32[16,24,128]{2,1,0:T(8,128)S(1)} all-to-all(f32[16,24,128]{2,1,0:T(8,128)S(1)} %substeps.1), channel_id=1, replica_groups=mesh['lat'=16,'lon'=32] {'lat'}, dimensions={0} | all-to-all | bytes 393216 | tf_op jit(solution)/shard_map/all_to_all | solution.py:665
  53.4 1.4 %finish.1 = (f32[4,8,16,128]{3,2,1,0:T(8,128)}, f32[2,8,16,128]{3,2,1,0:T(8,128)}, f32[16,128]{1,0:T(8,128)}, f32[16,128]{1,0:T(8,128)}) custom-call(s32[1]{0:T(128)} %bitcast.place_ref, f32[16,24,128]{2,1,0:T(8,128)S(1)} %all_to_all.11.in_ref, f32[52,16,128]{2,1,0:T(8,128)S(1)} %convert_add_fusion.own_ref, f32[8,16,128]{2,1,0:T(8,128)S(1)} %collective-permute-done.west_ref, ...), custom_call_target="tpu_custom_call" | custom-call | tf_op jit(solution)/shard_map/finish/pallas_call | solution.py:666
Async XLA Ops:
  1.9 17.0 %collective-permute-start = (f32[8,16,128]{2,1,0:T(8,128)S(1)}, f32[8,16,128]{2,1,0:T(8,128)S(1)}, u32[]{:S(2)}, u32[]{:S(2)}) collective-permute-start(f32[8,16,128]{2,1,0:T(8,128)S(1)} %get-tuple-element.8.right_ref), channel_id=1, source_target_pairs={{0,1},{1,2},{2,3},{3,4},{4,5},{5,6},{6,7},{7,8},{8,9},{9,10},{10,1... | collective-permute-start | bytes 196616 | tf_op jit(solution)/shard_map/ppermute | solution.py:627
  7.6 12.2 %collective-permute-start.1 = (f32[8,16,128]{2,1,0:T(8,128)S(1)}, f32[8,16,128]{2,1,0:T(8,128)S(1)}, u32[]{:S(2)}, u32[]{:S(2)}) collective-permute-start(f32[8,16,128]{2,1,0:T(8,128)S(1)} %get-tuple-element.9.left_ref), channel_id=1, source_target_pairs={{0,31},{1,0},{2,1},{3,2},{4,3},{5,4},{6,5},{7,6},{8,7},{9,8},{10,9... | collective-permute-start | bytes 196616 | tf_op jit(solution)/shard_map/ppermute | solution.py:628

commit v7 on v6

--- a/solution.py
+++ b/solution.py
@@ -188,12 +188,14 @@
     sub = ids((8, COLS), 0)
     tile_lane = ids((8, COLS), 1)
     spare_block = tile_lane // 8 == lax.rem(6 + place, 16)
+    moved = [at(edge, 8 * d - HALO + 4, 1)[:, :COLS] for d in range(MEMBERS)]
+    halves = [at(x, 64, 1) for x in moved]
+    rests = [jnp.where(tile_lane % 8 == sub, x[:, 64:65], 0.0) for x in moved]
+    for step in (1, 2, 4):
+        rests = [x + at(x, step, 0) for x in rests]
     for d in range(MEMBERS):
-        moved = at(edge, 8 * d - HALO + 4, 1)[:, :COLS]
-        pairs = jnp.where(tile_lane < 64, moved, at(at(moved, 64, 1), 1, 0))
-        rest = jnp.where(tile_lane % 8 == sub, moved[:, 64:65], 0.0)
-        for step in (1, 2, 4):
-            rest = rest + at(rest, step, 0)
+        pairs = jnp.where(tile_lane < 64, moved[d], at(halves[d], 1, 0))
+        rest = rests[d]
         out_ref[d, :8] = jnp.where(
             sub == 0, pairs, jnp.where(sub == 1, at(pairs, 1, 0), turned_ref[8 * d : 8 * d + 8])
         )
@@ -221,10 +223,14 @@
         packed(0, 1, 1), packed(0, 0, 0), packed(0, 0, 1), packed(1, 1, 1), packed(1, 0, 1),
     )
     high = at(high, 4, 1)
-    for n in range(TRACERS * LEVELS):
-        both = jnp.where(block == n, low, jnp.where(block == (n + 31) % 32, high, 0.0))
+    planes = range(TRACERS * LEVELS)
+    sides = [
+        at(jnp.where(block == n, low, jnp.where(block == (n + 31) % 32, high, 0.0)), 4 * n, 1)
+        for n in planes
+    ]
+    for n in planes:
         rows = slice(ROWS * n, ROWS * (n + 1))
-        along_ref[rows] = inner_ref[rows] + at(both, 4 * n, 1)
+        along_ref[rows] = inner_ref[rows] + sides[n]
 
 
     def spare(n):

time: 55 us -> 54 us (0.982)
  Pallas kernels: 7.96 us -> 6.97 us
    pallas_call x1, Pallas kernels: 2.31 us -> 1.31 us  [shards(): pl.pallas_call(send_kernel, out_shape=(struct(MEMBERS, CHUNK, COLS), stru...]
where the time goes in v7:
time: 54 us; the launch traced here: 53.8 us
  blocking collectives  27.7 us (51%)
  starting transfers between devices  16.5 us (31%)
  Pallas kernels  6.97 us (13%)
  other arithmetic  1.09 us (2%)
  waiting for transfers between devices  0.79 us (1%)
  between operations  0.7 us (1%)
    all_to_all x1, blocking collectives, shards(): slabs = lax.all_to_all(chunks, 'lat', 0, 0, tiled=True)  18 us
    ppermute x1, starting transfers between devices, shards(): east = lax.ppermute(to_left, 'lon', ring('lon', -1))  10.9 us
    all_to_all x1, blocking collectives, shards(): home = lax.all_to_all(answers, 'lat', 0, 0, tiled=True)  9.68 us
    ppermute x1, starting transfers between devices, shards(): west = lax.ppermute(to_right, 'lon', ring('lon', 1))  5.65 us
    pallas_call x1, Pallas kernels, shards(): pl.pallas_call(slab_kernel, out_shape=struct(MEMBERS, BACK, COLS), in_spe...  3.6 us
    pallas_call x1, Pallas kernels, shards(): pl.pallas_call(finish_kernel, out_shape=(struct(TRACERS, LEVELS, ROWS, CO...  1.37 us
    pallas_call x1, Pallas kernels, shards(): pl.pallas_call(send_kernel, out_shape=(struct(MEMBERS, CHUNK, COLS), stru...  1.31 us
    add x1, other arithmetic, stacked(): put(tracers, 0) + put(velocity, OWN_EAST) + put(surface, OWN_SURFACE)  1.09 us
  transfers between devices with their start and end apart: 2, of which 1 were waited for; matrix products, arithmetic and copies ran while one was open for 0% of the time, Pallas kernels for 1%

profile of v7, /device:TPU:1, one launch (start us, length us, event | category | flops | bytes accessed | tf_op | source)
XLA Modules:
  0.0 53.8 jit_solution(3091674608664997812)
XLA Ops:
  0.6 1.1 %convert_add_fusion.own_ref = f32[52,16,128]{2,1,0:T(8,128)S(1)} fusion(s32[1,16,128]{2,1,0:T(8,128)} %bitcast.7, f32[2,16,128]{2,1,0:T(8,128)} %param.8, f32[1,16,128]{2,1,0:T(8,128)} %bitcast.8, f32[16,16,128]{2,1,0:T(8,128)} %bitcast.6, f32[32,16,128]{2,1,0:T(8,128)} %bitcast.5), kind=kLoop, calls=%fused_computation | loop fusion | flops 532480 | bytes 851968 | tf_op jit(solution)/shard_map/add | solution.py:613
  1.7 0.2 pack.1
  1.9 5.7 %collective-permute-start = (f32[8,16,128]{2,1,0:T(8,128)S(1)}, f32[8,16,128]{2,1,0:T(8,128)S(1)}, u32[]{:S(2)}, u32[]{:S(2)}) collective-permute-start(f32[8,16,128]{2,1,0:T(8,128)S(1)} %get-tuple-element.8.right_ref), channel_id=1, source_target_pairs={{0,1},{1,2},{2,3},{3,4},{4,5},{5,6},{6,7},{7,8},{8,9},{9,10},{10,1... | collective-permute-start | bytes 196616 | tf_op jit(solution)/shard_map/ppermute | solution.py:633
  7.6 10.9 %collective-permute-start.1 = (f32[8,16,128]{2,1,0:T(8,128)S(1)}, f32[8,16,128]{2,1,0:T(8,128)S(1)}, u32[]{:S(2)}, u32[]{:S(2)}) collective-permute-start(f32[8,16,128]{2,1,0:T(8,128)S(1)} %get-tuple-element.9.left_ref), channel_id=1, source_target_pairs={{0,31},{1,0},{2,1},{3,2},{4,3},{5,4},{6,5},{7,6},{8,7},{9,8},{10,9... | collective-permute-start | bytes 196616 | tf_op jit(solution)/shard_map/ppermute | solution.py:634
  18.4 0.5 inner.1.inner_ref
  18.9 0.0 collective-permute-done.west_ref
  19.0 0.8 %collective-permute-done.1.east_ref = f32[8,16,128]{2,1,0:T(8,128)S(1)} collective-permute-done((f32[8,16,128]{2,1,0:T(8,128)S(1)}, f32[8,16,128]{2,1,0:T(8,128)S(1)}, u32[]{:S(2)}, u32[]{:S(2)}) %collective-permute-start.1) | collective-permute-done | bytes 65568 | tf_op jit(solution)/shard_map/ppermute | solution.py:634
  19.7 1.3 %columns.1 = (f32[16,88,128]{2,1,0:T(8,128)S(1)}, f32[512,128]{1,0:T(8,128)S(1)}) custom-call(s32[1]{0:T(128)} %bitcast.place_ref, f32[52,16,128]{2,1,0:T(8,128)S(1)} %convert_add_fusion.own_ref, f32[8,16,128]{2,1,0:T(8,128)S(1)} %collective-permute-done.west_ref, f32[8,16,128]{2,1,0:T(8,128)S(1)} %collective-permute-done.1.east_ref, ...), custom_call_target="tpu_custom_call" | custom-call | tf_op jit(solution)/shard_map/columns/pallas_call | solution.py:644
  21.1 18.0 %all_to_all.10.in_ref = f32[16,88,128]{2,1,0:T(8,128)S(1)} all-to-all(f32[16,88,128]{2,1,0:T(8,128)S(1)} %get-tuple-element.10), channel_id=1, replica_groups=mesh['lat'=16,'lon'=32] {'lat'}, dimensions={0} | all-to-all | bytes 1441792 | tf_op jit(solution)/shard_map/all_to_all | solution.py:661
  39.1 3.6 %substeps.1 = f32[16,24,128]{2,1,0:T(8,128)S(1)} custom-call(f32[16,88,128]{2,1,0:T(8,128)S(1)} %all_to_all.10.in_ref), custom_call_target="tpu_custom_call" | custom-call | tf_op jit(solution)/shard_map/substeps/pallas_call | solution.py:662
  42.7 9.7 %all_to_all.11.in_ref = f32[16,24,128]{2,1,0:T(8,128)S(1)} all-to-all(f32[16,24,128]{2,1,0:T(8,128)S(1)} %substeps.1), channel_id=1, replica_groups=mesh['lat'=16,'lon'=32] {'lat'}, dimensions={0} | all-to-all | bytes 393216 | tf_op jit(solution)/shard_map/all_to_all | solution.py:671
  52.4 1.4 %finish.1 = (f32[4,8,16,128]{3,2,1,0:T(8,128)}, f32[2,8,16,128]{3,2,1,0:T(8,128)}, f32[16,128]{1,0:T(8,128)}, f32[16,128]{1,0:T(8,128)}) custom-call(s32[1]{0:T(128)} %bitcast.place_ref, f32[16,24,128]{2,1,0:T(8,128)S(1)} %all_to_all.11.in_ref, f32[52,16,128]{2,1,0:T(8,128)S(1)} %convert_add_fusion.own_ref, f32[8,16,128]{2,1,0:T(8,128)S(1)} %collective-permute-done.west_ref, ...), custom_call_target="tpu_custom_call" | custom-call | tf_op jit(solution)/shard_map/finish/pallas_call | solution.py:672
Async XLA Ops:
  1.9 17.0 %collective-permute-start = (f32[8,16,128]{2,1,0:T(8,128)S(1)}, f32[8,16,128]{2,1,0:T(8,128)S(1)}, u32[]{:S(2)}, u32[]{:S(2)}) collective-permute-start(f32[8,16,128]{2,1,0:T(8,128)S(1)} %get-tuple-element.8.right_ref), channel_id=1, source_target_pairs={{0,1},{1,2},{2,3},{3,4},{4,5},{5,6},{6,7},{7,8},{8,9},{9,10},{10,1... | collective-permute-start | bytes 196616 | tf_op jit(solution)/shard_map/ppermute | solution.py:633
  7.6 12.2 %collective-permute-start.1 = (f32[8,16,128]{2,1,0:T(8,128)S(1)}, f32[8,16,128]{2,1,0:T(8,128)S(1)}, u32[]{:S(2)}, u32[]{:S(2)}) collective-permute-start(f32[8,16,128]{2,1,0:T(8,128)S(1)} %get-tuple-element.9.left_ref), channel_id=1, source_target_pairs={{0,31},{1,0},{2,1},{3,2},{4,3},{5,4},{6,5},{7,6},{8,7},{9,8},{10,9... | collective-permute-start | bytes 196616 | tf_op jit(solution)/shard_map/ppermute | solution.py:634

commit v8 on v7

--- a/solution.py
+++ b/solution.py
@@ -120,8 +120,8 @@
 
 
 def send_kernel(
-    place_ref, own_ref, west_ref, east_ref, right_ref, left_ref, inner_ref,
-    out_ref, along_ref, split_ref, stack_ref, edge_ref, turned_ref,
+    place_ref, own_ref, west_ref, east_ref, _,
+    out_ref, flows_ref, split_ref, stack_ref, edge_ref, turned_ref,
 ):
     place = place_ref[0]
     c = tracer_planes(own_ref)
@@ -205,32 +205,8 @@
         end = jnp.where(sub == 6, at(pairs, -2, 0), end)
         out_ref[d, SLAB - 8 : SLAB] = jnp.where(sub == 7, at(pairs, -1, 0), end)
 
-    block = ids((ROWS, COLS), 1) // 4
-    flows = [(us[k], jnp.where(count_u > k, tracer_diffusion, 0.0)) for k in range(LEVELS)]
-
-    def packed(which, half, ahead):
-        tile = jnp.zeros((ROWS, COLS), f32)
-        for k in range(LEVELS):
-            values = flows[k][which][:, COLS * half : COLS * (half + 1)]
-            tile = jnp.where(block % LEVELS == k, at(values, -4 * (k + ahead), 1), tile)
-        for step in (32, 64):
-            tile = jnp.where(block * 4 % (2 * step) < step, tile, at(tile, -step, 1))
-        return tile
-
-    last = PLANES // 4
-    low, high = outer(
-        at(west_ref[last], -4, 1), east_ref[last], left_ref[last], at(right_ref[last], -4, 1),
-        packed(0, 1, 1), packed(0, 0, 0), packed(0, 0, 1), packed(1, 1, 1), packed(1, 0, 1),
-    )
-    high = at(high, 4, 1)
-    planes = range(TRACERS * LEVELS)
-    sides = [
-        at(jnp.where(block == n, low, jnp.where(block == (n + 31) % 32, high, 0.0)), 4 * n, 1)
-        for n in planes
-    ]
-    for n in planes:
-        rows = slice(ROWS * n, ROWS * (n + 1))
-        along_ref[rows] = inner_ref[rows] + sides[n]
+    for n, values in enumerate((*us, count_u)):
+        flows_ref[ROWS * n : ROWS * (n + 1)] = values
 
 
     def spare(n):
@@ -261,7 +237,55 @@
         out_ref[m, MAIL_S:CHUNK] = jnp.where(sub < 4, bottoms(2 * m), at(bottoms(2 * m + 1), 4, 0))
 
 
-def slab_kernel(in_ref, out_ref, edge_ref):
+def edge_steps(flows_ref, west_ref, east_ref, right_ref, left_ref, inner_ref, along_ref):
+    block = ids((ROWS, COLS), 1) // 4
+    count = flows_ref[ROWS * LEVELS :]
+
+    def packed(of_level, half, ahead):
+        tile = jnp.zeros((ROWS, COLS), f32)
+        for k in range(LEVELS):
+            values = of_level(k)[:, COLS * half : COLS * (half + 1)]
+            tile = jnp.where(block % LEVELS == k, at(values, -4 * (k + ahead), 1), tile)
+        return tile
+
+    def repeated(tile):
+        for step in (32, 64):
+            tile = jnp.where(block * 4 % (2 * step) < step, tile, at(tile, -step, 1))
+        return tile
+
+    def flow(k):
+        return flows_ref[ROWS * k : ROWS * (k + 1)]
+
+    def diffusion(k):
+        return jnp.where(count > k, tracer_diffusion, 0.0)
+
+    tiles = []
+    for what in ((flow, 1, 1), (flow, 0, 0), (flow, 0, 1), (diffusion, 1, 1), (diffusion, 0, 1)):
+        tiles.append(packed(*what))
+        yield
+    tiles = [repeated(tile) for tile in tiles]
+    yield
+    last = PLANES // 4
+    low, high = outer(
+        at(west_ref[last], -4, 1), east_ref[last], left_ref[last], at(right_ref[last], -4, 1),
+        *tiles,
+    )
+    high = at(high, 4, 1)
+    yield
+    waiting = []
+    for n in range(TRACERS * LEVELS):
+        both = jnp.where(block == n, low, jnp.where(block == (n + 31) % 32, high, 0.0))
+        waiting.append((slice(ROWS * n, ROWS * (n + 1)), at(both, 4 * n, 1)))
+        if n % 2:
+            yield
+    for rows, side in waiting:
+        along_ref[rows] = inner_ref[rows] + side
+
+
+def slab_kernel(
+    in_ref, flows_ref, west_ref, east_ref, right_ref, left_ref, inner_ref,
+    out_ref, along_ref, edge_ref,
+):
     shape = (SLAB, COLS)
     lane = ids(shape, 1)
     r = lane % 8
@@ -298,22 +322,19 @@
         jnp.where(top, 0.0, jnp.minimum(bottom[1], at(bottom[0], 1, 1))),
     ]
 
-    ahead = jnp.concatenate([count_u[0], count_v[0]], axis=0)
-    first = (ids(ahead.shape, 1) % 8 == 0) & (ids(ahead.shape, 1) > 0)
-    counts = jnp.concatenate(
-        [
-            jnp.where(r == 7, count_u[1], 0.0),
-            jnp.where(r == 7, count_v[1], 0.0),
-            jnp.where(r == 7, count_v[0], 0.0),
-            at(jnp.where(first, ahead, 0.0), 1, 1),
-        ],
-        axis=0,
-    )
-    for step in (1, 2, 4):
-        counts = counts + at(counts, step, 1)
-    count_ua, count_va, count_vc, count_ub, count_vb = (
-        counts[SLAB * n : SLAB * (n + 1)] for n in range(5)
-    )
+    square = (COLS, COLS)
+
+    def spread_from(lane_at, values):
+        chosen = ids(square, 0) == ids(square, 1) // 8 * 8 + lane_at
+        spread = jnp.dot(
+            jnp.concatenate(values, axis=0).astype(jnp.bfloat16),
+            chosen.astype(f32).astype(jnp.bfloat16),
+            preferred_element_type=f32,
+        )
+        return [spread[SLAB * n : SLAB * (n + 1)] for n in range(len(values))]
+
+    count_ua, count_va, count_vc = spread_from(7, [count_u[1], count_v[1], count_v[0]])
+    count_ub, count_vb = spread_from(8, [count_u[0], count_v[0]])
     level = r.astype(f32)
     last = lane >= COLS - 8
     v_a = jnp.where(count_va > level, v_raw, 0.0)
@@ -376,6 +397,7 @@
     )
     state = (*surface, at(surface[0], 1, 1), *begin_u, *begin_v)
     total = (zeros,) * 4
+    beside = edge_steps(flows_ref, west_ref, east_ref, right_ref, left_ref, inner_ref, along_ref)
     for low, steps in ((0, 6), (8, 8), (16, 8), (24, 8)):
         cut = 8 if low else 0
         state = tuple(x[cut : x.shape[0] - cut] for x in state)
@@ -404,16 +426,19 @@
             sums = [a + b[centre : centre + 8] for a, b in zip(sums, (u0, u1, v0, v1))]
             return (h0, h1, h2, u0, u1, v0, v1, *sums)
 
-        *state, a0, a1, a2, a3 = lax.fori_loop(
-            0, steps, advance, (*state, *total), unroll=True
-        )
-        total = (a0, a1, a2, a3)
+        carry = (*state, *total)
+        for step in range(steps):
+            carry = advance(step, carry)
+            if low:
+                next(beside, None)
+        state, total = carry[:7], carry[7:]
+    for _ in beside:
+        pass
     height = [x[8:16] for x in state[:2]]
     average = [x * (1.0 / SUBSTEPS) for x in total]
     transport = [
         (-thickness * count_u[i][HALO : HALO + 8]) * average[i] for i in range(2)
     ]
-    square = (COLS, COLS)
     before = (ids(square, 0) < ids(square, 1)).astype(f32)
     south = jnp.dot(
         transport[0] + transport[1],
@@ -641,13 +666,13 @@
         cost_estimate=pl.CostEstimate(flops=1500000, bytes_accessed=3000000, transcendentals=0),
         name="inner",
     )(own)
-    chunks, along = pl.pallas_call(
+    chunks, flows = pl.pallas_call(
         send_kernel,
         out_shape=(
             struct(MEMBERS, CHUNK, COLS),
-            struct(TRACERS * LEVELS * ROWS, COLS),
+            struct((LEVELS + 1) * ROWS, 2 * COLS),
         ),
-        in_specs=specs(6, 1),
+        in_specs=specs(3, 1) + [pl.BlockSpec(memory_space=pl.ANY)],
         out_specs=tuple(specs(2)),
         scratch_shapes=[
             vmem(12 * ROWS, COLS),
@@ -657,17 +682,20 @@
         ],
         compiler_params=PARAMS,
         name="columns",
-    )(place, own, west, east, to_right, to_left, inner)
+    )(place, own, west, east, inner)
     slabs = lax.all_to_all(chunks, "lat", 0, 0, tiled=True)
-    answers = pl.pallas_call(
+    answers, along = pl.pallas_call(
         slab_kernel,
-        out_shape=struct(MEMBERS, BACK, COLS),
-        in_specs=specs(1),
-        out_specs=specs(1)[0],
+        out_shape=(
+            struct(MEMBERS, BACK, COLS),
+            struct(TRACERS * LEVELS * ROWS, COLS),
+        ),
+        in_specs=specs(7),
+        out_specs=tuple(specs(2)),
         scratch_shapes=[vmem(COLS, COLS)],
         compiler_params=PARAMS,
         name="substeps",
-    )(slabs)
+    )(slabs, flows, west, east, to_right, to_left, inner)
     home = lax.all_to_all(answers, "lat", 0, 0, tiled=True)
     return pl.pallas_call(
         finish_kernel,

time: 54 us -> 53.7 us (level)
  no operation moved by 1% of the time
where the time goes in v8:
time: 53.7 us; the launch traced here: 53.4 us
  blocking collectives  27.7 us (52%)
  starting transfers between devices  16.5 us (31%)
  Pallas kernels  6.66 us (12%)
  other arithmetic  1.09 us (2%)
  waiting for transfers between devices  0.79 us (1%)
  between operations  0.69 us (1%)
    all_to_all x1, blocking collectives, shards(): slabs = lax.all_to_all(chunks, 'lat', 0, 0, tiled=True)  18 us
    ppermute x1, starting transfers between devices, shards(): east = lax.ppermute(to_left, 'lon', ring('lon', -1))  10.9 us
    all_to_all x1, blocking collectives, shards(): home = lax.all_to_all(answers, 'lat', 0, 0, tiled=True)  9.68 us
    ppermute x1, starting transfers between devices, shards(): west = lax.ppermute(to_right, 'lon', ring('lon', 1))  5.65 us
    pallas_call x1, Pallas kernels, shards(): pl.pallas_call(slab_kernel, out_shape=(struct(MEMBERS, BACK, COLS), struc...  3.73 us
    pallas_call x1, Pallas kernels, shards(): pl.pallas_call(finish_kernel, out_shape=(struct(TRACERS, LEVELS, ROWS, CO...  1.37 us
    add x1, other arithmetic, stacked(): put(tracers, 0) + put(velocity, OWN_EAST) + put(surface, OWN_SURFACE)  1.09 us
  transfers between devices with their start and end apart: 2, of which 1 were waited for; matrix products, arithmetic and copies ran while one was open for 0% of the time, Pallas kernels for 1%

profile of v8, /device:TPU:1, one launch (start us, length us, event | category | flops | bytes accessed | tf_op | source)
XLA Modules:
  0.0 53.4 jit_solution(2070893602673239417)
XLA Ops:
  0.6 1.1 %convert_add_fusion.own_ref = f32[52,16,128]{2,1,0:T(8,128)S(1)} fusion(s32[1,16,128]{2,1,0:T(8,128)} %bitcast.7, f32[2,16,128]{2,1,0:T(8,128)} %param.8, f32[1,16,128]{2,1,0:T(8,128)} %bitcast.8, f32[16,16,128]{2,1,0:T(8,128)} %bitcast.6, f32[32,16,128]{2,1,0:T(8,128)} %bitcast.5), kind=kLoop, calls=%fused_computation | loop fusion | flops 532480 | bytes 851968 | tf_op jit(solution)/shard_map/add | solution.py:638
  1.7 0.2 pack.1
  1.9 5.7 %collective-permute-start = (f32[8,16,128]{2,1,0:T(8,128)S(1)}, f32[8,16,128]{2,1,0:T(8,128)S(1)}, u32[]{:S(2)}, u32[]{:S(2)}) collective-permute-start(f32[8,16,128]{2,1,0:T(8,128)S(1)} %get-tuple-element.10.right_ref), channel_id=1, source_target_pairs={{0,1},{1,2},{2,3},{3,4},{4,5},{5,6},{6,7},{7,8},{8,9},{9,10},{10,1... | collective-permute-start | bytes 196616 | tf_op jit(solution)/shard_map/ppermute | solution.py:658
  7.6 10.9 %collective-permute-start.1 = (f32[8,16,128]{2,1,0:T(8,128)S(1)}, f32[8,16,128]{2,1,0:T(8,128)S(1)}, u32[]{:S(2)}, u32[]{:S(2)}) collective-permute-start(f32[8,16,128]{2,1,0:T(8,128)S(1)} %get-tuple-element.11.left_ref), channel_id=1, source_target_pairs={{0,31},{1,0},{2,1},{3,2},{4,3},{5,4},{6,5},{7,6},{8,7},{9,8},{10,9... | collective-permute-start | bytes 196616 | tf_op jit(solution)/shard_map/ppermute | solution.py:659
  18.4 0.5 inner.1._.inner_ref
  18.9 0.0 collective-permute-done.west_ref
  19.0 0.8 %collective-permute-done.1.east_ref = f32[8,16,128]{2,1,0:T(8,128)S(1)} collective-permute-done((f32[8,16,128]{2,1,0:T(8,128)S(1)}, f32[8,16,128]{2,1,0:T(8,128)S(1)}, u32[]{:S(2)}, u32[]{:S(2)}) %collective-permute-start.1) | collective-permute-done | bytes 65568 | tf_op jit(solution)/shard_map/ppermute | solution.py:659
  19.7 0.9 %columns.1 = (f32[16,88,128]{2,1,0:T(8,128)S(1)}, f32[144,256]{1,0:T(8,128)S(1)}) custom-call(s32[1]{0:T(128)} %bitcast.place_ref, f32[52,16,128]{2,1,0:T(8,128)S(1)} %convert_add_fusion.own_ref, f32[8,16,128]{2,1,0:T(8,128)S(1)} %collective-permute-done.west_ref, f32[8,16,128]{2,1,0:T(8,128)S(1)} %collective-permute-done.1.east_ref, ...), custom_call_target="tpu_custom_call" | custom-call | tf_op jit(solution)/shard_map/columns/pallas_call | solution.py:669
  20.6 18.0 %all_to_all.10.in_ref = f32[16,88,128]{2,1,0:T(8,128)S(1)} all-to-all(f32[16,88,128]{2,1,0:T(8,128)S(1)} %get-tuple-element.12), channel_id=1, replica_groups=mesh['lat'=16,'lon'=32] {'lat'}, dimensions={0} | all-to-all | bytes 1441792 | tf_op jit(solution)/shard_map/all_to_all | solution.py:686
  38.7 3.7 %substeps.1 = (f32[16,24,128]{2,1,0:T(8,128)S(1)}, f32[512,128]{1,0:T(8,128)S(1)}) custom-call(f32[16,88,128]{2,1,0:T(8,128)S(1)} %all_to_all.10.in_ref, f32[144,256]{1,0:T(8,128)S(1)} %get-tuple-element.13.flows_ref, f32[8,16,128]{2,1,0:T(8,128)S(1)} %collective-permute-done.west_ref, f32[8,16,128]{2,1,0:T(8,128)S(1)} %collective-permute-done.1.east_ref, ...), custom_call_target="tpu_custom_call" | custom-call | tf_op jit(solution)/shard_map/substeps/pallas_call | solution.py:687
  42.4 9.7 %all_to_all.11.in_ref = f32[16,24,128]{2,1,0:T(8,128)S(1)} all-to-all(f32[16,24,128]{2,1,0:T(8,128)S(1)} %get-tuple-element.14), channel_id=1, replica_groups=mesh['lat'=16,'lon'=32] {'lat'}, dimensions={0} | all-to-all | bytes 393216 | tf_op jit(solution)/shard_map/all_to_all | solution.py:699
  52.1 1.4 %finish.1 = (f32[4,8,16,128]{3,2,1,0:T(8,128)}, f32[2,8,16,128]{3,2,1,0:T(8,128)}, f32[16,128]{1,0:T(8,128)}, f32[16,128]{1,0:T(8,128)}) custom-call(s32[1]{0:T(128)} %bitcast.place_ref, f32[16,24,128]{2,1,0:T(8,128)S(1)} %all_to_all.11.in_ref, f32[52,16,128]{2,1,0:T(8,128)S(1)} %convert_add_fusion.own_ref, f32[8,16,128]{2,1,0:T(8,128)S(1)} %collective-permute-done.west_ref, ...), custom_call_target="tpu_custom_call" | custom-call | tf_op jit(solution)/shard_map/finish/pallas_call | solution.py:700
Async XLA Ops:
  1.9 17.0 %collective-permute-start = (f32[8,16,128]{2,1,0:T(8,128)S(1)}, f32[8,16,128]{2,1,0:T(8,128)S(1)}, u32[]{:S(2)}, u32[]{:S(2)}) collective-permute-start(f32[8,16,128]{2,1,0:T(8,128)S(1)} %get-tuple-element.10.right_ref), channel_id=1, source_target_pairs={{0,1},{1,2},{2,3},{3,4},{4,5},{5,6},{6,7},{7,8},{8,9},{9,10},{10,1... | collective-permute-start | bytes 196616 | tf_op jit(solution)/shard_map/ppermute | solution.py:658
  7.6 12.2 %collective-permute-start.1 = (f32[8,16,128]{2,1,0:T(8,128)S(1)}, f32[8,16,128]{2,1,0:T(8,128)S(1)}, u32[]{:S(2)}, u32[]{:S(2)}) collective-permute-start(f32[8,16,128]{2,1,0:T(8,128)S(1)} %get-tuple-element.11.left_ref), channel_id=1, source_target_pairs={{0,31},{1,0},{2,1},{3,2},{4,3},{5,4},{6,5},{7,6},{8,7},{9,8},{10,9... | collective-permute-start | bytes 196616 | tf_op jit(solution)/shard_map/ppermute | solution.py:659

commit v9 on v8

--- a/solution.py
+++ b/solution.py
@@ -439,16 +439,29 @@
     transport = [
         (-thickness * count_u[i][HALO : HALO + 8]) * average[i] for i in range(2)
     ]
-    before = (ids(square, 0) < ids(square, 1)).astype(f32)
-    south = jnp.dot(
-        transport[0] + transport[1],
+    before = jnp.concatenate(
+        [
+            (ids(square, 0) < (ids(square, 1) - 8 * n) % COLS).astype(f32).astype(jnp.bfloat16)
+            for n in (2, 3)
+        ],
+        axis=1,
+    )
+    rest = jnp.concatenate([transport[0] + transport[1], zeros], axis=0)
+    parts = []
+    for _ in range(3):
+        parts.append(rest.astype(jnp.bfloat16).astype(f32))
+        rest = rest - parts[-1]
+    sums = jnp.dot(
+        jnp.concatenate(parts, axis=0).astype(jnp.bfloat16),
         before,
-        precision=lax.Precision.HIGHEST,
         preferred_element_type=f32,
     )
-    stream = [south + transport[0], south + (transport[0] + transport[1])]
+    south = (sums[32:40] + sums[16:24]) + sums[:8]
+    stream = [transport[0], transport[0] + transport[1]]
     results = [*height, *stream, *average]
     moved = [at(values, -8 * n, 1) for n, values in enumerate(results)]
+    moved[2] = south[:, :COLS] + moved[2]
+    moved[3] = south[:, COLS:] + moved[3]
     for e in range(MEMBERS):
         packed = moved[0]
         for n in range(1, 8):

time: 53.7 us -> 53.6 us (level)
  no operation moved by 1% of the time
where the time goes in v9:
time: 53.6 us; the launch traced here: 53.3 us
  blocking collectives  27.7 us (52%)
  starting transfers between devices  16.5 us (31%)
  Pallas kernels  6.53 us (12%)
  other arithmetic  1.09 us (2%)
  waiting for transfers between devices  0.79 us (1%)
  between operations  0.69 us (1%)
    all_to_all x1, blocking collectives, shards(): slabs = lax.all_to_all(chunks, 'lat', 0, 0, tiled=True)  18 us
    ppermute x1, starting transfers between devices, shards(): east = lax.ppermute(to_left, 'lon', ring('lon', -1))  10.9 us
    all_to_all x1, blocking collectives, shards(): home = lax.all_to_all(answers, 'lat', 0, 0, tiled=True)  9.68 us
    ppermute x1, starting transfers between devices, shards(): west = lax.ppermute(to_right, 'lon', ring('lon', 1))  5.65 us
    pallas_call x1, Pallas kernels, shards(): pl.pallas_call(slab_kernel, out_shape=(struct(MEMBERS, BACK, COLS), struc...  3.6 us
    pallas_call x1, Pallas kernels, shards(): pl.pallas_call(finish_kernel, out_shape=(struct(TRACERS, LEVELS, ROWS, CO...  1.37 us
    add x1, other arithmetic, stacked(): put(tracers, 0) + put(velocity, OWN_EAST) + put(surface, OWN_SURFACE)  1.09 us
  transfers between devices with their start and end apart: 2, of which 1 were waited for; matrix products, arithmetic and copies ran while one was open for 0% of the time, Pallas kernels for 1%

profile of v9, /device:TPU:1, one launch (start us, length us, event | category | flops | bytes accessed | tf_op | source)
XLA Modules:
  0.0 53.3 jit_solution(12453281938792261660)
XLA Ops:
  0.6 1.1 %convert_add_fusion.own_ref = f32[52,16,128]{2,1,0:T(8,128)S(1)} fusion(s32[1,16,128]{2,1,0:T(8,128)} %bitcast.7, f32[2,16,128]{2,1,0:T(8,128)} %param.8, f32[1,16,128]{2,1,0:T(8,128)} %bitcast.8, f32[16,16,128]{2,1,0:T(8,128)} %bitcast.6, f32[32,16,128]{2,1,0:T(8,128)} %bitcast.5), kind=kLoop, calls=%fused_computation | loop fusion | flops 532480 | bytes 851968 | tf_op jit(solution)/shard_map/add | solution.py:651
  1.7 0.2 pack.1
  1.9 5.7 %collective-permute-start = (f32[8,16,128]{2,1,0:T(8,128)S(1)}, f32[8,16,128]{2,1,0:T(8,128)S(1)}, u32[]{:S(2)}, u32[]{:S(2)}) collective-permute-start(f32[8,16,128]{2,1,0:T(8,128)S(1)} %get-tuple-element.10.right_ref), channel_id=1, source_target_pairs={{0,1},{1,2},{2,3},{3,4},{4,5},{5,6},{6,7},{7,8},{8,9},{9,10},{10,1... | collective-permute-start | bytes 196616 | tf_op jit(solution)/shard_map/ppermute | solution.py:671
  7.6 10.9 %collective-permute-start.1 = (f32[8,16,128]{2,1,0:T(8,128)S(1)}, f32[8,16,128]{2,1,0:T(8,128)S(1)}, u32[]{:S(2)}, u32[]{:S(2)}) collective-permute-start(f32[8,16,128]{2,1,0:T(8,128)S(1)} %get-tuple-element.11.left_ref), channel_id=1, source_target_pairs={{0,31},{1,0},{2,1},{3,2},{4,3},{5,4},{6,5},{7,6},{8,7},{9,8},{10,9... | collective-permute-start | bytes 196616 | tf_op jit(solution)/shard_map/ppermute | solution.py:672
  18.4 0.5 inner.1._.inner_ref
  18.9 0.0 collective-permute-done.west_ref
  19.0 0.8 %collective-permute-done.1.east_ref = f32[8,16,128]{2,1,0:T(8,128)S(1)} collective-permute-done((f32[8,16,128]{2,1,0:T(8,128)S(1)}, f32[8,16,128]{2,1,0:T(8,128)S(1)}, u32[]{:S(2)}, u32[]{:S(2)}) %collective-permute-start.1) | collective-permute-done | bytes 65568 | tf_op jit(solution)/shard_map/ppermute | solution.py:672
  19.7 0.9 %columns.1 = (f32[16,88,128]{2,1,0:T(8,128)S(1)}, f32[144,256]{1,0:T(8,128)S(1)}) custom-call(s32[1]{0:T(128)} %bitcast.place_ref, f32[52,16,128]{2,1,0:T(8,128)S(1)} %convert_add_fusion.own_ref, f32[8,16,128]{2,1,0:T(8,128)S(1)} %collective-permute-done.west_ref, f32[8,16,128]{2,1,0:T(8,128)S(1)} %collective-permute-done.1.east_ref, ...), custom_call_target="tpu_custom_call" | custom-call | tf_op jit(solution)/shard_map/columns/pallas_call | solution.py:682
  20.6 18.0 %all_to_all.10.in_ref = f32[16,88,128]{2,1,0:T(8,128)S(1)} all-to-all(f32[16,88,128]{2,1,0:T(8,128)S(1)} %get-tuple-element.12), channel_id=1, replica_groups=mesh['lat'=16,'lon'=32] {'lat'}, dimensions={0} | all-to-all | bytes 1441792 | tf_op jit(solution)/shard_map/all_to_all | solution.py:699
  38.7 3.6 %substeps.1 = (f32[16,24,128]{2,1,0:T(8,128)S(1)}, f32[512,128]{1,0:T(8,128)S(1)}) custom-call(f32[16,88,128]{2,1,0:T(8,128)S(1)} %all_to_all.10.in_ref, f32[144,256]{1,0:T(8,128)S(1)} %get-tuple-element.13.flows_ref, f32[8,16,128]{2,1,0:T(8,128)S(1)} %collective-permute-done.west_ref, f32[8,16,128]{2,1,0:T(8,128)S(1)} %collective-permute-done.1.east_ref, ...), custom_call_target="tpu_custom_call" | custom-call | tf_op jit(solution)/shard_map/substeps/pallas_call | solution.py:700
  42.3 9.7 %all_to_all.11.in_ref = f32[16,24,128]{2,1,0:T(8,128)S(1)} all-to-all(f32[16,24,128]{2,1,0:T(8,128)S(1)} %get-tuple-element.14), channel_id=1, replica_groups=mesh['lat'=16,'lon'=32] {'lat'}, dimensions={0} | all-to-all | bytes 393216 | tf_op jit(solution)/shard_map/all_to_all | solution.py:712
  51.9 1.4 %finish.1 = (f32[4,8,16,128]{3,2,1,0:T(8,128)}, f32[2,8,16,128]{3,2,1,0:T(8,128)}, f32[16,128]{1,0:T(8,128)}, f32[16,128]{1,0:T(8,128)}) custom-call(s32[1]{0:T(128)} %bitcast.place_ref, f32[16,24,128]{2,1,0:T(8,128)S(1)} %all_to_all.11.in_ref, f32[52,16,128]{2,1,0:T(8,128)S(1)} %convert_add_fusion.own_ref, f32[8,16,128]{2,1,0:T(8,128)S(1)} %collective-permute-done.west_ref, ...), custom_call_target="tpu_custom_call" | custom-call | tf_op jit(solution)/shard_map/finish/pallas_call | solution.py:713
Async XLA Ops:
  1.9 17.0 %collective-permute-start = (f32[8,16,128]{2,1,0:T(8,128)S(1)}, f32[8,16,128]{2,1,0:T(8,128)S(1)}, u32[]{:S(2)}, u32[]{:S(2)}) collective-permute-start(f32[8,16,128]{2,1,0:T(8,128)S(1)} %get-tuple-element.10.right_ref), channel_id=1, source_target_pairs={{0,1},{1,2},{2,3},{3,4},{4,5},{5,6},{6,7},{7,8},{8,9},{9,10},{10,1... | collective-permute-start | bytes 196616 | tf_op jit(solution)/shard_map/ppermute | solution.py:671
  7.6 12.2 %collective-permute-start.1 = (f32[8,16,128]{2,1,0:T(8,128)S(1)}, f32[8,16,128]{2,1,0:T(8,128)S(1)}, u32[]{:S(2)}, u32[]{:S(2)}) collective-permute-start(f32[8,16,128]{2,1,0:T(8,128)S(1)} %get-tuple-element.11.left_ref), channel_id=1, source_target_pairs={{0,31},{1,0},{2,1},{3,2},{4,3},{5,4},{6,5},{7,6},{8,7},{9,8},{10,9... | collective-permute-start | bytes 196616 | tf_op jit(solution)/shard_map/ppermute | solution.py:672

commit v10 on v9

--- a/solution.py
+++ b/solution.py
@@ -189,7 +189,7 @@
     tile_lane = ids((8, COLS), 1)
     spare_block = tile_lane // 8 == lax.rem(6 + place, 16)
     moved = [at(edge, 8 * d - HALO + 4, 1)[:, :COLS] for d in range(MEMBERS)]
-    halves = [at(x, 64, 1) for x in moved]
+    halves = [at(edge, 8 * d - HALO + 4 - 64, 1)[:, :COLS] for d in range(MEMBERS)]
     rests = [jnp.where(tile_lane % 8 == sub, x[:, 64:65], 0.0) for x in moved]
     for step in (1, 2, 4):
         rests = [x + at(x, step, 0) for x in rests]

time: 53.6 us -> 53.6 us (level)
  no operation moved by 1% of the time
where the time goes in v10:
time: 53.6 us; the launch traced here: 53.3 us
  blocking collectives  27.7 us (52%)
  starting transfers between devices  16.5 us (31%)
  Pallas kernels  6.52 us (12%)
  other arithmetic  1.09 us (2%)
  waiting for transfers between devices  0.79 us (1%)
  between operations  0.69 us (1%)
    all_to_all x1, blocking collectives, shards(): slabs = lax.all_to_all(chunks, 'lat', 0, 0, tiled=True)  18 us
    ppermute x1, starting transfers between devices, shards(): east = lax.ppermute(to_left, 'lon', ring('lon', -1))  10.9 us
    all_to_all x1, blocking collectives, shards(): home = lax.all_to_all(answers, 'lat', 0, 0, tiled=True)  9.68 us
    ppermute x1, starting transfers between devices, shards(): west = lax.ppermute(to_right, 'lon', ring('lon', 1))  5.65 us
    pallas_call x1, Pallas kernels, shards(): pl.pallas_call(slab_kernel, out_shape=(struct(MEMBERS, BACK, COLS), struc...  3.6 us
    pallas_call x1, Pallas kernels, shards(): pl.pallas_call(finish_kernel, out_shape=(struct(TRACERS, LEVELS, ROWS, CO...  1.37 us
    add x1, other arithmetic, stacked(): put(tracers, 0) + put(velocity, OWN_EAST) + put(surface, OWN_SURFACE)  1.09 us
  transfers between devices with their start and end apart: 2, of which 1 were waited for; matrix products, arithmetic and copies ran while one was open for 0% of the time, Pallas kernels for 1%

profile of v10, /device:TPU:1, one launch (start us, length us, event | category | flops | bytes accessed | tf_op | source)
XLA Modules:
  0.0 53.3 jit_solution(4010252919988801386)
XLA Ops:
  0.6 1.1 %convert_add_fusion.own_ref = f32[52,16,128]{2,1,0:T(8,128)S(1)} fusion(s32[1,16,128]{2,1,0:T(8,128)} %bitcast.7, f32[2,16,128]{2,1,0:T(8,128)} %param.8, f32[1,16,128]{2,1,0:T(8,128)} %bitcast.8, f32[16,16,128]{2,1,0:T(8,128)} %bitcast.6, f32[32,16,128]{2,1,0:T(8,128)} %bitcast.5), kind=kLoop, calls=%fused_computation | loop fusion | flops 532480 | bytes 851968 | tf_op jit(solution)/shard_map/add | solution.py:651
  1.7 0.2 pack.1
  1.9 5.7 %collective-permute-start = (f32[8,16,128]{2,1,0:T(8,128)S(1)}, f32[8,16,128]{2,1,0:T(8,128)S(1)}, u32[]{:S(2)}, u32[]{:S(2)}) collective-permute-start(f32[8,16,128]{2,1,0:T(8,128)S(1)} %get-tuple-element.10.right_ref), channel_id=1, source_target_pairs={{0,1},{1,2},{2,3},{3,4},{4,5},{5,6},{6,7},{7,8},{8,9},{9,10},{10,1... | collective-permute-start | bytes 196616 | tf_op jit(solution)/shard_map/ppermute | solution.py:671
  7.6 10.9 %collective-permute-start.1 = (f32[8,16,128]{2,1,0:T(8,128)S(1)}, f32[8,16,128]{2,1,0:T(8,128)S(1)}, u32[]{:S(2)}, u32[]{:S(2)}) collective-permute-start(f32[8,16,128]{2,1,0:T(8,128)S(1)} %get-tuple-element.11.left_ref), channel_id=1, source_target_pairs={{0,31},{1,0},{2,1},{3,2},{4,3},{5,4},{6,5},{7,6},{8,7},{9,8},{10,9... | collective-permute-start | bytes 196616 | tf_op jit(solution)/shard_map/ppermute | solution.py:672
  18.4 0.5 inner.1._.inner_ref
  18.9 0.0 collective-permute-done.west_ref
  19.0 0.8 %collective-permute-done.1.east_ref = f32[8,16,128]{2,1,0:T(8,128)S(1)} collective-permute-done((f32[8,16,128]{2,1,0:T(8,128)S(1)}, f32[8,16,128]{2,1,0:T(8,128)S(1)}, u32[]{:S(2)}, u32[]{:S(2)}) %collective-permute-start.1) | collective-permute-done | bytes 65568 | tf_op jit(solution)/shard_map/ppermute | solution.py:672
  19.7 0.9 %columns.1 = (f32[16,88,128]{2,1,0:T(8,128)S(1)}, f32[144,256]{1,0:T(8,128)S(1)}) custom-call(s32[1]{0:T(128)} %bitcast.place_ref, f32[52,16,128]{2,1,0:T(8,128)S(1)} %convert_add_fusion.own_ref, f32[8,16,128]{2,1,0:T(8,128)S(1)} %collective-permute-done.west_ref, f32[8,16,128]{2,1,0:T(8,128)S(1)} %collective-permute-done.1.east_ref, ...), custom_call_target="tpu_custom_call" | custom-call | tf_op jit(solution)/shard_map/columns/pallas_call | solution.py:682
  20.6 18.0 %all_to_all.10.in_ref = f32[16,88,128]{2,1,0:T(8,128)S(1)} all-to-all(f32[16,88,128]{2,1,0:T(8,128)S(1)} %get-tuple-element.12), channel_id=1, replica_groups=mesh['lat'=16,'lon'=32] {'lat'}, dimensions={0} | all-to-all | bytes 1441792 | tf_op jit(solution)/shard_map/all_to_all | solution.py:699
  38.6 3.6 %substeps.1 = (f32[16,24,128]{2,1,0:T(8,128)S(1)}, f32[512,128]{1,0:T(8,128)S(1)}) custom-call(f32[16,88,128]{2,1,0:T(8,128)S(1)} %all_to_all.10.in_ref, f32[144,256]{1,0:T(8,128)S(1)} %get-tuple-element.13.flows_ref, f32[8,16,128]{2,1,0:T(8,128)S(1)} %collective-permute-done.west_ref, f32[8,16,128]{2,1,0:T(8,128)S(1)} %collective-permute-done.1.east_ref, ...), custom_call_target="tpu_custom_call" | custom-call | tf_op jit(solution)/shard_map/substeps/pallas_call | solution.py:700
  42.3 9.7 %all_to_all.11.in_ref = f32[16,24,128]{2,1,0:T(8,128)S(1)} all-to-all(f32[16,24,128]{2,1,0:T(8,128)S(1)} %get-tuple-element.14), channel_id=1, replica_groups=mesh['lat'=16,'lon'=32] {'lat'}, dimensions={0} | all-to-all | bytes 393216 | tf_op jit(solution)/shard_map/all_to_all | solution.py:712
  51.9 1.4 %finish.1 = (f32[4,8,16,128]{3,2,1,0:T(8,128)}, f32[2,8,16,128]{3,2,1,0:T(8,128)}, f32[16,128]{1,0:T(8,128)}, f32[16,128]{1,0:T(8,128)}) custom-call(s32[1]{0:T(128)} %bitcast.place_ref, f32[16,24,128]{2,1,0:T(8,128)S(1)} %all_to_all.11.in_ref, f32[52,16,128]{2,1,0:T(8,128)S(1)} %convert_add_fusion.own_ref, f32[8,16,128]{2,1,0:T(8,128)S(1)} %collective-permute-done.west_ref, ...), custom_call_target="tpu_custom_call" | custom-call | tf_op jit(solution)/shard_map/finish/pallas_call | solution.py:713
Async XLA Ops:
  1.9 17.0 %collective-permute-start = (f32[8,16,128]{2,1,0:T(8,128)S(1)}, f32[8,16,128]{2,1,0:T(8,128)S(1)}, u32[]{:S(2)}, u32[]{:S(2)}) collective-permute-start(f32[8,16,128]{2,1,0:T(8,128)S(1)} %get-tuple-element.10.right_ref), channel_id=1, source_target_pairs={{0,1},{1,2},{2,3},{3,4},{4,5},{5,6},{6,7},{7,8},{8,9},{9,10},{10,1... | collective-permute-start | bytes 196616 | tf_op jit(solution)/shard_map/ppermute | solution.py:671
  7.6 12.2 %collective-permute-start.1 = (f32[8,16,128]{2,1,0:T(8,128)S(1)}, f32[8,16,128]{2,1,0:T(8,128)S(1)}, u32[]{:S(2)}, u32[]{:S(2)}) collective-permute-start(f32[8,16,128]{2,1,0:T(8,128)S(1)} %get-tuple-element.11.left_ref), channel_id=1, source_target_pairs={{0,31},{1,0},{2,1},{3,2},{4,3},{5,4},{6,5},{7,6},{8,7},{9,8},{10,9... | collective-permute-start | bytes 196616 | tf_op jit(solution)/shard_map/ppermute | solution.py:672

commit v11 on v10

--- a/solution.py
+++ b/solution.py
@@ -355,9 +355,13 @@
         ],
         axis=0,
     )
-    for step in (1, 2, 4):
+    one = at(terms, -1, 1)
+    middle = one[SLAB : 3 * SLAB] + at(terms[SLAB : 3 * SLAB], -2, 1)
+    terms = terms + one
+    terms = jnp.concatenate([terms[:SLAB], middle, terms[3 * SLAB :]], axis=0)
+    for step in (2, 4):
         terms = terms + at(terms, -step, 1)
-    shifted = at(terms[SLAB : 3 * SLAB], -1, 1)
+    shifted = terms[SLAB : 3 * SLAB]
     u_15, v_14, v_15, begin_15 = (
         jnp.where(r == 7, terms[SLAB * n : SLAB * (n + 1)], 0.0) for n in (0, 3, 4, 5)
     )

time: 53.6 us -> 53.6 us (level)
  no operation moved by 1% of the time
where the time goes in v11:
time: 53.6 us; the launch traced here: 53.3 us
  blocking collectives  27.7 us (52%)
  starting transfers between devices  16.5 us (31%)
  Pallas kernels  6.53 us (12%)
  other arithmetic  1.09 us (2%)
  waiting for transfers between devices  0.79 us (1%)
  between operations  0.69 us (1%)
    all_to_all x1, blocking collectives, shards(): slabs = lax.all_to_all(chunks, 'lat', 0, 0, tiled=True)  18 us
    ppermute x1, starting transfers between devices, shards(): east = lax.ppermute(to_left, 'lon', ring('lon', -1))  10.9 us
    all_to_all x1, blocking collectives, shards(): home = lax.all_to_all(answers, 'lat', 0, 0, tiled=True)  9.68 us
    ppermute x1, starting transfers between devices, shards(): west = lax.ppermute(to_right, 'lon', ring('lon', 1))  5.65 us
    pallas_call x1, Pallas kernels, shards(): pl.pallas_call(slab_kernel, out_shape=(struct(MEMBERS, BACK, COLS), struc...  3.61 us
    pallas_call x1, Pallas kernels, shards(): pl.pallas_call(finish_kernel, out_shape=(struct(TRACERS, LEVELS, ROWS, CO...  1.37 us
    add x1, other arithmetic, stacked(): put(tracers, 0) + put(velocity, OWN_EAST) + put(surface, OWN_SURFACE)  1.09 us
  transfers between devices with their start and end apart: 2, of which 1 were waited for; matrix products, arithmetic and copies ran while one was open for 0% of the time, Pallas kernels for 1%

profile of v11, /device:TPU:1, one launch (start us, length us, event | category | flops | bytes accessed | tf_op | source)
XLA Modules:
  0.0 53.3 jit_solution(15533134460486201578)
XLA Ops:
  0.6 1.1 %convert_add_fusion.own_ref = f32[52,16,128]{2,1,0:T(8,128)S(1)} fusion(s32[1,16,128]{2,1,0:T(8,128)} %bitcast.7, f32[2,16,128]{2,1,0:T(8,128)} %param.8, f32[1,16,128]{2,1,0:T(8,128)} %bitcast.8, f32[16,16,128]{2,1,0:T(8,128)} %bitcast.6, f32[32,16,128]{2,1,0:T(8,128)} %bitcast.5), kind=kLoop, calls=%fused_computation | loop fusion | flops 532480 | bytes 851968 | tf_op jit(solution)/shard_map/add | solution.py:655
  1.7 0.2 pack.1
  1.9 5.7 %collective-permute-start = (f32[8,16,128]{2,1,0:T(8,128)S(1)}, f32[8,16,128]{2,1,0:T(8,128)S(1)}, u32[]{:S(2)}, u32[]{:S(2)}) collective-permute-start(f32[8,16,128]{2,1,0:T(8,128)S(1)} %get-tuple-element.10.right_ref), channel_id=1, source_target_pairs={{0,1},{1,2},{2,3},{3,4},{4,5},{5,6},{6,7},{7,8},{8,9},{9,10},{10,1... | collective-permute-start | bytes 196616 | tf_op jit(solution)/shard_map/ppermute | solution.py:675
  7.6 10.9 %collective-permute-start.1 = (f32[8,16,128]{2,1,0:T(8,128)S(1)}, f32[8,16,128]{2,1,0:T(8,128)S(1)}, u32[]{:S(2)}, u32[]{:S(2)}) collective-permute-start(f32[8,16,128]{2,1,0:T(8,128)S(1)} %get-tuple-element.11.left_ref), channel_id=1, source_target_pairs={{0,31},{1,0},{2,1},{3,2},{4,3},{5,4},{6,5},{7,6},{8,7},{9,8},{10,9... | collective-permute-start | bytes 196616 | tf_op jit(solution)/shard_map/ppermute | solution.py:676
  18.4 0.5 inner.1._.inner_ref
  18.9 0.0 collective-permute-done.west_ref
  19.0 0.8 %collective-permute-done.1.east_ref = f32[8,16,128]{2,1,0:T(8,128)S(1)} collective-permute-done((f32[8,16,128]{2,1,0:T(8,128)S(1)}, f32[8,16,128]{2,1,0:T(8,128)S(1)}, u32[]{:S(2)}, u32[]{:S(2)}) %collective-permute-start.1) | collective-permute-done | bytes 65568 | tf_op jit(solution)/shard_map/ppermute | solution.py:676
  19.7 0.9 %columns.1 = (f32[16,88,128]{2,1,0:T(8,128)S(1)}, f32[144,256]{1,0:T(8,128)S(1)}) custom-call(s32[1]{0:T(128)} %bitcast.place_ref, f32[52,16,128]{2,1,0:T(8,128)S(1)} %convert_add_fusion.own_ref, f32[8,16,128]{2,1,0:T(8,128)S(1)} %collective-permute-done.west_ref, f32[8,16,128]{2,1,0:T(8,128)S(1)} %collective-permute-done.1.east_ref, ...), custom_call_target="tpu_custom_call" | custom-call | tf_op jit(solution)/shard_map/columns/pallas_call | solution.py:686
  20.6 18.0 %all_to_all.10.in_ref = f32[16,88,128]{2,1,0:T(8,128)S(1)} all-to-all(f32[16,88,128]{2,1,0:T(8,128)S(1)} %get-tuple-element.12), channel_id=1, replica_groups=mesh['lat'=16,'lon'=32] {'lat'}, dimensions={0} | all-to-all | bytes 1441792 | tf_op jit(solution)/shard_map/all_to_all | solution.py:703
  38.6 3.6 %substeps.1 = (f32[16,24,128]{2,1,0:T(8,128)S(1)}, f32[512,128]{1,0:T(8,128)S(1)}) custom-call(f32[16,88,128]{2,1,0:T(8,128)S(1)} %all_to_all.10.in_ref, f32[144,256]{1,0:T(8,128)S(1)} %get-tuple-element.13.flows_ref, f32[8,16,128]{2,1,0:T(8,128)S(1)} %collective-permute-done.west_ref, f32[8,16,128]{2,1,0:T(8,128)S(1)} %collective-permute-done.1.east_ref, ...), custom_call_target="tpu_custom_call" | custom-call | tf_op jit(solution)/shard_map/substeps/pallas_call | solution.py:704
  42.3 9.7 %all_to_all.11.in_ref = f32[16,24,128]{2,1,0:T(8,128)S(1)} all-to-all(f32[16,24,128]{2,1,0:T(8,128)S(1)} %get-tuple-element.14), channel_id=1, replica_groups=mesh['lat'=16,'lon'=32] {'lat'}, dimensions={0} | all-to-all | bytes 393216 | tf_op jit(solution)/shard_map/all_to_all | solution.py:716
  51.9 1.4 %finish.1 = (f32[4,8,16,128]{3,2,1,0:T(8,128)}, f32[2,8,16,128]{3,2,1,0:T(8,128)}, f32[16,128]{1,0:T(8,128)}, f32[16,128]{1,0:T(8,128)}) custom-call(s32[1]{0:T(128)} %bitcast.place_ref, f32[16,24,128]{2,1,0:T(8,128)S(1)} %all_to_all.11.in_ref, f32[52,16,128]{2,1,0:T(8,128)S(1)} %convert_add_fusion.own_ref, f32[8,16,128]{2,1,0:T(8,128)S(1)} %collective-permute-done.west_ref, ...), custom_call_target="tpu_custom_call" | custom-call | tf_op jit(solution)/shard_map/finish/pallas_call | solution.py:717
Async XLA Ops:
  1.9 17.0 %collective-permute-start = (f32[8,16,128]{2,1,0:T(8,128)S(1)}, f32[8,16,128]{2,1,0:T(8,128)S(1)}, u32[]{:S(2)}, u32[]{:S(2)}) collective-permute-start(f32[8,16,128]{2,1,0:T(8,128)S(1)} %get-tuple-element.10.right_ref), channel_id=1, source_target_pairs={{0,1},{1,2},{2,3},{3,4},{4,5},{5,6},{6,7},{7,8},{8,9},{9,10},{10,1... | collective-permute-start | bytes 196616 | tf_op jit(solution)/shard_map/ppermute | solution.py:675
  7.6 12.2 %collective-permute-start.1 = (f32[8,16,128]{2,1,0:T(8,128)S(1)}, f32[8,16,128]{2,1,0:T(8,128)S(1)}, u32[]{:S(2)}, u32[]{:S(2)}) collective-permute-start(f32[8,16,128]{2,1,0:T(8,128)S(1)} %get-tuple-element.11.left_ref), channel_id=1, source_target_pairs={{0,31},{1,0},{2,1},{3,2},{4,3},{5,4},{6,5},{7,6},{8,7},{9,8},{10,9... | collective-permute-start | bytes 196616 | tf_op jit(solution)/shard_map/ppermute | solution.py:676
